TPU v7x, 32 devices: a whole 2x2x4 slice. The times are simulated.
32 devices in a mesh: row: 8 (over z, x), col: 4 (over y, core).
Axes of the slice: x: 2, y: 2, z: 4, core: 2. Of those that a mesh axis runs over, the one named last changes fastest.
Arguments:
- right_sides: float32 [4, 32, 128, 128], P(None, 'row'), may hold values from -6 to 6
- inverse_diag: float32 [4, 32, 128, 128], P(None, 'row', 'col'), may hold values from -1 to 2
- lower_blocks: float32 [3, 32, 16, 128, 128], P(None, 'row', None, 'col'), may hold values from -0.09375 to 0.09375
- depends_on: int32 [3, 32, 16], replicated, may hold values from 0 to 31, as said below
Outputs:
- solution: float32 [4, 32, 128, 128], P(None, 'row', 'col')
Inputs may be any that keep to these rules, and one draw needn't show every extreme that they name: `depends_on`: in each level, the supernodes of one device along row name the supernodes of any one device along row at most 16 times in all, and some pair of devices reaches 16 in every level.
All inputs are finite; a program needn't handle non-finite values.
Results may differ from a plain program's by a relative error of at most 0.0001.
Values sent between devices are 32-bit elements; how exact they have to be, the bound alone decides.
No kernel may reach another device: no remote copies, remote signals or barrier semaphores. Data moves between devices by JAX's collectives and lax.ppermute only.
A program may use at most 64 MiB of HBM per device.

v0:
```python
import jax
import jax.numpy as jnp
from jax import lax
from jax.sharding import PartitionSpec as P

exact_mode = lax.Precision.HIGHEST


def fetch_blocks(previous, wanted):
    shard_rows = lax.all_gather(previous, "row", axis=0, tiled=True)
    chooser = (wanted[:, None] == jnp.arange(shard_rows.shape[0], dtype=jnp.int32)[None, :]).astype(
        jnp.float32
    )
    return jnp.einsum("en,nrk->erk", chooser, shard_rows, precision=exact_mode)


def return_terms(terms, wanted, local_count):
    owners = (
        jnp.arange(local_count * lax.axis_size("row"), dtype=jnp.int32)[:, None] == wanted[None, :]
    ).astype(jnp.float32)
    return lax.psum_scatter(
        jnp.einsum("me,erk->mrk", owners, terms, precision=exact_mode),
        "row",
        scatter_dimension=0,
        tiled=True,
    )


def forward_update(partial_value):
    return lax.psum(partial_value, "col")


def backward_solve(inverse_level, rest):
    partial_value = jnp.einsum("jab,jak->jbk", inverse_level, rest, precision=exact_mode)
    return lax.psum(partial_value, "col")


def on_device(right_sides, inverse_diag, lower_blocks, depends_on):
    levels, local_count, width, columns = right_sides.shape
    share = inverse_diag.shape[2]
    fan_in = lower_blocks.shape[2]
    my_row = lax.axis_index("row")
    my_col = lax.axis_index("col")
    entries = local_count * fan_in
    wanted_all = [
        lax.dynamic_slice_in_dim(
            depends_on[level_no], my_row * local_count, local_count, 0
        ).reshape(entries)
        for level_no in range(levels - 1)
    ]
    solved_here = [
        jnp.einsum("jab,jbk->jak", inverse_diag[0], right_sides[0], precision=exact_mode)
    ]
    for level_no in range(1, levels):
        picked = fetch_blocks(solved_here[-1], wanted_all[level_no - 1])
        partial_value = jnp.einsum(
            "jdba,jdbk->jak",
            lower_blocks[level_no - 1],
            picked.reshape(local_count, fan_in, share, columns),
            precision=exact_mode,
        )
        update = forward_update(partial_value)
        residual = right_sides[level_no] - update
        solved_here.append(
            jnp.einsum("jab,jbk->jak", inverse_diag[level_no], residual, precision=exact_mode)
        )
    full_sol = backward_solve(inverse_diag[levels - 1], solved_here[levels - 1])
    pieces = [lax.dynamic_slice_in_dim(full_sol, my_col * share, share, 1)]
    for level_no in range(levels - 2, -1, -1):
        terms = jnp.einsum(
            "jdba,jak->jdbk", lower_blocks[level_no], full_sol, precision=exact_mode
        ).reshape(entries, share, columns)
        returned = return_terms(terms, wanted_all[level_no], local_count)
        rest = solved_here[level_no] - returned
        full_sol = backward_solve(inverse_diag[level_no], rest)
        pieces.insert(0, lax.dynamic_slice_in_dim(full_sol, my_col * share, share, 1))
    return jnp.stack(pieces)


def solution(mesh):
    return jax.shard_map(
        on_device,
        mesh=mesh,
        in_specs=(
            P(None, "row", None, None),
            P(None, "row", "col", None),
            P(None, "row", None, "col", None),
            P(),
        ),
        out_specs=P(None, "row", "col", None),
        check_vma=False,
    )
```

profile of v0, /device:TPU:0, one launch (start us, length us, event | category | flops | bytes accessed | tf_op | source)
XLA Modules:
  0.0 564.6 jit_solution(17270012204401654376)
XLA Ops:
  9.5 33.0 %all_gather.9 = f32[32,32,128]{2,1,0:T(8,128)S(1)} all-gather(f32[4,32,128]{2,1,0:T(8,128)S(1)} %fusion.22), channel_id=1, replica_groups=mesh['row'=8,'col'=4] {'row'}, dimensions={0}, use_global_device_ids=true | all-gather | bytes 589824 | tf_op jit(solution)/shard_map/all_gather | solution.py:10
  42.5 3.2 fusion.65
  46.6 3.0 convolution_bitcast_fusion.6
  50.8 32.0 %all-reduce.8.cloned.1.call-done = f32[4,128,128]{1,2,0:T(8,128)} async-done(((f32[4,128,128]{1,2,0:T(8,128)}), f32[4,128,128]{1,2,0:T(8,128)}) %all-reduce.8.cloned.1.call-update) | async-done | bytes 262160 | tf_op jit(solution)/shard_map/psum | solution.py:30
  84.3 31.5 %all_gather.10 = f32[32,32,128]{2,1,0:T(8,128)S(1)} all-gather(f32[4,32,128]{2,1,0:T(8,128)S(1)} %convolution_bitcast_fusion.8), channel_id=1, replica_groups=mesh['row'=8,'col'=4] {'row'}, dimensions={0}, use_global_device_ids=true | all-gather | bytes 589824 | tf_op jit(solution)/shard_map/all_gather | solution.py:10
  116.7 2.9 convolution_bitcast_fusion.5
  120.0 31.7 %all-reduce.10.cloned.1.call-done = f32[4,128,128]{1,2,0:T(8,128)} async-done(((f32[4,128,128]{1,2,0:T(8,128)}), f32[4,128,128]{1,2,0:T(8,128)}) %all-reduce.10.cloned.1.call-update) | async-done | bytes 262160 | tf_op jit(solution)/shard_map/psum | solution.py:30
  153.2 31.5 %all_gather.11 = f32[32,32,128]{2,1,0:T(8,128)S(1)} all-gather(f32[4,32,128]{2,1,0:T(8,128)S(1)} %convolution_bitcast_fusion.7), channel_id=1, replica_groups=mesh['row'=8,'col'=4] {'row'}, dimensions={0}, use_global_device_ids=true | all-gather | bytes 589824 | tf_op jit(solution)/shard_map/all_gather | solution.py:10
  185.5 4.3 convolution_bitcast_fusion.4
  190.1 1.8 copy.74
  191.9 30.0 %all-reduce.12.cloned.1.call-done = f32[4,128,128]{1,2,0:T(8,128)} async-done(((f32[4,128,128]{1,2,0:T(8,128)}), f32[4,128,128]{1,2,0:T(8,128)}) %all-reduce.12.cloned.1.call-update) | async-done | bytes 262160 | tf_op jit(solution)/shard_map/psum | solution.py:30
  224.9 32.1 %all-reduce.14.cloned.1.call-done = f32[4,128,128]{1,2,0:T(8,128)} async-done(((f32[4,128,128]{1,2,0:T(8,128)}), f32[4,128,128]{1,2,0:T(8,128)}) %all-reduce.14.cloned.1.call-update) | async-done | bytes 262160 | tf_op jit(solution)/shard_map/psum | solution.py:35
  256.9 1.9 fusion.4
  261.2 61.9 %reduce-scatter.4.cloned.1.call-done = f32[4,32,128]{2,1,0:T(8,128)} async-done(((f32[32,32,128]{2,1,0:T(8,128)}), f32[4,32,128]{2,1,0:T(8,128)}) %reduce-scatter.4.cloned.1.call-update) | async-done | bytes 65552 | tf_op jit(solution)/shard_map/reduce_scatter | solution.py:21
  323.1 2.1 convolution_bitcast_fusion.2
  325.3 31.2 %all-reduce.16.cloned.1.call-done = f32[4,128,128]{1,2,0:T(8,128)} async-done(((f32[4,128,128]{1,2,0:T(8,128)}), f32[4,128,128]{1,2,0:T(8,128)}) %all-reduce.16.cloned.1.call-update) | async-done | bytes 262160 | tf_op jit(solution)/shard_map/psum | solution.py:35
  356.5 1.9 fusion.2
  360.7 62.1 %reduce-scatter.6.cloned.1.call-done = f32[4,32,128]{2,1,0:T(8,128)} async-done(((f32[32,32,128]{2,1,0:T(8,128)}), f32[4,32,128]{2,1,0:T(8,128)}) %reduce-scatter.6.cloned.1.call-update) | async-done | bytes 65552 | tf_op jit(solution)/shard_map/reduce_scatter | solution.py:21
  422.8 2.2 convolution_bitcast_fusion.1
  425.0 31.2 %all-reduce.18.cloned.1.call-done = f32[4,128,128]{1,2,0:T(8,128)} async-done(((f32[4,128,128]{1,2,0:T(8,128)}), f32[4,128,128]{1,2,0:T(8,128)}) %all-reduce.18.cloned.1.call-update) | async-done | bytes 262160 | tf_op jit(solution)/shard_map/psum | solution.py:35
  456.2 1.9 fusion
  460.7 61.7 %reduce-scatter.8.cloned.1.call-done = f32[4,32,128]{2,1,0:T(8,128)} async-done(((f32[32,32,128]{2,1,0:T(8,128)}), f32[4,32,128]{2,1,0:T(8,128)}) %reduce-scatter.8.cloned.1.call-update) | async-done | bytes 65552 | tf_op jit(solution)/shard_map/reduce_scatter | solution.py:21
  522.5 2.2 convolution_bitcast_fusion
  525.2 30.7 %all-reduce.20.cloned.1.call-done = f32[4,128,128]{1,2,0:T(8,128)} async-done(((f32[4,128,128]{1,2,0:T(8,128)}), f32[4,128,128]{1,2,0:T(8,128)}) %all-reduce.20.cloned.1.call-update) | async-done | bytes 262160 | tf_op jit(solution)/shard_map/psum | solution.py:35
  (71 shorter events, 22.9 us)
Async XLA Ops:
  6.5 76.3 %all-reduce.8.cloned.1.call-start = ((), (), s32[]{:S(2)}) async-start(), calls=%async_computation.3 | async-start | bytes 524288 | tf_op jit(solution)/shard_map/psum | solution.py:30
  8.8 0.6 copy-start.6
  45.7 4.0 copy-start.5
  46.6 36.2 %copy-start.4 = (f32[4,4,32,128]{3,2,1,0:T(8,128)S(1)}, f32[4,4,32,128]{3,2,1,0:T(8,128)}, u32[]{:S(2)}) copy-start(f32[4,4,32,128]{3,2,1,0:T(8,128)} %param.5) | copy-start | bytes 786436
  49.6 102.1 %all-reduce.10.cloned.1.call-start = ((), (), s32[]{:S(2)}) async-start(), calls=%async_computation.4 | async-start | bytes 524288 | tf_op jit(solution)/shard_map/psum | solution.py:30
  119.6 102.3 %all-reduce.12.cloned.1.call-start = ((), (), s32[]{:S(2)}) async-start(), calls=%async_computation.5 | async-start | bytes 524288 | tf_op jit(solution)/shard_map/psum | solution.py:30
  185.5 71.4 %copy-start = (f32[3,4,16,32,128]{4,3,2,1,0:T(8,128)S(1)}, f32[3,4,16,32,128]{4,3,2,1,0:T(8,128)}, u32[]{:S(2)}) copy-start(f32[3,4,16,32,128]{4,3,2,1,0:T(8,128)} %param.6) | copy-start | bytes 9437188
  189.9 67.1 %all-reduce.14.cloned.1.call-start = ((), (), s32[]{:S(2)}) async-start(), calls=%async_computation.6 | async-start | bytes 524288 | tf_op jit(solution)/shard_map/psum | solution.py:35
  224.8 98.3 %reduce-scatter.4.cloned.1.call-start = ((), (), s32[]{:S(2)}) async-start(), calls=%async_computation.7 | async-start | bytes 589824 | tf_op jit(solution)/shard_map/reduce_scatter | solution.py:21
  261.1 95.4 %all-reduce.16.cloned.1.call-start = ((), (), s32[]{:S(2)}) async-start(), calls=%async_computation.8 | async-start | bytes 524288 | tf_op jit(solution)/shard_map/psum | solution.py:35
  325.3 97.5 %reduce-scatter.6.cloned.1.call-start = ((), (), s32[]{:S(2)}) async-start(), calls=%async_computation.9 | async-start | bytes 589824 | tf_op jit(solution)/shard_map/reduce_scatter | solution.py:21
  360.7 99.8 %copy-start.1 = (f32[4,128,128]{1,2,0:T(8,128)S(1)}, f32[4,128,128]{1,2,0:T(8,128)}, u32[]{:S(2)}) copy-start(f32[4,128,128]{1,2,0:T(8,128)} %all-reduce.14.cloned.1.call-done) | copy-start | bytes 786436
  360.7 95.5 %all-reduce.18.cloned.1.call-start = ((), (), s32[]{:S(2)}) async-start(), calls=%async_computation.10 | async-start | bytes 524288 | tf_op jit(solution)/shard_map/psum | solution.py:35
  425.0 97.5 %copy-start.7 = (f32[4,32,128]{2,1,0:T(8,128)S(1)}, f32[4,32,128]{2,1,0:T(8,128)}, u32[]{:S(2)}) copy-start(f32[4,32,128]{2,1,0:T(8,128)} %copy-done.6) | copy-start | bytes 196612
  425.0 97.5 %reduce-scatter.8.cloned.1.call-start = ((), (), s32[]{:S(2)}) async-start(), calls=%async_computation.11 | async-start | bytes 589824 | tf_op jit(solution)/shard_map/reduce_scatter | solution.py:21
  458.2 66.5 %copy-start.2 = (f32[4,128,128]{1,2,0:T(8,128)S(1)}, f32[4,128,128]{1,2,0:T(8,128)}, u32[]{:S(2)}) copy-start(f32[4,128,128]{1,2,0:T(8,128)} %all-reduce.16.cloned.1.call-done) | copy-start | bytes 786436
  458.2 66.7 %copy-start.3 = (f32[4,128,128]{1,2,0:T(8,128)S(1)}, f32[4,128,128]{1,2,0:T(8,128)}, u32[]{:S(2)}) copy-start(f32[4,128,128]{1,2,0:T(8,128)} %all-reduce.18.cloned.1.call-done) | copy-start | bytes 786436
  460.4 95.4 %all-reduce.20.cloned.1.call-start = ((), (), s32[]{:S(2)}) async-start(), calls=%async_computation.12 | async-start | bytes 524288 | tf_op jit(solution)/shard_map/psum | solution.py:35
Sparse Core Ops, SparseCore 0:
  49.7 33.0 all-reduce.7
  119.7 31.8 all-reduce.9
  190.0 31.9 all-reduce.11
  224.9 31.9 all-reduce.13
  261.2 61.8 reduce-scatter.3
  325.4 31.0 all-reduce.15
  360.8 61.9 reduce-scatter.5
  425.2 30.9 all-reduce.17
  460.6 61.8 reduce-scatter.7
  524.8 31.0 all-reduce.19
where the time goes:
time: 565 us
  waiting for transfers between devices  405 us (72%)
  blocking collectives  95.9 us (17%)
  matrix products  35.6 us (6%)
  between operations  13.7 us (2%)
  local copies, waits for them, and re-layouts  13.3 us (2%)
    reduce_scatter x3, waiting for transfers between devices, return_terms(): lax.psum_scatter(jnp.einsum('me,erk->mrk', owners, terms, precision=exact...  186 us
    psum x4, waiting for transfers between devices, backward_solve(): return lax.psum(partial_value, 'col')  125 us
    all_gather x3, blocking collectives, fetch_blocks(): shard_rows = lax.all_gather(previous, 'row', axis=0, tiled=True)  95.9 us
    psum x3, waiting for transfers between devices, forward_update(): return lax.psum(partial_value, 'col')  93.8 us
  transfers between devices with their start and end apart: 10, of which 10 were waited for; matrix products, arithmetic and copies ran while one was open for 1% of the time, Pallas kernels for 0%

commit v1 on v0

v1 whole, which is shorter than its diff:
```python
import functools

import jax
import jax.numpy as jnp
from jax import lax
from jax.experimental import pallas as pl
from jax.experimental.pallas import tpu as pltpu
from jax.sharding import PartitionSpec as P

F32 = jnp.float32
BF16 = jnp.bfloat16
EXACT = lax.Precision.HIGHEST
VMEM = pl.BlockSpec(memory_space=pltpu.VMEM)
SMEM = pl.BlockSpec(memory_space=pltpu.SMEM)
ANY = pl.BlockSpec(memory_space=pl.ANY)


def nn(a, b):
    return lax.dot_general(a, b, (((1,), (0,)), ((), ())), precision=EXACT, preferred_element_type=F32)


def nt(a, b):
    return lax.dot_general(a, b, (((1,), (1,)), ((), ())), precision=EXACT, preferred_element_type=F32)


def tn(a, b):
    return lax.dot_general(a, b, (((0,), (0,)), ((), ())), precision=EXACT, preferred_element_type=F32)


def half(a, b, contract):
    return lax.dot_general(a, b, ((contract[:1], contract[1:]), ((), ())), preferred_element_type=F32)


def split(value):
    high = value.astype(BF16)
    return high, (value - high.astype(F32)).astype(BF16)


def call(body, out_shape, in_specs, scratch=(), flops=0, moved=0, limit=40):
    return pl.pallas_call(
        body,
        out_shape=out_shape,
        in_specs=in_specs,
        out_specs=jax.tree.map(lambda _: VMEM, out_shape),
        scratch_shapes=list(scratch),
        compiler_params=pltpu.CompilerParams(vmem_limit_bytes=limit * 1024 * 1024),
        cost_estimate=pl.CostEstimate(flops=flops, bytes_accessed=moved, transcendentals=0),
    )


def swap(value, axis, mask):
    size = lax.axis_size(axis)
    return lax.ppermute(value, axis, [(i, i ^ mask) for i in range(size)])


def far_masks(size):
    masks, mask = [], size // 2
    while mask >= 4:
        masks.append(mask)
        mask //= 2
    return masks


def slot_of(mask, size):
    place = (mask & 3) * (size // 4)
    for step, far in enumerate(far_masks(size)):
        place = place + jnp.where((mask & far) != 0, 1 << step, 0)
    return place


def gather_row(own):
    held = own
    for mask in far_masks(lax.axis_size("row")):
        held = jnp.concatenate([held, swap(held, "row", mask)], axis=0)
    return [held] + [swap(held, "row", mask) for mask in (1, 2, 3)]


def scatter_row(parts):
    total = parts[0]
    got = [swap(part, "row", mask) for mask, part in zip((1, 2, 3), parts[1:])]
    total = total + got[0] + got[1] + got[2]
    other = None
    for mask in reversed(far_masks(lax.axis_size("row"))):
        if other is not None:
            total = total + other
        keep, send = jnp.split(total, 2, axis=0)
        total, other = keep, swap(send, "row", mask)
    return total, other


def first_kernel(inverse_ref, sides_ref, out_ref):
    for j in range(out_ref.shape[0]):
        out_ref[j] = nn(inverse_ref[j], sides_ref[j])


def turn_kernel(col_ref, sides_ref, out_ref, whole):
    count = out_ref.shape[1]
    start = pl.multiple_of(col_ref[0] * count, count)
    for i in range(out_ref.shape[0]):
        whole[i % 2] = sides_ref[i].T
        out_ref[i] = whole[i % 2, pl.ds(start, count), :]


def join_kernel(col_ref, *refs):
    parts, (high_ref, low_ref) = refs[:-2], refs[-2:]
    share = parts[0].shape[2]
    width = share * len(parts)
    for mask, part in enumerate(parts):
        offset = pl.multiple_of((col_ref[0] ^ mask) * share, share)
        for d in range(part.shape[1]):
            high, low = split(part[0, d])
            high_ref[0, pl.ds(d * width + offset, share), :] = high
            low_ref[0, pl.ds(d * width + offset, share), :] = low


def join_inverse_kernel(col_ref, *refs):
    parts, out_ref = refs[:-1], refs[-1]
    share = parts[0].shape[1]
    for mask, part in enumerate(parts):
        offset = pl.multiple_of((col_ref[0] ^ mask) * share, share)
        for i in range(part.shape[0]):
            out_ref[i, pl.ds(offset, share), :] = part[i]


def partial_kernel(col_ref, slot_ref, x0, x1, x2, x3, lower_ref, *refs):
    outs, (blocks, picked, turned) = refs[:-3], refs[-3:]
    count, fan_in, share, width = lower_ref.shape
    each = x0.shape[0]
    for q, x in enumerate((x0, x1, x2, x3)):
        blocks[q * each:(q + 1) * each] = x[...]
    for j in range(count):
        for d in range(fan_in):
            picked[j % 2, d * share:(d + 1) * share, :] = blocks[slot_ref[j * fan_in + d]]
        turned[j] = tn(picked[j % 2], lower_ref[j].reshape(fan_in * share, width))
    columns = outs[0].shape[1]
    for mask, out in enumerate(outs):
        start = pl.multiple_of((col_ref[0] ^ mask) * columns, columns)
        for j in range(count):
            out[j] = turned[j, pl.ds(start, columns), :]


def solve_first_kernel(u0, u1, u2, u3, sides_ref, inverse_ref, out_ref):
    for j in range(out_ref.shape[0]):
        rest = sides_ref[j] - ((u0[j] + u1[j]) + (u2[j] + u3[j]))
        out_ref[j] = nt(rest, inverse_ref[j])


def fetch(pairs, sems):
    copies = []
    for i in range(pairs[0][0].shape[0]):
        group = []
        for k, (source, target) in enumerate(pairs):
            copy = pltpu.make_async_copy(source.at[i], target.at[i], sems.at[i, k])
            copy.start()
            group.append(copy)
        copies.append(group)
    return copies


def forward_levels(slot_ref, xs, sides_ref, inverse_ref, high, low, copies, out_ref, blocks, picked):
    count, columns = out_ref.shape[:2]
    fan_in = slot_ref.shape[0] // count
    each = xs[0].shape[0]
    width = out_ref.shape[2]
    for q, x in enumerate(xs):
        for i in range(each):
            top, bottom = split(x[i])
            blocks[q * each + i, :columns] = top
            blocks[q * each + i, columns:] = bottom
    for j in range(count):
        for d in range(fan_in):
            picked[j, :, d * width:(d + 1) * width] = blocks[slot_ref[j * fan_in + d]]
    for j in range(count):
        for copy in copies[j]:
            copy.wait()
        both = half(picked[j], high[j], (1, 0)) + half(picked[j], low[j], (1, 0))
        update = both[:columns] + both[columns:]
        out_ref[j] = nt(sides_ref[j] - update, inverse_ref[j])


def backward_terms(slot_ref, solved, high, low, outs, total):
    count = high.shape[0]
    fan_in = slot_ref.shape[0] // count
    width = high.shape[2]
    total[...] = jnp.zeros_like(total)
    for j in range(count):
        value = solved(j)
        columns = value.shape[0]
        both = jnp.concatenate(split(value), axis=0)
        terms = half(both, high[j], (1, 1)) + half(both, low[j], (1, 1))
        terms = terms[:columns] + terms[columns:]
        for d in range(fan_in):
            slot = slot_ref[j * fan_in + d]
            total[slot] = total[slot] + terms[:, d * width:(d + 1) * width]
    each = outs[0].shape[0]
    for q, out in enumerate(outs):
        out[...] = total[q * each:(q + 1) * each]


def forward_kernel(slot_ref, x0, x1, x2, x3, sides_ref, inverse_ref, high_ref, low_ref, out_ref, high, low, sems, blocks, picked):
    copies = fetch(((high_ref, high), (low_ref, low)), sems)
    forward_levels(slot_ref, (x0, x1, x2, x3), sides_ref, inverse_ref, high, low, copies, out_ref, blocks, picked)


def top_kernel(
    slot_ref, x0, x1, x2, x3, sides_ref, inverse_ref, high_ref, low_ref, sol_ref, t0, t1, t2, t3,
    high, low, sems, blocks, picked, solved, total,
):
    copies = fetch(((high_ref, high), (low_ref, low)), sems)
    forward_levels(slot_ref, (x0, x1, x2, x3), sides_ref, inverse_ref, high, low, copies, solved, blocks, picked)

    def value(j):
        sol_ref[j] = nn(solved[j], inverse_ref[j])
        return sol_ref[j]

    backward_terms(slot_ref, value, high, low, (t0, t1, t2, t3), total)


def backward_kernel(
    slot_ref, ret0, ret1, forward_ref, inverse_ref, high_ref, low_ref, sol_ref, t0, t1, t2, t3, high, low, sems, total
):
    copies = fetch(((high_ref, high), (low_ref, low)), sems)

    def value(j):
        sol_ref[j] = nn(forward_ref[j] - (ret0[j] + ret1[j]), inverse_ref[j])
        for copy in copies[j]:
            copy.wait()
        return sol_ref[j]

    backward_terms(slot_ref, value, high, low, (t0, t1, t2, t3), total)


def last_kernel(col_ref, ret0, ret1, sides_ref, inverse_ref, s1, s2, s3, *refs):
    outs, (solved, packed) = refs[:-2], refs[-2:]
    count = sides_ref.shape[0]
    share = sides_ref.shape[2] // len(outs)
    for j in range(count):
        rest = nt(sides_ref[j], inverse_ref[j]) - (ret0[j] + ret1[j])
        solved[j] = nn(rest, inverse_ref[j])
    for level, source in enumerate((solved, s1, s2, s3)):
        for c in range(len(outs)):
            packed[c, level] = jnp.concatenate(
                [source[j, :, c * share:(c + 1) * share] for j in range(count)], axis=1
            )
    for mask, out in enumerate(outs):
        out[...] = packed[col_ref[0] ^ mask]


def out_kernel(col_ref, *refs):
    parts, (out_ref, whole) = refs[:-2], refs[-2:]
    levels, count, share, columns = out_ref.shape
    piece = parts[0].shape[1]
    for mask, part in enumerate(parts):
        start = pl.multiple_of((col_ref[0] ^ mask) * piece, piece)
        for level in range(levels):
            whole[level, pl.ds(start, piece), :] = part[level]
    for level in range(levels):
        out_ref[level] = whole[level].T.reshape(count, share, columns)


def collect(value):
    beside = swap(value, "col", 1)
    across = swap(value, "col", 2)
    return value, beside, across, swap(across, "col", 1)


def on_device(right_sides, inverse_diag, lower_blocks, depends_on):
    levels, count, width, columns = right_sides.shape
    share = inverse_diag.shape[2]
    fan_in = lower_blocks.shape[2]
    rows, cols = lax.axis_size("row"), lax.axis_size("col")
    my_row, my_col = lax.axis_index("row"), lax.axis_index("col")
    col = my_col.astype(jnp.int32).reshape(1)
    mine = columns // cols
    entries = count * fan_in
    wanted = lax.dynamic_slice_in_dim(depends_on, my_row * count, count, 1).reshape(levels - 1, entries)
    slots = slot_of((wanted // count) ^ my_row, rows) * count + wanted % count
    slots = [slots[i] for i in range(levels - 1)]

    def like(*shape, dtype=F32):
        return jax.ShapeDtypeStruct(shape, dtype)

    block = like(count, mine, width)
    quarter = like(rows // 4 * count, mine, width)
    solve_flops = 2 * count * mine * width * width * 6
    level_flops = 2 * entries * mine * width * width * 6
    level_bytes = 4 * entries * width * width

    first = call(
        first_kernel, like(count, share, columns), [VMEM] * 2, flops=solve_flops, moved=4 * count * width * width
    )(inverse_diag[0], right_sides[0])

    parts_inverse = collect(inverse_diag.reshape(levels * count, share, width))
    parts_lower = [None] * (levels - 1)
    for level in (1, 2, 0):
        parts_lower[level] = collect(lower_blocks[level])

    gathered = gather_row(first)

    sides = call(
        turn_kernel, like(levels * count, mine, width), [SMEM, VMEM],
        scratch=[pltpu.VMEM((2, columns, width), F32)], flops=0, moved=5 * levels * count * width * columns,
    )(col, right_sides.reshape(levels * count, width, columns))
    sides = [sides[i * count:(i + 1) * count] for i in range(levels)]

    partials = call(
        partial_kernel, [like(count, mine, width)] * cols, [SMEM, SMEM] + [VMEM] * 5,
        scratch=[
            pltpu.VMEM((rows * count, share, columns), F32),
            pltpu.VMEM((2, fan_in * share, columns), F32),
            pltpu.VMEM((count, columns, width), F32),
        ],
        flops=level_flops, moved=level_bytes // cols,
    )(col, slots[0], *gathered, lower_blocks[0])
    updates = [partials[0]] + [swap(partials[mask], "col", mask) for mask in range(1, cols)]

    inverse = call(
        join_inverse_kernel, like(levels * count, width, width), [SMEM] + [VMEM] * cols,
        flops=0, moved=8 * levels * count * width * width,
    )(col, *parts_inverse)
    inverse = [inverse[i * count:(i + 1) * count] for i in range(levels)]

    def join(parts):
        part_spec = pl.BlockSpec((1, fan_in, share, width), lambda j: (j, 0, 0, 0))
        out_spec = pl.BlockSpec((1, fan_in * width, width), lambda j: (j, 0, 0))
        return pl.pallas_call(
            join_kernel,
            grid=(count,),
            out_shape=[like(count, fan_in * width, width, dtype=BF16)] * 2,
            in_specs=[SMEM] + [part_spec] * cols,
            out_specs=[out_spec] * 2,
            compiler_params=pltpu.CompilerParams(vmem_limit_bytes=40 * 1024 * 1024),
            cost_estimate=pl.CostEstimate(flops=0, bytes_accessed=2 * level_bytes, transcendentals=0),
        )(col, *parts)

    lower = [None] * (levels - 1)
    for level in (1, 2, 0):
        lower[level] = join(parts_lower[level])

    fetched = [
        pltpu.VMEM((count, fan_in * width, width), BF16),
        pltpu.VMEM((count, fan_in * width, width), BF16),
        pltpu.SemaphoreType.DMA((count, 2)),
    ]
    picking = [
        pltpu.VMEM((rows * count, 2 * mine, width), BF16),
        pltpu.VMEM((count, 2 * mine, fan_in * width), BF16),
    ]
    total = [pltpu.VMEM((rows * count, mine, width), F32)]

    forward = [None] * levels
    forward[1] = call(
        solve_first_kernel, block, [VMEM] * 6, flops=solve_flops, moved=4 * count * width * width
    )(*updates, sides[1], inverse[1])
    for level in range(2, levels - 1):
        forward[level] = call(
            forward_kernel, block, [SMEM] + [VMEM] * 6 + [ANY] * 2, scratch=fetched + picking,
            flops=level_flops, moved=level_bytes,
        )(slots[level - 1], *gather_row(forward[level - 1]), sides[level], inverse[level], *lower[level - 1])

    solved = [None] * levels
    top = levels - 1
    solved[top], *terms = call(
        top_kernel, [block] + [quarter] * 4, [SMEM] + [VMEM] * 6 + [ANY] * 2,
        scratch=fetched + picking + [pltpu.VMEM((count, mine, width), F32)] + total,
        flops=2 * level_flops, moved=level_bytes,
    )(slots[top - 1], *gather_row(forward[top - 1]), sides[top], inverse[top], *lower[top - 1])
    for level in range(top - 1, 0, -1):
        solved[level], *terms = call(
            backward_kernel, [block] + [quarter] * 4, [SMEM] + [VMEM] * 4 + [ANY] * 2,
            scratch=fetched + total, flops=level_flops, moved=level_bytes,
        )(slots[level - 1], *scatter_row(terms), forward[level], inverse[level], *lower[level - 1])

    pieces = call(
        last_kernel, [like(levels, mine, count * share)] * cols, [SMEM] + [VMEM] * (4 + top),
        scratch=[
            pltpu.VMEM((count, mine, width), F32),
            pltpu.VMEM((cols, levels, mine, count * share), F32),
        ],
        flops=2 * solve_flops, moved=8 * count * width * width,
    )(col, *scatter_row(terms), sides[0], inverse[0], *solved[1:])
    pieces = [pieces[0]] + [swap(pieces[mask], "col", mask) for mask in range(1, cols)]
    return call(
        out_kernel, like(levels, count, share, columns), [SMEM] + [VMEM] * cols,
        scratch=[pltpu.VMEM((levels, columns, count * share), F32)],
        flops=0, moved=8 * levels * count * share * columns,
    )(col, *pieces)


def solution(mesh):
    return jax.shard_map(
        on_device,
        mesh=mesh,
        in_specs=(
            P(None, "row", None, None),
            P(None, "row", "col", None),
            P(None, "row", None, "col", None),
            P(),
        ),
        out_specs=P(None, "row", "col", None),
        check_vma=False,
    )
```

time: 565 us -> 164 us (0.29)
  waiting for transfers between devices: 405 us -> 78 us
  blocking collectives: 95.9 us -> 0 us
  starting transfers between devices: 0.56 us -> 51.7 us
  matrix products: 35.6 us -> 0 us
  Pallas kernels: 0 us -> 27.7 us
  between operations: 13.7 us -> 0.24 us
  local copies, waits for them, and re-layouts: 13.3 us -> 4.82 us
    psum x7 -> x0, waiting for transfers between devices: 219 us -> none  [the longest x4 125 us: backward_solve(): return lax.psum(partial_value, 'col')]
    reduce_scatter x3 -> x0, waiting for transfers between devices: 186 us -> none  [return_terms(): lax.psum_scatter(jnp.einsum('me,erk->mrk', owners, terms, precision=exact...]
    all_gather x3 -> x0, blocking collectives: 95.9 us -> none  [fetch_blocks(): shard_rows = lax.all_gather(previous, 'row', axis=0, tiled=True)]
    ppermute x0 -> x42, waiting for transfers between devices: none -> 78 us  [swap(): return lax.ppermute(value, axis, [(i, i ^ mask) for i in range(size)])]
    ppermute x0 -> x42, starting transfers between devices: none -> 51.7 us  [swap(): return lax.ppermute(value, axis, [(i, i ^ mask) for i in range(size)])]
    dot_general x20 -> x0, matrix products: 35.6 us -> none  [the longest x3 10.2 us: on_device(): jnp.einsum('jdba,jdbk->jak', lower_blocks[level_no - 1], picked.reshape(l...]
    pallas_call x0 -> x14, Pallas kernels: none -> 27.7 us  [the longest x2 6.86 us: on_device(): call(backward_kernel, [block] + [quarter] * 4, [SMEM] + [VMEM] * 4 + [ANY...]
  transfers between devices with their start and end apart: 10 -> 42, of which waited for: 10 -> 26; matrix products, arithmetic and copies ran while one was open for 1% -> 1% of each run, Pallas kernels for 0% -> 13%
where the time goes in v1:
time: 164 us; the launch traced here: 163 us
  waiting for transfers between devices  78 us (48%)
  starting transfers between devices  51.7 us (32%)
  Pallas kernels  27.7 us (17%)
  local copies, waits for them, and re-layouts  4.82 us (3%)
    ppermute x42, waiting for transfers between devices, swap(): return lax.ppermute(value, axis, [(i, i ^ mask) for i in range(size)])  78 us
    ppermute x42, starting transfers between devices, swap(): return lax.ppermute(value, axis, [(i, i ^ mask) for i in range(size)])  51.7 us
    pallas_call x2, Pallas kernels, on_device(): call(backward_kernel, [block] + [quarter] * 4, [SMEM] + [VMEM] * 4 + [ANY...  6.86 us
    pallas_call x1, Pallas kernels, on_device(): call(top_kernel, [block] + [quarter] * 4, [SMEM] + [VMEM] * 6 + [ANY] * 2...  5.58 us
    pallas_call x3, Pallas kernels, join(): pl.pallas_call(join_kernel, grid=(count,), out_shape=[like(count, fan_in...  5.1 us
    pallas_call x1, Pallas kernels, on_device(): call(forward_kernel, block, [SMEM] + [VMEM] * 6 + [ANY] * 2, scratch=fetc...  3.63 us
  transfers between devices with their start and end apart: 42, of which 26 were waited for; matrix products, arithmetic and copies ran while one was open for 1% of the time, Pallas kernels for 13%

profile of v1, /device:TPU:0, one launch (start us, length us, event | category | flops | bytes accessed | tf_op | source)
XLA Modules:
  0.0 163.5 jit_solution(15993444514706016350)
XLA Ops:
  2.2 3.0 %collective-permute-start.15 = (f32[4,16,32,128]{3,2,1,0:T(8,128)S(1)}, f32[4,16,32,128]{3,2,1,0:T(8,128)}, u32[]{:S(2)}, u32[]{:S(2)}) collective-permute-start(f32[4,16,32,128]{3,2,1,0:T(8,128)S(1)} %get-tuple-element.65.refs_0_), channel_id=1, source_target_pairs={{0,2},{1,3},{2,0},{3,1},{4,6},{5,7},{6,4},{7,5},{8,10},{9,11},{10,... | collective-permute-start | bytes 3145736 | tf_op jit(solution)/shard_map/ppermute | solution.py:53
  6.6 2.6 %collective-permute-start = (f32[4,32,128]{2,1,0:T(8,128)S(1)}, f32[4,32,128]{2,1,0:T(8,128)}, u32[]{:S(2)}, u32[]{:S(2)}) collective-permute-start(f32[4,32,128]{2,1,0:T(8,128)S(1)} %shard_map.46), channel_id=1, source_target_pairs={{0,16},{4,20},{8,24},{12,28},{16,0},{20,4},{24,8},{28,12},{1,17},{... | collective-permute-start | bytes 196616 | tf_op jit(solution)/shard_map/ppermute | solution.py:53
  16.9 3.4 %collective-permute-done.3.x3 = f32[8,32,128]{2,1,0:T(8,128)S(1)} collective-permute-done((f32[8,32,128]{2,1,0:T(8,128)S(1)}, f32[8,32,128]{2,1,0:T(8,128)S(1)}, u32[]{:S(2)}, u32[]{:S(2)}) %collective-permute-start.3) | collective-permute-done | bytes 131104 | tf_op jit(solution)/shard_map/ppermute | solution.py:53
  22.3 12.6 %collective-permute-done.8.refs_2_ = f32[16,32,128]{2,1,0:T(8,128)} collective-permute-done((f32[16,32,128]{2,1,0:T(8,128)S(1)}, f32[16,32,128]{2,1,0:T(8,128)}, u32[]{:S(2)}, u32[]{:S(2)}) %collective-permute-start.8) | collective-permute-done | bytes 262176 | tf_op jit(solution)/shard_map/ppermute | solution.py:53
  41.0 16.9 %collective-permute-done.5.u2 = f32[4,32,128]{2,1,0:T(8,128)S(1)} collective-permute-done((f32[4,32,128]{2,1,0:T(8,128)S(1)}, f32[4,32,128]{2,1,0:T(8,128)S(1)}, u32[]{:S(2)}, u32[]{:S(2)}) %collective-permute-start.5) | collective-permute-done | bytes 65568 | tf_op jit(solution)/shard_map/ppermute | solution.py:53
  58.4 3.6 %collective-permute-done.6.u3 = f32[4,32,128]{2,1,0:T(8,128)S(1)} collective-permute-done((f32[4,32,128]{2,1,0:T(8,128)S(1)}, f32[4,32,128]{2,1,0:T(8,128)S(1)}, u32[]{:S(2)}, u32[]{:S(2)}) %collective-permute-start.6) | collective-permute-done | bytes 65568 | tf_op jit(solution)/shard_map/ppermute | solution.py:53
  62.5 3.0 %collective-permute-start.10 = (f32[4,32,128]{2,1,0:T(8,128)S(1)}, f32[4,32,128]{2,1,0:T(8,128)S(1)}, u32[]{:S(2)}, u32[]{:S(2)}) collective-permute-start(f32[4,32,128]{2,1,0:T(8,128)S(1)} %shard_map.50.forward_ref), channel_id=1, source_target_pairs={{0,16},{4,20},{8,24},{12,28},{16,0},{20,4},{24,8},{28,12},{1,17},{... | collective-permute-start | bytes 196616 | tf_op jit(solution)/shard_map/ppermute | solution.py:53
  65.6 3.8 %collective-permute-done.10 = f32[4,32,128]{2,1,0:T(8,128)S(1)} collective-permute-done((f32[4,32,128]{2,1,0:T(8,128)S(1)}, f32[4,32,128]{2,1,0:T(8,128)S(1)}, u32[]{:S(2)}, u32[]{:S(2)}) %collective-permute-start.10) | collective-permute-done | bytes 65568 | tf_op jit(solution)/shard_map/ppermute | solution.py:53
  71.1 4.2 %collective-permute-done.13.x3 = f32[8,32,128]{2,1,0:T(8,128)S(1)} collective-permute-done((f32[8,32,128]{2,1,0:T(8,128)S(1)}, f32[8,32,128]{2,1,0:T(8,128)S(1)}, u32[]{:S(2)}, u32[]{:S(2)}) %collective-permute-start.13) | collective-permute-done | bytes 131104 | tf_op jit(solution)/shard_map/ppermute | solution.py:53
  81.5 3.6 %shard_map.52.forward_ref = f32[4,32,128]{2,1,0:T(8,128)S(1)} custom-call(s32[64]{0:T(128)S(1)} %get-tuple-element.81.slot_ref, f32[8,32,128]{2,1,0:T(8,128)S(1)} %pad_maximum_fusion.1.x0, f32[8,32,128]{2,1,0:T(8,128)S(1)} %collective-permute-done.11.x1, f32[8,32,128]{2,1,0:T(8,128)S(1)} %collective-permute-done.12.x2, ...), custom_call_target="tpu_custom_call" | custom-call | flops 402653184 | bytes 4194304 | tf_op jit(solution)/shard_map/pallas_call | solution.py:356
  85.2 3.3 %collective-permute-start.17 = (f32[4,32,128]{2,1,0:T(8,128)S(1)}, f32[4,32,128]{2,1,0:T(8,128)S(1)}, u32[]{:S(2)}, u32[]{:S(2)}) collective-permute-start(f32[4,32,128]{2,1,0:T(8,128)S(1)} %shard_map.52.forward_ref), channel_id=1, source_target_pairs={{0,16},{4,20},{8,24},{12,28},{16,0},{20,4},{24,8},{28,12},{1,17},{... | collective-permute-start | bytes 196616 | tf_op jit(solution)/shard_map/ppermute | solution.py:53
  88.5 2.8 %collective-permute-done.17 = f32[4,32,128]{2,1,0:T(8,128)S(1)} collective-permute-done((f32[4,32,128]{2,1,0:T(8,128)S(1)}, f32[4,32,128]{2,1,0:T(8,128)S(1)}, u32[]{:S(2)}, u32[]{:S(2)}) %collective-permute-start.17) | collective-permute-done | bytes 65568 | tf_op jit(solution)/shard_map/ppermute | solution.py:53
  99.5 5.6 %shard_map.54 = (f32[4,32,128]{2,1,0:T(8,128)S(1)}, f32[8,32,128]{2,1,0:T(8,128)S(1)}, f32[8,32,128]{2,1,0:T(8,128)S(1)}, f32[8,32,128]{2,1,0:T(8,128)S(1)}, f32[8,32,128]{2,1,0:T(8,128)S(1)}) custom-call(s32[64]{0:T(128)S(1)} %get-tuple-element.80.slot_ref, f32[8,32,128]{2,1,0:T(8,128)S(1)} %pad_maximum_fusion.2.x0, ...), custom_call_target="tpu_custom_call" | custom-call | flops 805306368 | bytes 4194304 | tf_op jit(solution)/shard_map/pallas_call | solution.py:363
  106.0 2.6 %collective-permute-start.26 = (f32[8,32,128]{2,1,0:T(8,128)S(1)}, f32[8,32,128]{2,1,0:T(8,128)S(1)}, u32[]{:S(2)}, u32[]{:S(2)}) collective-permute-start(f32[8,32,128]{2,1,0:T(8,128)S(1)} %get-tuple-element.45), channel_id=1, source_target_pairs={{0,12},{4,8},{8,4},{12,0},{16,28},{20,24},{24,20},{28,16},{1,13},{... | collective-permute-start | bytes 393224 | tf_op jit(solution)/shard_map/ppermute | solution.py:53
  113.0 3.7 %collective-permute-start.27 = (f32[4,32,128]{2,1,0:T(8,128)S(1)}, f32[4,32,128]{2,1,0:T(8,128)S(1)}, u32[]{:S(2)}, u32[]{:S(2)}) collective-permute-start(f32[4,32,128]{2,1,0:T(8,128)S(1)} %get-tuple-element.78), channel_id=1, source_target_pairs={{0,16},{4,20},{8,24},{12,28},{16,0},{20,4},{24,8},{28,12},{1,17},{... | collective-permute-start | bytes 196616 | tf_op jit(solution)/shard_map/ppermute | solution.py:53
  116.7 2.9 %collective-permute-done.27.ret1 = f32[4,32,128]{2,1,0:T(8,128)S(1)} collective-permute-done((f32[4,32,128]{2,1,0:T(8,128)S(1)}, f32[4,32,128]{2,1,0:T(8,128)S(1)}, u32[]{:S(2)}, u32[]{:S(2)}) %collective-permute-start.27) | collective-permute-done | bytes 65568 | tf_op jit(solution)/shard_map/ppermute | solution.py:53
  119.6 3.4 %shard_map.55 = (f32[4,32,128]{2,1,0:T(8,128)S(1)}, f32[8,32,128]{2,1,0:T(8,128)S(1)}, f32[8,32,128]{2,1,0:T(8,128)S(1)}, f32[8,32,128]{2,1,0:T(8,128)S(1)}, f32[8,32,128]{2,1,0:T(8,128)S(1)}) custom-call(s32[64]{0:T(128)S(1)} %get-tuple-element.81.slot_ref, f32[4,32,128]{2,1,0:T(8,128)S(1)} %get-tuple-element.79.ret0, ...), custom_call_target="tpu_custom_call" | custom-call | flops 402653184 | bytes 4194304 | tf_op jit(solution)/shard_map/pallas_call | solution.py:369
  128.4 2.9 %collective-permute-done.30 = f32[8,32,128]{2,1,0:T(8,128)S(1)} collective-permute-done((f32[8,32,128]{2,1,0:T(8,128)S(1)}, f32[8,32,128]{2,1,0:T(8,128)S(1)}, u32[]{:S(2)}, u32[]{:S(2)}) %collective-permute-start.30) | collective-permute-done | bytes 131104 | tf_op jit(solution)/shard_map/ppermute | solution.py:53
  131.3 2.8 %collective-permute-start.31 = (f32[4,32,128]{2,1,0:T(8,128)S(1)}, f32[4,32,128]{2,1,0:T(8,128)S(1)}, u32[]{:S(2)}, u32[]{:S(2)}) collective-permute-start(f32[4,32,128]{2,1,0:T(8,128)S(1)} %get-tuple-element.76), channel_id=1, source_target_pairs={{0,16},{4,20},{8,24},{12,28},{16,0},{20,4},{24,8},{28,12},{1,17},{... | collective-permute-start | bytes 196616 | tf_op jit(solution)/shard_map/ppermute | solution.py:53
  134.6 2.7 %collective-permute-done.31.ret1 = f32[4,32,128]{2,1,0:T(8,128)S(1)} collective-permute-done((f32[4,32,128]{2,1,0:T(8,128)S(1)}, f32[4,32,128]{2,1,0:T(8,128)S(1)}, u32[]{:S(2)}, u32[]{:S(2)}) %collective-permute-start.31) | collective-permute-done | bytes 65568 | tf_op jit(solution)/shard_map/ppermute | solution.py:53
  137.4 3.4 %shard_map.57 = (f32[4,32,128]{2,1,0:T(8,128)S(1)}, f32[8,32,128]{2,1,0:T(8,128)S(1)}, f32[8,32,128]{2,1,0:T(8,128)S(1)}, f32[8,32,128]{2,1,0:T(8,128)S(1)}, f32[8,32,128]{2,1,0:T(8,128)S(1)}) custom-call(s32[64]{0:T(128)S(1)} %get-tuple-element.82.slot_ref, f32[4,32,128]{2,1,0:T(8,128)S(1)} %get-tuple-element.77.ret0, ...), custom_call_target="tpu_custom_call" | custom-call | flops 402653184 | bytes 4194304 | tf_op jit(solution)/shard_map/pallas_call | solution.py:369
  145.9 2.8 %collective-permute-done.37 = f32[8,32,128]{2,1,0:T(8,128)S(1)} collective-permute-done((f32[8,32,128]{2,1,0:T(8,128)S(1)}, f32[8,32,128]{2,1,0:T(8,128)S(1)}, u32[]{:S(2)}, u32[]{:S(2)}) %collective-permute-start.37) | collective-permute-done | bytes 131104 | tf_op jit(solution)/shard_map/ppermute | solution.py:53
  151.3 3.2 %collective-permute-done.38.ret1 = f32[4,32,128]{2,1,0:T(8,128)S(1)} collective-permute-done((f32[4,32,128]{2,1,0:T(8,128)S(1)}, f32[4,32,128]{2,1,0:T(8,128)S(1)}, u32[]{:S(2)}, u32[]{:S(2)}) %collective-permute-start.38) | collective-permute-done | bytes 65568 | tf_op jit(solution)/shard_map/ppermute | solution.py:53
  158.6 2.6 %collective-permute-done.40.refs_2_ = f32[4,32,128]{2,1,0:T(8,128)S(1)} collective-permute-done((f32[4,32,128]{2,1,0:T(8,128)S(1)}, f32[4,32,128]{2,1,0:T(8,128)S(1)}, u32[]{:S(2)}, u32[]{:S(2)}) %collective-permute-start.40) | collective-permute-done | bytes 65568 | tf_op jit(solution)/shard_map/ppermute | solution.py:53
  (99 shorter events, 61.6 us)
Async XLA Ops:
  2.2 37.2 %collective-permute-start.15 = (f32[4,16,32,128]{3,2,1,0:T(8,128)S(1)}, f32[4,16,32,128]{3,2,1,0:T(8,128)}, u32[]{:S(2)}, u32[]{:S(2)}) collective-permute-start(f32[4,16,32,128]{3,2,1,0:T(8,128)S(1)} %get-tuple-element.65.refs_0_), channel_id=1, source_target_pairs={{0,2},{1,3},{2,0},{3,1},{4,6},{5,7},{6,4},{7,5},{8,10},{9,11},{10,... | collective-permute-start | bytes 3145736 | tf_op jit(solution)/shard_map/ppermute | solution.py:53
  6.6 6.5 %collective-permute-start = (f32[4,32,128]{2,1,0:T(8,128)S(1)}, f32[4,32,128]{2,1,0:T(8,128)}, u32[]{:S(2)}, u32[]{:S(2)}) collective-permute-start(f32[4,32,128]{2,1,0:T(8,128)S(1)} %shard_map.46), channel_id=1, source_target_pairs={{0,16},{4,20},{8,24},{12,28},{16,0},{20,4},{24,8},{28,12},{1,17},{... | collective-permute-start | bytes 196616 | tf_op jit(solution)/shard_map/ppermute | solution.py:53
  9.2 25.8 %collective-permute-start.8 = (f32[16,32,128]{2,1,0:T(8,128)S(1)}, f32[16,32,128]{2,1,0:T(8,128)}, u32[]{:S(2)}, u32[]{:S(2)}) collective-permute-start(f32[16,32,128]{2,1,0:T(8,128)S(1)} %bitcast.20), channel_id=1, source_target_pairs={{0,2},{1,3},{2,0},{3,1},{4,6},{5,7},{6,4},{7,5},{8,10},{9,11},{10,... | collective-permute-start | bytes 786440 | tf_op jit(solution)/shard_map/ppermute | solution.py:53
  9.7 55.9 %collective-permute-start.22 = (f32[4,16,32,128]{3,2,1,0:T(8,128)S(1)}, f32[4,16,32,128]{3,2,1,0:T(8,128)}, u32[]{:S(2)}, u32[]{:S(2)}) collective-permute-start(f32[4,16,32,128]{3,2,1,0:T(8,128)S(1)} %get-tuple-element.63.refs_0_), channel_id=1, source_target_pairs={{0,2},{1,3},{2,0},{3,1},{4,6},{5,7},{6,4},{7,5},{8,10},{9,11},{10,... | collective-permute-start | bytes 3145736 | tf_op jit(solution)/shard_map/ppermute | solution.py:53
  13.9 6.5 %collective-permute-start.3 = (f32[8,32,128]{2,1,0:T(8,128)S(1)}, f32[8,32,128]{2,1,0:T(8,128)S(1)}, u32[]{:S(2)}, u32[]{:S(2)}) collective-permute-start(f32[8,32,128]{2,1,0:T(8,128)S(1)} %pad_maximum_fusion.x0), channel_id=1, source_target_pairs={{0,12},{4,8},{8,4},{12,0},{16,28},{20,24},{24,20},{28,16},{1,13},{... | collective-permute-start | bytes 393224 | tf_op jit(solution)/shard_map/ppermute | solution.py:53
  20.4 16.8 %collective-permute-start.7 = (f32[16,32,128]{2,1,0:T(8,128)S(1)}, f32[16,32,128]{2,1,0:T(8,128)S(1)}, u32[]{:S(2)}, u32[]{:S(2)}) collective-permute-start(f32[16,32,128]{2,1,0:T(8,128)S(1)} %bitcast.21), channel_id=1, source_target_pairs={{0,1},{1,0},{2,3},{3,2},{4,5},{5,4},{6,7},{7,6},{8,9},{9,8},{10,11... | collective-permute-start | bytes 786440 | tf_op jit(solution)/shard_map/ppermute | solution.py:53
  21.8 13.2 %collective-permute-start.1 = (f32[8,32,128]{2,1,0:T(8,128)S(1)}, f32[8,32,128]{2,1,0:T(8,128)S(1)}, u32[]{:S(2)}, u32[]{:S(2)}) collective-permute-start(f32[8,32,128]{2,1,0:T(8,128)S(1)} %pad_maximum_fusion.x0), channel_id=1, source_target_pairs={{0,4},{4,0},{8,12},{12,8},{16,20},{20,16},{24,28},{28,24},{1,5},{5... | collective-permute-start | bytes 393224 | tf_op jit(solution)/shard_map/ppermute | solution.py:53
  35.0 40.3 %collective-permute-start.14 = (f32[4,16,32,128]{3,2,1,0:T(8,128)S(1)}, f32[4,16,32,128]{3,2,1,0:T(8,128)S(1)}, u32[]{:S(2)}, u32[]{:S(2)}) collective-permute-start(f32[4,16,32,128]{3,2,1,0:T(8,128)S(1)} %get-tuple-element.65.refs_0_), channel_id=1, source_target_pairs={{0,1},{1,0},{2,3},{3,2},{4,5},{5,4},{6,7},{7,6},{8,9},{9,8},{10,11... | collective-permute-start | bytes 3145736 | tf_op jit(solution)/shard_map/ppermute | solution.py:53
  37.3 20.6 %collective-permute-start.5 = (f32[4,32,128]{2,1,0:T(8,128)S(1)}, f32[4,32,128]{2,1,0:T(8,128)S(1)}, u32[]{:S(2)}, u32[]{:S(2)}) collective-permute-start(f32[4,32,128]{2,1,0:T(8,128)S(1)} %get-tuple-element.36), channel_id=1, source_target_pairs={{0,2},{1,3},{2,0},{3,1},{4,6},{5,7},{6,4},{7,5},{8,10},{9,11},{10,... | collective-permute-start | bytes 196616 | tf_op jit(solution)/shard_map/ppermute | solution.py:53
  39.4 37.2 %collective-permute-start.16 = (f32[4,16,32,128]{3,2,1,0:T(8,128)}, f32[4,16,32,128]{3,2,1,0:T(8,128)S(1)}, u32[]{:S(2)}, u32[]{:S(2)}) collective-permute-start(f32[4,16,32,128]{3,2,1,0:T(8,128)} %collective-permute-done.15.refs_2_), channel_id=1, source_target_pairs={{0,1},{1,0},{2,3},{3,2},{4,5},{5,4},{6,7},{7,6},{8,9},{9,8},{10,11... | collective-permute-start | bytes 3145736 | tf_op jit(solution)/shard_map/ppermute | solution.py:53
  40.6 53.9 %collective-permute-start.21 = (f32[4,16,32,128]{3,2,1,0:T(8,128)S(1)}, f32[4,16,32,128]{3,2,1,0:T(8,128)S(1)}, u32[]{:S(2)}, u32[]{:S(2)}) collective-permute-start(f32[4,16,32,128]{3,2,1,0:T(8,128)S(1)} %get-tuple-element.63.refs_0_), channel_id=1, source_target_pairs={{0,1},{1,0},{2,3},{3,2},{4,5},{5,4},{6,7},{7,6},{8,9},{9,8},{10,11... | collective-permute-start | bytes 3145736 | tf_op jit(solution)/shard_map/ppermute | solution.py:53
  62.5 6.8 %collective-permute-start.10 = (f32[4,32,128]{2,1,0:T(8,128)S(1)}, f32[4,32,128]{2,1,0:T(8,128)S(1)}, u32[]{:S(2)}, u32[]{:S(2)}) collective-permute-start(f32[4,32,128]{2,1,0:T(8,128)S(1)} %shard_map.50.forward_ref), channel_id=1, source_target_pairs={{0,16},{4,20},{8,24},{12,28},{16,0},{20,4},{24,8},{28,12},{1,17},{... | collective-permute-start | bytes 196616 | tf_op jit(solution)/shard_map/ppermute | solution.py:53
  65.6 29.3 %collective-permute-start.23 = (f32[4,16,32,128]{3,2,1,0:T(8,128)}, f32[4,16,32,128]{3,2,1,0:T(8,128)S(1)}, u32[]{:S(2)}, u32[]{:S(2)}) collective-permute-start(f32[4,16,32,128]{3,2,1,0:T(8,128)} %collective-permute-done.22.refs_2_), channel_id=1, source_target_pairs={{0,1},{1,0},{2,3},{3,2},{4,5},{5,4},{6,7},{7,6},{8,9},{9,8},{10,11... | collective-permute-start | bytes 3145736 | tf_op jit(solution)/shard_map/ppermute | solution.py:53
  69.3 5.9 %collective-permute-start.13 = (f32[8,32,128]{2,1,0:T(8,128)S(1)}, f32[8,32,128]{2,1,0:T(8,128)S(1)}, u32[]{:S(2)}, u32[]{:S(2)}) collective-permute-start(f32[8,32,128]{2,1,0:T(8,128)S(1)} %pad_maximum_fusion.1.x0), channel_id=1, source_target_pairs={{0,12},{4,8},{8,4},{12,0},{16,28},{20,24},{24,20},{28,16},{1,13},{... | collective-permute-start | bytes 393224 | tf_op jit(solution)/shard_map/ppermute | solution.py:53
  75.3 33.3 %collective-permute-start.33 = (f32[4,16,32,128]{3,2,1,0:T(8,128)S(1)}, f32[4,16,32,128]{3,2,1,0:T(8,128)S(1)}, u32[]{:S(2)}, u32[]{:S(2)}) collective-permute-start(f32[4,16,32,128]{3,2,1,0:T(8,128)S(1)} %get-tuple-element.64.lower_ref.refs_0_), channel_id=1, source_target_pairs={{0,2},{1,3},{2,0},{3,1},{4,6},{5,7},{6,4},{7,5},{8,10},{9,11},{10,... | collective-permute-start | bytes 3145736 | tf_op jit(solution)/shard_map/ppermute | solution.py:53
  85.2 6.1 %collective-permute-start.17 = (f32[4,32,128]{2,1,0:T(8,128)S(1)}, f32[4,32,128]{2,1,0:T(8,128)S(1)}, u32[]{:S(2)}, u32[]{:S(2)}) collective-permute-start(f32[4,32,128]{2,1,0:T(8,128)S(1)} %shard_map.52.forward_ref), channel_id=1, source_target_pairs={{0,16},{4,20},{8,24},{12,28},{16,0},{20,4},{24,8},{28,12},{1,17},{... | collective-permute-start | bytes 196616 | tf_op jit(solution)/shard_map/ppermute | solution.py:53
  92.5 6.4 %collective-permute-start.19 = (f32[8,32,128]{2,1,0:T(8,128)S(1)}, f32[8,32,128]{2,1,0:T(8,128)S(1)}, u32[]{:S(2)}, u32[]{:S(2)}) collective-permute-start(f32[8,32,128]{2,1,0:T(8,128)S(1)} %pad_maximum_fusion.2.x0), channel_id=1, source_target_pairs={{0,8},{4,12},{8,0},{12,4},{16,24},{20,28},{24,16},{28,20},{1,9},{5... | collective-permute-start | bytes 393224 | tf_op jit(solution)/shard_map/ppermute | solution.py:53
  106.0 7.0 %collective-permute-start.26 = (f32[8,32,128]{2,1,0:T(8,128)S(1)}, f32[8,32,128]{2,1,0:T(8,128)S(1)}, u32[]{:S(2)}, u32[]{:S(2)}) collective-permute-start(f32[8,32,128]{2,1,0:T(8,128)S(1)} %get-tuple-element.45), channel_id=1, source_target_pairs={{0,12},{4,8},{8,4},{12,0},{16,28},{20,24},{24,20},{28,16},{1,13},{... | collective-permute-start | bytes 393224 | tf_op jit(solution)/shard_map/ppermute | solution.py:53
  108.6 25.5 %collective-permute-start.32 = (f32[4,16,32,128]{3,2,1,0:T(8,128)S(1)}, f32[4,16,32,128]{3,2,1,0:T(8,128)S(1)}, u32[]{:S(2)}, u32[]{:S(2)}) collective-permute-start(f32[4,16,32,128]{3,2,1,0:T(8,128)S(1)} %get-tuple-element.64.lower_ref.refs_0_), channel_id=1, source_target_pairs={{0,1},{1,0},{2,3},{3,2},{4,5},{5,4},{6,7},{7,6},{8,9},{9,8},{10,11... | collective-permute-start | bytes 3145736 | tf_op jit(solution)/shard_map/ppermute | solution.py:53
  108.6 25.5 %collective-permute-start.34 = (f32[4,16,32,128]{3,2,1,0:T(8,128)S(1)}, f32[4,16,32,128]{3,2,1,0:T(8,128)S(1)}, u32[]{:S(2)}, u32[]{:S(2)}) collective-permute-start(f32[4,16,32,128]{3,2,1,0:T(8,128)S(1)} %collective-permute-done.33.refs_2_), channel_id=1, source_target_pairs={{0,1},{1,0},{2,3},{3,2},{4,5},{5,4},{6,7},{7,6},{8,9},{9,8},{10,11... | collective-permute-start | bytes 3145736 | tf_op jit(solution)/shard_map/ppermute | solution.py:53
  113.0 6.6 %collective-permute-start.27 = (f32[4,32,128]{2,1,0:T(8,128)S(1)}, f32[4,32,128]{2,1,0:T(8,128)S(1)}, u32[]{:S(2)}, u32[]{:S(2)}) collective-permute-start(f32[4,32,128]{2,1,0:T(8,128)S(1)} %get-tuple-element.78), channel_id=1, source_target_pairs={{0,16},{4,20},{8,24},{12,28},{16,0},{20,4},{24,8},{28,12},{1,17},{... | collective-permute-start | bytes 196616 | tf_op jit(solution)/shard_map/ppermute | solution.py:53
  124.8 6.5 %collective-permute-start.30 = (f32[8,32,128]{2,1,0:T(8,128)S(1)}, f32[8,32,128]{2,1,0:T(8,128)S(1)}, u32[]{:S(2)}, u32[]{:S(2)}) collective-permute-start(f32[8,32,128]{2,1,0:T(8,128)S(1)} %get-tuple-element.49), channel_id=1, source_target_pairs={{0,12},{4,8},{8,4},{12,0},{16,28},{20,24},{24,20},{28,16},{1,13},{... | collective-permute-start | bytes 393224 | tf_op jit(solution)/shard_map/ppermute | solution.py:53
  131.3 6.0 %collective-permute-start.31 = (f32[4,32,128]{2,1,0:T(8,128)S(1)}, f32[4,32,128]{2,1,0:T(8,128)S(1)}, u32[]{:S(2)}, u32[]{:S(2)}) collective-permute-start(f32[4,32,128]{2,1,0:T(8,128)S(1)} %get-tuple-element.76), channel_id=1, source_target_pairs={{0,16},{4,20},{8,24},{12,28},{16,0},{20,4},{24,8},{28,12},{1,17},{... | collective-permute-start | bytes 196616 | tf_op jit(solution)/shard_map/ppermute | solution.py:53
  142.1 6.6 %collective-permute-start.37 = (f32[8,32,128]{2,1,0:T(8,128)S(1)}, f32[8,32,128]{2,1,0:T(8,128)S(1)}, u32[]{:S(2)}, u32[]{:S(2)}) collective-permute-start(f32[8,32,128]{2,1,0:T(8,128)S(1)} %get-tuple-element.55), channel_id=1, source_target_pairs={{0,12},{4,8},{8,4},{12,0},{16,28},{20,24},{24,20},{28,16},{1,13},{... | collective-permute-start | bytes 393224 | tf_op jit(solution)/shard_map/ppermute | solution.py:53
  (21 other events, 100.9 us)

commit v2 on v1

v2 whole, which is shorter than its diff:
```python
import functools

import jax
import jax.numpy as jnp
from jax import lax
from jax.experimental import pallas as pl
from jax.experimental.pallas import tpu as pltpu
from jax.sharding import PartitionSpec as P

F32 = jnp.float32
BF16 = jnp.bfloat16
EXACT = lax.Precision.HIGHEST
VMEM = pl.BlockSpec(memory_space=pltpu.VMEM)
SMEM = pl.BlockSpec(memory_space=pltpu.SMEM)
ANY = pl.BlockSpec(memory_space=pl.ANY)
HBM = pl.BlockSpec(memory_space=pltpu.HBM)
TINY = pl.CostEstimate(flops=1, bytes_accessed=1, transcendentals=0)


def nn(a, b):
    return lax.dot_general(a, b, (((1,), (0,)), ((), ())), precision=EXACT, preferred_element_type=F32)


def half(a, b, contract):
    return lax.dot_general(a, b, ((contract[:1], contract[1:]), ((), ())), preferred_element_type=F32)


def split(value):
    high = value.astype(BF16)
    return high, (value - high.astype(F32)).astype(BF16)


def times(value, pair):
    rows, width = value.shape[0], pair.shape[1] // 2
    both = half(jnp.concatenate(split(value), axis=0), pair, (1, 0))
    both = both[:, :width] + both[:, width:]
    return both[:rows] + both[rows:]


def times_turned(value, pair):
    rows = value.shape[0]
    high, low = split(value)
    wide = jnp.concatenate([jnp.concatenate([high, high], axis=1), jnp.concatenate([low, low], axis=1)], axis=0)
    both = half(wide, pair, (1, 1))
    return both[:rows] + both[rows:]


def call(body, out_shape, in_specs, scratch=(), limit=24):
    return pl.pallas_call(
        body,
        out_shape=out_shape,
        in_specs=in_specs,
        out_specs=jax.tree.map(lambda _: VMEM, out_shape),
        scratch_shapes=list(scratch),
        compiler_params=pltpu.CompilerParams(vmem_limit_bytes=limit * 1024 * 1024),
        cost_estimate=TINY,
    )


def swap(value, axis, mask):
    size = lax.axis_size(axis)
    return lax.ppermute(value, axis, [(i, i ^ mask) for i in range(size)])


def far_masks(size):
    masks, mask = [], size // 2
    while mask >= 4:
        masks.append(mask)
        mask //= 2
    return masks


def slot_of(mask, size):
    place = (mask & 3) * (size // 4)
    for step, far in enumerate(far_masks(size)):
        place = place + jnp.where((mask & far) != 0, 1 << step, 0)
    return place


def gather_row(own):
    held = own
    for mask in far_masks(lax.axis_size("row")):
        got = swap(held, "row", mask)
        held = jnp.concatenate([held, got], axis=0)
    return got, [held] + [swap(held, "row", mask) for mask in (1, 2, 3)]


def scatter_row(parts):
    total = parts[0]
    got = [swap(part, "row", mask) for mask, part in zip((1, 2, 3), parts[1:])]
    total = total + got[0] + got[1] + got[2]
    other = None
    for mask in reversed(far_masks(lax.axis_size("row"))):
        if other is not None:
            total = total + other
        keep, send = jnp.split(total, 2, axis=0)
        total, other = keep, swap(send, "row", mask)
    return total, other


def first_kernel(level, inverse_ref, sides_ref, lower_ref, out_ref, early_ref, inverse, sides, sems):
    copies = [
        pltpu.make_async_copy(inverse_ref.at[0], inverse, sems.at[0]),
        pltpu.make_async_copy(sides_ref.at[0], sides, sems.at[1]),
        pltpu.make_async_copy(lower_ref.at[level, pl.ds(0, early_ref.shape[0])], early_ref, sems.at[2]),
    ]
    for copy in copies:
        copy.start()
    for copy in copies[:2]:
        copy.wait()
    for j in range(out_ref.shape[0]):
        out_ref[j] = nn(inverse[j], sides[j])
    copies[2].wait()


def turn_kernel(col_ref, sides_ref, out_ref, whole):
    count = out_ref.shape[1]
    start = pl.multiple_of(col_ref[0] * count, count)
    for i in range(out_ref.shape[0]):
        whole[i % 2] = sides_ref[i].T
        out_ref[i] = whole[i % 2, pl.ds(start, count), :]


def join_kernel(col_ref, *refs):
    parts, out_ref = refs[:-1], refs[-1]
    share, width = parts[0].shape[2:]
    for mask, part in enumerate(parts):
        offset = pl.multiple_of((col_ref[0] ^ mask) * share, share)
        for d in range(part.shape[1]):
            high, low = split(part[0, d])
            out_ref[0, pl.ds(d * width + offset, share), :width] = high
            out_ref[0, pl.ds(d * width + offset, share), width:] = low


def join_inverse_kernel(col_ref, *refs):
    parts, (out_ref, token_ref) = refs[:-2], refs[-2:]
    token_ref[...] = jnp.zeros_like(token_ref)
    share, width = parts[0].shape[1:]
    for mask, part in enumerate(parts):
        offset = pl.multiple_of((col_ref[0] ^ mask) * share, share)
        for i in range(part.shape[0]):
            high, low = split(part[i])
            out_ref[i, pl.ds(offset, share), :width] = high
            out_ref[i, pl.ds(offset, share), width:] = low


def stand_kernel(lower_ref, out_ref, own, sem):
    count, fan_in, share, width = own.shape
    copy = pltpu.make_async_copy(lower_ref.at[0], own, sem)
    copy.start()
    copy.wait()
    for j in range(count):
        high, low = split(own[j].reshape(fan_in * share, width).T)
        out_ref[j, :width] = high
        out_ref[j, width:] = low


def partial_kernel(col_ref, slot_ref, x0, x1, x2, x3, lower_ref, early_ref, token_ref, *refs):
    outs, (blocks, picked, turned) = refs[:-3], refs[-3:]
    count = lower_ref.shape[0]
    fan_in = slot_ref.shape[0] // count
    each, share, columns = x0.shape
    width = lower_ref.shape[1] // 2
    for q, x in enumerate((x0, x1, x2, x3)):
        for i in range(each):
            high, low = split(x[i])
            blocks[q * each + i, :, :columns] = high
            blocks[q * each + i, :, columns:] = low
    for j in range(count):
        for d in range(fan_in):
            picked[j, d * share:(d + 1) * share, :] = blocks[slot_ref[j * fan_in + d]]
    for j in range(count):
        both = half(lower_ref[j], picked[j], (1, 0))
        both = both[:width] + both[width:]
        turned[j] = (both[:, :columns] + both[:, columns:]).T
    columns = outs[0].shape[1]
    for place, mask in enumerate((0, 2, 1, 3)):
        start = pl.multiple_of((col_ref[0] ^ mask) * columns, columns)
        out = outs[place] if place < 2 else outs[2].at[pl.ds((place - 2) * count, count)]
        for j in range(count):
            out[j] = turned[j, pl.ds(start, columns), :]


def solve_first_kernel(u0, u1, u2, sides_ref, inverse_ref, out_ref):
    for j in range(out_ref.shape[0]):
        out_ref[j] = times_turned(sides_ref[j] - ((u0[j] + u1[j]) + u2[j]), inverse_ref[j])


def block_of(lower, j):
    some = lower[0].shape[0]
    return lower[j // some][j % some]


def forward_levels(slot_ref, xs, sides_ref, inverse_ref, lower, out_ref, blocks, picked):
    count, columns, width = out_ref.shape
    fan_in = slot_ref.shape[0] // count
    each = xs[0].shape[0]
    for q, x in enumerate(xs):
        for i in range(each):
            high, low = split(x[i])
            blocks[q * each + i, :columns] = high
            blocks[q * each + i, columns:] = low
    for j in range(count):
        for d in range(fan_in):
            picked[j, :, d * width:(d + 1) * width] = blocks[slot_ref[j * fan_in + d]]
    rest = []
    for j in range(count):
        both = half(picked[j], block_of(lower, j), (1, 0))
        both = both[:, :width] + both[:, width:]
        rest.append(sides_ref[j] - (both[:columns] + both[columns:]))
    for j in range(count):
        out_ref[j] = times_turned(rest[j], inverse_ref[j])


def backward_terms(slot_ref, solved, lower, outs, total):
    count, _, width = solved.shape
    fan_in = slot_ref.shape[0] // count
    total[...] = jnp.zeros_like(total)
    for j in range(count):
        terms = times_turned(solved[j], block_of(lower, j))
        for d in range(fan_in):
            slot = slot_ref[j * fan_in + d]
            total[slot] = total[slot] + terms[:, d * width:(d + 1) * width]
    each = outs[0].shape[0]
    for q, out in enumerate(outs):
        out[...] = total[q * each:(q + 1) * each]


def forward_kernel(chunks, slot_ref, x0, x1, x2, x3, sides_ref, inverse_ref, *refs):
    lower, (out_ref, blocks, picked) = refs[:chunks], refs[chunks:]
    forward_levels(slot_ref, (x0, x1, x2, x3), sides_ref, inverse_ref, lower, out_ref, blocks, picked)


def top_kernel(chunks, slot_ref, x0, x1, x2, x3, sides_ref, inverse_ref, *refs):
    lower, outs = refs[:chunks], refs[chunks + 1:chunks + 5]
    sol_ref, (blocks, picked, solved, total) = refs[chunks], refs[chunks + 5:]
    forward_levels(slot_ref, (x0, x1, x2, x3), sides_ref, inverse_ref, lower, solved, blocks, picked)
    for j in range(sol_ref.shape[0]):
        sol_ref[j] = times(solved[j], inverse_ref[j])
    backward_terms(slot_ref, sol_ref, lower, outs, total)


def backward_kernel(chunks, slot_ref, ret0, ret1, forward_ref, inverse_ref, *refs):
    lower, outs = refs[:chunks], refs[chunks + 1:chunks + 5]
    sol_ref, total = refs[chunks], refs[chunks + 5]
    for j in range(sol_ref.shape[0]):
        sol_ref[j] = times(forward_ref[j] - (ret0[j] + ret1[j]), inverse_ref[j])
    backward_terms(slot_ref, sol_ref, lower, outs, total)


def last_kernel(col_ref, ret0, ret1, sides_ref, inverse_ref, s1, s2, s3, *refs):
    outs, (solved, packed) = refs[:-2], refs[-2:]
    count = sides_ref.shape[0]
    share = sides_ref.shape[2] // len(outs)
    for j in range(count):
        rest = times_turned(sides_ref[j], inverse_ref[j]) - (ret0[j] + ret1[j])
        solved[j] = times(rest, inverse_ref[j])
    for level, source in enumerate((solved, s1, s2, s3)):
        for c in range(len(outs)):
            packed[c, level] = jnp.concatenate(
                [source[j, :, c * share:(c + 1) * share] for j in range(count)], axis=1
            )
    for mask, out in enumerate(outs):
        out[...] = packed[col_ref[0] ^ mask]


def out_kernel(col_ref, *refs):
    parts, (out_ref, whole) = refs[:-2], refs[-2:]
    levels, count, share, columns = out_ref.shape
    piece = parts[0].shape[1]
    for mask, part in enumerate(parts):
        start = pl.multiple_of((col_ref[0] ^ mask) * piece, piece)
        for level in range(levels):
            whole[level, pl.ds(start, piece), :] = part[level]
    for level in range(levels):
        out_ref[level] = whole[level].T.reshape(count, share, columns)


def same_kernel(value_ref, *refs):
    refs[-1][...] = value_ref[...]


def after(value, *others):
    return pl.pallas_call(
        same_kernel,
        out_shape=jax.ShapeDtypeStruct(value.shape, value.dtype),
        in_specs=[VMEM] * (1 + len(others)),
        out_specs=VMEM,
        compiler_params=pltpu.CompilerParams(vmem_limit_bytes=8 * 1024 * 1024),
        cost_estimate=TINY,
    )(value, *others)


def pack_kernel(level, start, lower_ref, *refs):
    out_ref, sem = refs[-2:]
    copy = pltpu.make_async_copy(lower_ref.at[level, pl.ds(start, out_ref.shape[0])], out_ref, sem)
    copy.start()
    copy.wait()


def pack(lower_blocks, level, start, size, *others):
    return pl.pallas_call(
        functools.partial(pack_kernel, level, start),
        out_shape=jax.ShapeDtypeStruct((size,) + lower_blocks.shape[2:], F32),
        in_specs=[HBM] + [VMEM] * len(others),
        out_specs=VMEM,
        scratch_shapes=[pltpu.SemaphoreType.DMA],
        compiler_params=pltpu.CompilerParams(vmem_limit_bytes=8 * 1024 * 1024),
        cost_estimate=TINY,
    )(lower_blocks, *others)


def on_device(right_sides, inverse_diag, lower_blocks, depends_on):
    levels, count, width, columns = right_sides.shape
    share = inverse_diag.shape[2]
    fan_in = lower_blocks.shape[2]
    rows, cols = lax.axis_size("row"), lax.axis_size("col")
    my_row, my_col = lax.axis_index("row"), lax.axis_index("col")
    col = my_col.astype(jnp.int32).reshape(1)
    mine = columns // cols
    entries = count * fan_in
    wanted = lax.dynamic_slice_in_dim(depends_on, my_row * count, count, 1).reshape(levels - 1, entries)
    slots = slot_of((wanted // count) ^ my_row, rows) * count + wanted % count
    slots = [slots[i] for i in range(levels - 1)]

    def like(*shape, dtype=F32):
        return jax.ShapeDtypeStruct(shape, dtype)

    block = like(count, mine, width)
    quarter = like(rows // 4 * count, mine, width)

    def join(level, start, across):
        some = across.shape[0]
        own_spec = pl.BlockSpec((None, 1, fan_in, share, width), lambda j: (level, start + j, 0, 0, 0))
        part_spec = pl.BlockSpec((1, fan_in, share, width), lambda j: (j, 0, 0, 0))
        out_spec = pl.BlockSpec((1, fan_in * width, 2 * width), lambda j: (j, 0, 0))
        return pl.pallas_call(
            join_kernel,
            grid=(some,),
            out_shape=like(some, fan_in * width, 2 * width, dtype=BF16),
            in_specs=[SMEM, own_spec, own_spec, part_spec, part_spec],
            out_specs=out_spec,
            compiler_params=pltpu.CompilerParams(vmem_limit_bytes=24 * 1024 * 1024),
            cost_estimate=TINY,
        )(col, lower_blocks, lower_beside, *near(across))

    def near(value):
        return value, swap(value, "col", 1)

    top = levels - 1
    middle = count // 2
    first, early = call(
        functools.partial(first_kernel, 1), [like(count, share, columns), like(middle, fan_in, share, width)], [HBM] * 3,
        scratch=[
            pltpu.VMEM((count, share, width), F32),
            pltpu.VMEM((count, width, columns), F32),
            pltpu.SemaphoreType.DMA((3,)),
        ],
        limit=60,
    )(inverse_diag, right_sides, lower_blocks)
    early = swap(early, "col", 2)
    _, gathered = gather_row(first)
    all_inverse = inverse_diag.reshape(levels * count, share, width)
    parts_inverse = near(all_inverse) + near(swap(all_inverse, "col", 2))
    lower_beside = swap(lower_blocks, "col", 1)

    inverse, token = call(
        join_inverse_kernel, [like(levels * count, width, 2 * width, dtype=BF16), like(8, width)], [SMEM] + [VMEM] * cols
    )(col, *parts_inverse)
    inverse = [inverse[i * count:(i + 1) * count] for i in range(levels)]

    sides = call(
        turn_kernel, like(levels * count, mine, width), [SMEM, VMEM],
        scratch=[pltpu.VMEM((2, columns, width), F32)],
    )(col, right_sides.reshape(levels * count, width, columns))
    sides = [sides[i * count:(i + 1) * count] for i in range(levels)]

    standing = call(
        stand_kernel, like(count, 2 * width, fan_in * share, dtype=BF16), [HBM],
        scratch=[pltpu.VMEM(lower_blocks.shape[1:], F32), pltpu.SemaphoreType.DMA],
    )(lower_blocks)
    kept, passed, sent = call(
        partial_kernel, [block] * 2 + [like(2 * count, mine, width)], [SMEM] * 2 + [VMEM] * 7,
        scratch=[
            pltpu.VMEM((rows * count, share, 2 * columns), BF16),
            pltpu.VMEM((count, fan_in * share, 2 * columns), BF16),
            pltpu.VMEM((count, columns, width), F32),
        ],
    )(col, slots[0], *gathered, standing, early, token)
    beside = swap(sent, "col", 1)
    across = swap(passed + beside[count:], "col", 2)

    late = swap(pack(lower_blocks, 1, middle, count - middle, across), "col", 2)

    picking = [
        pltpu.VMEM((rows * count, 2 * mine, width), BF16),
        pltpu.VMEM((count, 2 * mine, fan_in * width), BF16),
    ]
    total = [pltpu.VMEM((rows * count, mine, width), F32)]

    forward, lower = [None] * levels, [None] * (levels - 1)
    forward[1] = call(solve_first_kernel, block, [VMEM] * 5)(
        kept, beside[:count], across, sides[1], inverse[1]
    )

    got, gathered = gather_row(forward[1])
    whole_early = swap(pack(lower_blocks, 2, 0, middle, forward[1]), "col", 2)
    whole_late = swap(pack(lower_blocks, 2, middle, count - middle, got), "col", 2)
    lower[1] = [
        join(1, 0, early),
        join(1, middle, after(late, got)),
    ]
    forward[2] = call(
        functools.partial(forward_kernel, len(lower[1])), block, [SMEM] + [VMEM] * 6 + [VMEM] * len(lower[1]),
        scratch=picking,
    )(slots[1], *gathered, sides[2], inverse[2], *lower[1])

    last = swap(pack(lower_blocks, 0, 0, count, forward[2]), "col", 2)
    got, gathered = gather_row(forward[2])
    lower[2] = [
        join(2, 0, after(whole_early, got)),
        join(2, middle, after(whole_late, *gathered[1:])),
    ]

    solved = [None] * levels
    solved[top], *terms = call(
        functools.partial(top_kernel, len(lower[2])), [block] + [quarter] * 4,
        [SMEM] + [VMEM] * 6 + [VMEM] * len(lower[2]),
        scratch=picking + [pltpu.VMEM((count, mine, width), F32)] + total,
    )(slots[2], *gathered, sides[top], inverse[top], *lower[2])

    returned = scatter_row(terms)
    solved[2], *terms = call(
        functools.partial(backward_kernel, len(lower[1])), [block] + [quarter] * 4,
        [SMEM] + [VMEM] * 4 + [VMEM] * len(lower[1]), scratch=total,
    )(slots[1], *returned, forward[2], inverse[2], *lower[1])

    returned = scatter_row(terms)
    lower[0] = [join(0, 0, after(last, solved[2]))]
    solved[1], *terms = call(
        functools.partial(backward_kernel, len(lower[0])), [block] + [quarter] * 4,
        [SMEM] + [VMEM] * 4 + [VMEM] * len(lower[0]), scratch=total,
    )(slots[0], *returned, forward[1], inverse[1], *lower[0])

    pieces = call(
        last_kernel, [like(levels, mine, count * share)] * cols, [SMEM] + [VMEM] * (4 + top),
        scratch=[
            pltpu.VMEM((count, mine, width), F32),
            pltpu.VMEM((cols, levels, mine, count * share), F32),
        ],
    )(col, *scatter_row(terms), sides[0], inverse[0], *solved[1:])
    pieces = [pieces[0]] + [swap(pieces[mask], "col", mask) for mask in range(1, cols)]
    return call(
        out_kernel, like(levels, count, share, columns), [SMEM] + [VMEM] * cols,
        scratch=[pltpu.VMEM((levels, columns, count * share), F32)],
    )(col, *pieces)


def solution(mesh):
    return jax.shard_map(
        on_device,
        mesh=mesh,
        in_specs=(
            P(None, "row", None, None),
            P(None, "row", "col", None),
            P(None, "row", None, "col", None),
            P(),
        ),
        out_specs=P(None, "row", "col", None),
        check_vma=False,
    )
```

time: 164 us -> 139 us (0.85)
  waiting for transfers between devices: 78 us -> 57 us
  Pallas kernels: 27.7 us -> 24.9 us
    ppermute x42 -> x43, waiting for transfers between devices: 78 us -> 57 us  [swap(): return lax.ppermute(value, axis, [(i, i ^ mask) for i in range(size)])]
    squeeze x3 -> x0, local copies, waits for them, and re-layouts: 3.18 us -> none  [the longest x1 2.2 us: on_device(): parts_lower[level] = collect(lower_blocks[level])]
    pallas_call x11 -> x22, Pallas kernels: 24.7 us -> 22.8 us  [the longest x5 7.92 us: join(): pl.pallas_call(join_kernel, grid=(some,), out_shape=like(some, fan_in * w...]
    ppermute x42 -> x43, starting transfers between devices: 51.7 us -> 52.8 us  [swap(): return lax.ppermute(value, axis, [(i, i ^ mask) for i in range(size)])]
  transfers between devices with their start and end apart: 42 -> 43, of which waited for: 26 -> 30; matrix products, arithmetic and copies ran while one was open for 1% -> 1% of each run, Pallas kernels for 13% -> 15%
where the time goes in v2:
time: 139 us
  waiting for transfers between devices  57 us (41%)
  starting transfers between devices  52.8 us (38%)
  Pallas kernels  24.9 us (18%)
  local copies, waits for them, and re-layouts  3.44 us (2%)
    ppermute x43, waiting for transfers between devices, swap(): return lax.ppermute(value, axis, [(i, i ^ mask) for i in range(size)])  57 us
    ppermute x43, starting transfers between devices, swap(): return lax.ppermute(value, axis, [(i, i ^ mask) for i in range(size)])  52.8 us
    pallas_call x5, Pallas kernels, join(): pl.pallas_call(join_kernel, grid=(some,), out_shape=like(some, fan_in * w...  7.92 us
    pallas_call x1, Pallas kernels, on_device(): call(functools.partial(top_kernel, len(lower[2])), [block] + [quarter] *...  3.04 us
  transfers between devices with their start and end apart: 43, of which 30 were waited for; matrix products, arithmetic and copies ran while one was open for 1% of the time, Pallas kernels for 15%

profile of v2, /device:TPU:0, one launch (start us, length us, event | category | flops | bytes accessed | tf_op | source)
XLA Modules:
  0.0 138.7 jit_solution(2039862186782990881)
XLA Ops:
  0.5 2.6 %collective-permute-start.6 = (f32[16,32,128]{2,1,0:T(8,128)}, f32[16,32,128]{2,1,0:T(8,128)}, u32[]{:S(2)}, u32[]{:S(2)}) collective-permute-start(f32[16,32,128]{2,1,0:T(8,128)} %bitcast.10), channel_id=1, source_target_pairs={{0,2},{1,3},{2,0},{3,1},{4,6},{5,7},{6,4},{7,5},{8,10},{9,11},{10,... | collective-permute-start | bytes 786440 | tf_op jit(solution)/shard_map/ppermute | solution.py:62
  3.2 2.2 %shard_map.46 = (f32[4,32,128]{2,1,0:T(8,128)}, f32[2,16,32,128]{3,2,1,0:T(8,128)}) custom-call(f32[4,4,32,128]{3,2,1,0:T(8,128)} %inverse_ref.1, f32[4,4,128,128]{3,2,1,0:T(8,128)} %sides_ref.1, f32[3,4,16,32,128]{4,3,2,1,0:T(8,128)} %refs_0_.9), custom_call_target="tpu_custom_call" | custom-call | flops 1 | bytes 1 | tf_op jit(solution)/shard_map/pallas_call | solution.py:352
  5.4 2.7 %collective-permute-start = (f32[4,32,128]{2,1,0:T(8,128)}, f32[4,32,128]{2,1,0:T(8,128)}, u32[]{:S(2)}, u32[]{:S(2)}) collective-permute-start(f32[4,32,128]{2,1,0:T(8,128)} %get-tuple-element.31), channel_id=1, source_target_pairs={{0,16},{4,20},{8,24},{12,28},{16,0},{20,4},{24,8},{28,12},{1,17},{... | collective-permute-start | bytes 196616 | tf_op jit(solution)/shard_map/ppermute | solution.py:62
  13.3 2.2 %collective-permute-start.3 = (f32[8,32,128]{2,1,0:T(8,128)S(1)}, f32[8,32,128]{2,1,0:T(8,128)S(1)}, u32[]{:S(2)}, u32[]{:S(2)}) collective-permute-start(f32[8,32,128]{2,1,0:T(8,128)S(1)} %constant_dynamic-update-slice_fusion.x0), channel_id=1, source_target_pairs={{0,12},{4,8},{8,4},{12,0},{16,28},{20,24},{24,20},{28,16},{1,13},{... | collective-permute-start | bytes 393224 | tf_op jit(solution)/shard_map/ppermute | solution.py:62
  18.0 2.5 %collective-permute-done.3.x3 = f32[8,32,128]{2,1,0:T(8,128)S(1)} collective-permute-done((f32[8,32,128]{2,1,0:T(8,128)S(1)}, f32[8,32,128]{2,1,0:T(8,128)S(1)}, u32[]{:S(2)}, u32[]{:S(2)}) %collective-permute-start.3) | collective-permute-done | bytes 131104 | tf_op jit(solution)/shard_map/ppermute | solution.py:62
  29.0 2.2 %collective-permute-done.9.u2.refs_0_ = f32[4,32,128]{2,1,0:T(8,128)S(1)} collective-permute-done((f32[4,32,128]{2,1,0:T(8,128)S(1)}, f32[4,32,128]{2,1,0:T(8,128)S(1)}, u32[]{:S(2)}, u32[]{:S(2)}) %collective-permute-start.9) | collective-permute-done | bytes 65568 | tf_op jit(solution)/shard_map/ppermute | solution.py:62
  33.3 3.0 %collective-permute-start.10 = (f32[4,32,128]{2,1,0:T(8,128)S(1)}, f32[4,32,128]{2,1,0:T(8,128)S(1)}, u32[]{:S(2)}, u32[]{:S(2)}) collective-permute-start(f32[4,32,128]{2,1,0:T(8,128)S(1)} %shard_map.51.refs_0_.forward_ref), channel_id=1, source_target_pairs={{0,16},{4,20},{8,24},{12,28},{16,0},{20,4},{24,8},{28,12},{1,17},{... | collective-permute-start | bytes 196616 | tf_op jit(solution)/shard_map/ppermute | solution.py:62
  36.3 2.3 %collective-permute-done.10.refs_0_ = f32[4,32,128]{2,1,0:T(8,128)S(1)} collective-permute-done((f32[4,32,128]{2,1,0:T(8,128)S(1)}, f32[4,32,128]{2,1,0:T(8,128)S(1)}, u32[]{:S(2)}, u32[]{:S(2)}) %collective-permute-start.10) | collective-permute-done | bytes 65568 | tf_op jit(solution)/shard_map/ppermute | solution.py:62
  38.6 5.6 %collective-permute-done.16.value_ref = f32[2,16,32,128]{3,2,1,0:T(8,128)S(1)} collective-permute-done((f32[2,16,32,128]{3,2,1,0:T(8,128)S(1)}, f32[2,16,32,128]{3,2,1,0:T(8,128)S(1)}, u32[]{:S(2)}, u32[]{:S(2)}) %collective-permute-start.16) | collective-permute-done | bytes 524320 | tf_op jit(solution)/shard_map/ppermute | solution.py:62
  46.6 2.5 %collective-permute-start.13 = (f32[8,32,128]{2,1,0:T(8,128)S(1)}, f32[8,32,128]{2,1,0:T(8,128)S(1)}, u32[]{:S(2)}, u32[]{:S(2)}) collective-permute-start(f32[8,32,128]{2,1,0:T(8,128)S(1)} %pad_maximum_fusion.x0), channel_id=1, source_target_pairs={{0,12},{4,8},{8,4},{12,0},{16,28},{20,24},{24,20},{28,16},{1,13},{... | collective-permute-start | bytes 393224 | tf_op jit(solution)/shard_map/ppermute | solution.py:62
  57.3 3.1 %collective-permute-start.18 = (f32[4,32,128]{2,1,0:T(8,128)S(1)}, f32[4,32,128]{2,1,0:T(8,128)S(1)}, u32[]{:S(2)}, u32[]{:S(2)}) collective-permute-start(f32[4,32,128]{2,1,0:T(8,128)S(1)} %shard_map.56.forward_ref.refs_0_), channel_id=1, source_target_pairs={{0,16},{4,20},{8,24},{12,28},{16,0},{20,4},{24,8},{28,12},{1,17},{... | collective-permute-start | bytes 196616 | tf_op jit(solution)/shard_map/ppermute | solution.py:62
  60.4 3.4 %collective-permute-done.18.refs_0_ = f32[4,32,128]{2,1,0:T(8,128)S(1)} collective-permute-done((f32[4,32,128]{2,1,0:T(8,128)S(1)}, f32[4,32,128]{2,1,0:T(8,128)S(1)}, u32[]{:S(2)}, u32[]{:S(2)}) %collective-permute-start.18) | collective-permute-done | bytes 65568 | tf_op jit(solution)/shard_map/ppermute | solution.py:62
  67.5 2.5 %collective-permute-done.24.value_ref = f32[2,16,32,128]{3,2,1,0:T(8,128)S(1)} collective-permute-done((f32[2,16,32,128]{3,2,1,0:T(8,128)S(1)}, f32[2,16,32,128]{3,2,1,0:T(8,128)S(1)}, u32[]{:S(2)}, u32[]{:S(2)}) %collective-permute-start.24) | collective-permute-done | bytes 524320 | tf_op jit(solution)/shard_map/ppermute | solution.py:62
  76.5 3.0 %shard_map.63 = (f32[4,32,128]{2,1,0:T(8,128)S(1)}, f32[8,32,128]{2,1,0:T(8,128)S(1)}, f32[8,32,128]{2,1,0:T(8,128)S(1)}, f32[8,32,128]{2,1,0:T(8,128)S(1)}, f32[8,32,128]{2,1,0:T(8,128)S(1)}) custom-call(s32[64]{0:T(128)S(1)} %get-tuple-element.73.slot_ref, f32[8,32,128]{2,1,0:T(8,128)S(1)} %pad_maximum_fusion.1.x0, ...), custom_call_target="tpu_custom_call" | custom-call | flops 1 | bytes 1 | tf_op jit(solution)/shard_map/pallas_call | solution.py:426
  83.1 2.1 %collective-permute-done.26 = f32[8,32,128]{2,1,0:T(8,128)S(1)} collective-permute-done((f32[8,32,128]{2,1,0:T(8,128)S(1)}, f32[8,32,128]{2,1,0:T(8,128)S(1)}, u32[]{:S(2)}, u32[]{:S(2)}) %collective-permute-start.26) | collective-permute-done | bytes 131104 | tf_op jit(solution)/shard_map/ppermute | solution.py:62
  89.3 3.3 %collective-permute-start.29 = (f32[4,32,128]{2,1,0:T(8,128)S(1)}, f32[4,32,128]{2,1,0:T(8,128)S(1)}, u32[]{:S(2)}, u32[]{:S(2)}) collective-permute-start(f32[4,32,128]{2,1,0:T(8,128)S(1)} %get-tuple-element.69), channel_id=1, source_target_pairs={{0,16},{4,20},{8,24},{12,28},{16,0},{20,4},{24,8},{28,12},{1,17},{... | collective-permute-start | bytes 196616 | tf_op jit(solution)/shard_map/ppermute | solution.py:62
  92.5 2.5 %collective-permute-done.29.ret1 = f32[4,32,128]{2,1,0:T(8,128)S(1)} collective-permute-done((f32[4,32,128]{2,1,0:T(8,128)S(1)}, f32[4,32,128]{2,1,0:T(8,128)S(1)}, u32[]{:S(2)}, u32[]{:S(2)}) %collective-permute-start.29) | collective-permute-done | bytes 65568 | tf_op jit(solution)/shard_map/ppermute | solution.py:62
  101.5 2.4 %collective-permute-done.30 = f32[8,32,128]{2,1,0:T(8,128)S(1)} collective-permute-done((f32[8,32,128]{2,1,0:T(8,128)S(1)}, f32[8,32,128]{2,1,0:T(8,128)S(1)}, u32[]{:S(2)}, u32[]{:S(2)}) %collective-permute-start.30) | collective-permute-done | bytes 131104 | tf_op jit(solution)/shard_map/ppermute | solution.py:62
  105.6 2.3 %collective-permute-done.32 = f32[8,32,128]{2,1,0:T(8,128)S(1)} collective-permute-done((f32[8,32,128]{2,1,0:T(8,128)S(1)}, f32[8,32,128]{2,1,0:T(8,128)S(1)}, u32[]{:S(2)}, u32[]{:S(2)}) %collective-permute-start.32) | collective-permute-done | bytes 131104 | tf_op jit(solution)/shard_map/ppermute | solution.py:62
  107.9 3.3 %collective-permute-start.33 = (f32[4,32,128]{2,1,0:T(8,128)S(1)}, f32[4,32,128]{2,1,0:T(8,128)S(1)}, u32[]{:S(2)}, u32[]{:S(2)}) collective-permute-start(f32[4,32,128]{2,1,0:T(8,128)S(1)} %get-tuple-element.67), channel_id=1, source_target_pairs={{0,16},{4,20},{8,24},{12,28},{16,0},{20,4},{24,8},{28,12},{1,17},{... | collective-permute-start | bytes 196616 | tf_op jit(solution)/shard_map/ppermute | solution.py:62
  111.2 2.5 %shard_map.67.refs_0_ = bf16[4,2048,256]{2,1,0:T(8,128)(2,1)S(1)} custom-call(s32[1]{0:T(128)} %bitcast.col_ref, f32[3,4,16,32,128]{4,3,2,1,0:T(8,128)S(1)} %copy-done.1, f32[3,4,16,32,128]{4,3,2,1,0:T(8,128)} %collective-permute-done.14.refs_1_, f32[4,16,32,128]{3,2,1,0:T(8,128)S(1)} %shard_map.66.refs_2_, ...), custom_call_target="tpu_custom_call" | custom-call | flops 1 | bytes 1 | tf_op jit(solution)/shard_map/pallas_call | solution.py:337
  125.3 2.9 %collective-permute-start.39 = (f32[4,32,128]{2,1,0:T(8,128)S(1)}, f32[4,32,128]{2,1,0:T(8,128)S(1)}, u32[]{:S(2)}, u32[]{:S(2)}) collective-permute-start(f32[4,32,128]{2,1,0:T(8,128)S(1)} %get-tuple-element.65), channel_id=1, source_target_pairs={{0,16},{4,20},{8,24},{12,28},{16,0},{20,4},{24,8},{28,12},{1,17},{... | collective-permute-start | bytes 196616 | tf_op jit(solution)/shard_map/ppermute | solution.py:62
  128.2 3.1 %collective-permute-done.39.ret1 = f32[4,32,128]{2,1,0:T(8,128)S(1)} collective-permute-done((f32[4,32,128]{2,1,0:T(8,128)S(1)}, f32[4,32,128]{2,1,0:T(8,128)S(1)}, u32[]{:S(2)}, u32[]{:S(2)}) %collective-permute-start.39) | collective-permute-done | bytes 65568 | tf_op jit(solution)/shard_map/ppermute | solution.py:62
  134.0 2.6 %collective-permute-done.41.refs_2_ = f32[4,32,128]{2,1,0:T(8,128)S(1)} collective-permute-done((f32[4,32,128]{2,1,0:T(8,128)S(1)}, f32[4,32,128]{2,1,0:T(8,128)S(1)}, u32[]{:S(2)}, u32[]{:S(2)}) %collective-permute-start.41) | collective-permute-done | bytes 65568 | tf_op jit(solution)/shard_map/ppermute | solution.py:62
  (119 shorter events, 71.7 us)
Async XLA Ops:
  0.0 49.6 %collective-permute-start.14 = (f32[3,4,16,32,128]{4,3,2,1,0:T(8,128)}, f32[3,4,16,32,128]{4,3,2,1,0:T(8,128)}, u32[]{:S(2)}, u32[]{:S(2)}) collective-permute-start(f32[3,4,16,32,128]{4,3,2,1,0:T(8,128)} %refs_0_.9), channel_id=1, source_target_pairs={{0,1},{1,0},{2,3},{3,2},{4,5},{5,4},{6,7},{7,6},{8,9},{9,8},{10,11... | collective-permute-start | bytes 9437192 | tf_op jit(solution)/shard_map/ppermute | solution.py:62
  0.5 9.8 %collective-permute-start.6 = (f32[16,32,128]{2,1,0:T(8,128)}, f32[16,32,128]{2,1,0:T(8,128)}, u32[]{:S(2)}, u32[]{:S(2)}) collective-permute-start(f32[16,32,128]{2,1,0:T(8,128)} %bitcast.10), channel_id=1, source_target_pairs={{0,2},{1,3},{2,0},{3,1},{4,6},{5,7},{6,4},{7,5},{8,10},{9,11},{10,... | collective-permute-start | bytes 786440 | tf_op jit(solution)/shard_map/ppermute | solution.py:62
  3.1 12.4 %collective-permute-start.5 = (f32[16,32,128]{2,1,0:T(8,128)}, f32[16,32,128]{2,1,0:T(8,128)}, u32[]{:S(2)}, u32[]{:S(2)}) collective-permute-start(f32[16,32,128]{2,1,0:T(8,128)} %bitcast.11), channel_id=1, source_target_pairs={{0,1},{1,0},{2,3},{3,2},{4,5},{5,4},{6,7},{7,6},{8,9},{9,8},{10,11... | collective-permute-start | bytes 786440 | tf_op jit(solution)/shard_map/ppermute | solution.py:62
  5.4 7.0 %collective-permute-start = (f32[4,32,128]{2,1,0:T(8,128)}, f32[4,32,128]{2,1,0:T(8,128)}, u32[]{:S(2)}, u32[]{:S(2)}) collective-permute-start(f32[4,32,128]{2,1,0:T(8,128)} %get-tuple-element.31), channel_id=1, source_target_pairs={{0,16},{4,20},{8,24},{12,28},{16,0},{20,4},{24,8},{28,12},{1,17},{... | collective-permute-start | bytes 196616 | tf_op jit(solution)/shard_map/ppermute | solution.py:62
  8.0 14.5 %collective-permute-start.4 = (f32[2,16,32,128]{3,2,1,0:T(8,128)}, f32[2,16,32,128]{3,2,1,0:T(8,128)}, u32[]{:S(2)}, u32[]{:S(2)}) collective-permute-start(f32[2,16,32,128]{3,2,1,0:T(8,128)} %get-tuple-element.32), channel_id=1, source_target_pairs={{0,2},{1,3},{2,0},{3,1},{4,6},{5,7},{6,4},{7,5},{8,10},{9,11},{10,... | collective-permute-start | bytes 1572872 | tf_op jit(solution)/shard_map/ppermute | solution.py:62
  13.3 7.3 %collective-permute-start.3 = (f32[8,32,128]{2,1,0:T(8,128)S(1)}, f32[8,32,128]{2,1,0:T(8,128)S(1)}, u32[]{:S(2)}, u32[]{:S(2)}) collective-permute-start(f32[8,32,128]{2,1,0:T(8,128)S(1)} %constant_dynamic-update-slice_fusion.x0), channel_id=1, source_target_pairs={{0,12},{4,8},{8,4},{12,0},{16,28},{20,24},{24,20},{28,16},{1,13},{... | collective-permute-start | bytes 393224 | tf_op jit(solution)/shard_map/ppermute | solution.py:62
  15.4 7.1 %collective-permute-start.2 = (f32[8,32,128]{2,1,0:T(8,128)S(1)}, f32[8,32,128]{2,1,0:T(8,128)S(1)}, u32[]{:S(2)}, u32[]{:S(2)}) collective-permute-start(f32[8,32,128]{2,1,0:T(8,128)S(1)} %constant_dynamic-update-slice_fusion.x0), channel_id=1, source_target_pairs={{0,8},{4,12},{8,0},{12,4},{16,24},{20,28},{24,16},{28,20},{1,9},{5... | collective-permute-start | bytes 393224 | tf_op jit(solution)/shard_map/ppermute | solution.py:62
  16.2 6.4 %collective-permute-start.1 = (f32[8,32,128]{2,1,0:T(8,128)S(1)}, f32[8,32,128]{2,1,0:T(8,128)S(1)}, u32[]{:S(2)}, u32[]{:S(2)}) collective-permute-start(f32[8,32,128]{2,1,0:T(8,128)S(1)} %constant_dynamic-update-slice_fusion.x0), channel_id=1, source_target_pairs={{0,4},{4,0},{8,12},{12,8},{16,20},{20,16},{24,28},{28,24},{1,5},{5... | collective-permute-start | bytes 393224 | tf_op jit(solution)/shard_map/ppermute | solution.py:62
  31.3 12.9 %collective-permute-start.16 = (f32[2,16,32,128]{3,2,1,0:T(8,128)S(1)}, f32[2,16,32,128]{3,2,1,0:T(8,128)S(1)}, u32[]{:S(2)}, u32[]{:S(2)}) collective-permute-start(f32[2,16,32,128]{3,2,1,0:T(8,128)S(1)} %shard_map.53), channel_id=1, source_target_pairs={{0,2},{1,3},{2,0},{3,1},{4,6},{5,7},{6,4},{7,5},{8,10},{9,11},{10,... | collective-permute-start | bytes 1572872 | tf_op jit(solution)/shard_map/ppermute | solution.py:62
  36.3 10.3 %collective-permute-start.15 = (f32[2,16,32,128]{3,2,1,0:T(8,128)}, f32[2,16,32,128]{3,2,1,0:T(8,128)S(1)}, u32[]{:S(2)}, u32[]{:S(2)}) collective-permute-start(f32[2,16,32,128]{3,2,1,0:T(8,128)} %collective-permute-done.4.early_ref.refs_2_), channel_id=1, source_target_pairs={{0,1},{1,0},{2,3},{3,2},{4,5},{5,4},{6,7},{7,6},{8,9},{9,8},{10,11... | collective-permute-start | bytes 1572872 | tf_op jit(solution)/shard_map/ppermute | solution.py:62
  44.4 23.0 %collective-permute-start.22 = (f32[2,16,32,128]{3,2,1,0:T(8,128)S(1)}, f32[2,16,32,128]{3,2,1,0:T(8,128)S(1)}, u32[]{:S(2)}, u32[]{:S(2)}) collective-permute-start(f32[2,16,32,128]{3,2,1,0:T(8,128)S(1)} %shard_map.57), channel_id=1, source_target_pairs={{0,2},{1,3},{2,0},{3,1},{4,6},{5,7},{6,4},{7,5},{8,10},{9,11},{10,... | collective-permute-start | bytes 1572872 | tf_op jit(solution)/shard_map/ppermute | solution.py:62
  46.2 23.8 %collective-permute-start.24 = (f32[2,16,32,128]{3,2,1,0:T(8,128)S(1)}, f32[2,16,32,128]{3,2,1,0:T(8,128)S(1)}, u32[]{:S(2)}, u32[]{:S(2)}) collective-permute-start(f32[2,16,32,128]{3,2,1,0:T(8,128)S(1)} %shard_map.60), channel_id=1, source_target_pairs={{0,2},{1,3},{2,0},{3,1},{4,6},{5,7},{6,4},{7,5},{8,10},{9,11},{10,... | collective-permute-start | bytes 1572872 | tf_op jit(solution)/shard_map/ppermute | solution.py:62
  46.6 7.3 %collective-permute-start.13 = (f32[8,32,128]{2,1,0:T(8,128)S(1)}, f32[8,32,128]{2,1,0:T(8,128)S(1)}, u32[]{:S(2)}, u32[]{:S(2)}) collective-permute-start(f32[8,32,128]{2,1,0:T(8,128)S(1)} %pad_maximum_fusion.x0), channel_id=1, source_target_pairs={{0,12},{4,8},{8,4},{12,0},{16,28},{20,24},{24,20},{28,16},{1,13},{... | collective-permute-start | bytes 393224 | tf_op jit(solution)/shard_map/ppermute | solution.py:62
  49.1 6.6 %collective-permute-start.12 = (f32[8,32,128]{2,1,0:T(8,128)S(1)}, f32[8,32,128]{2,1,0:T(8,128)S(1)}, u32[]{:S(2)}, u32[]{:S(2)}) collective-permute-start(f32[8,32,128]{2,1,0:T(8,128)S(1)} %pad_maximum_fusion.x0), channel_id=1, source_target_pairs={{0,8},{4,12},{8,0},{12,4},{16,24},{20,28},{24,16},{28,20},{1,9},{5... | collective-permute-start | bytes 393224 | tf_op jit(solution)/shard_map/ppermute | solution.py:62
  57.3 6.5 %collective-permute-start.18 = (f32[4,32,128]{2,1,0:T(8,128)S(1)}, f32[4,32,128]{2,1,0:T(8,128)S(1)}, u32[]{:S(2)}, u32[]{:S(2)}) collective-permute-start(f32[4,32,128]{2,1,0:T(8,128)S(1)} %shard_map.56.forward_ref.refs_0_), channel_id=1, source_target_pairs={{0,16},{4,20},{8,24},{12,28},{16,0},{20,4},{24,8},{28,12},{1,17},{... | collective-permute-start | bytes 196616 | tf_op jit(solution)/shard_map/ppermute | solution.py:62
  63.8 6.5 %collective-permute-start.21 = (f32[8,32,128]{2,1,0:T(8,128)S(1)}, f32[8,32,128]{2,1,0:T(8,128)S(1)}, u32[]{:S(2)}, u32[]{:S(2)}) collective-permute-start(f32[8,32,128]{2,1,0:T(8,128)S(1)} %pad_maximum_fusion.1.x0), channel_id=1, source_target_pairs={{0,12},{4,8},{8,4},{12,0},{16,28},{20,24},{24,20},{28,16},{1,13},{... | collective-permute-start | bytes 393224 | tf_op jit(solution)/shard_map/ppermute | solution.py:62
  67.4 6.4 %collective-permute-start.23 = (f32[2,16,32,128]{3,2,1,0:T(8,128)S(1)}, f32[2,16,32,128]{3,2,1,0:T(8,128)S(1)}, u32[]{:S(2)}, u32[]{:S(2)}) collective-permute-start(f32[2,16,32,128]{3,2,1,0:T(8,128)S(1)} %shard_map.58.refs_2_), channel_id=1, source_target_pairs={{0,1},{1,0},{2,3},{3,2},{4,5},{5,4},{6,7},{7,6},{8,9},{9,8},{10,11... | collective-permute-start | bytes 1572872 | tf_op jit(solution)/shard_map/ppermute | solution.py:62
  72.2 25.6 %collective-permute-start.34 = (f32[4,16,32,128]{3,2,1,0:T(8,128)S(1)}, f32[4,16,32,128]{3,2,1,0:T(8,128)S(1)}, u32[]{:S(2)}, u32[]{:S(2)}) collective-permute-start(f32[4,16,32,128]{3,2,1,0:T(8,128)S(1)} %shard_map.65), channel_id=1, source_target_pairs={{0,2},{1,3},{2,0},{3,1},{4,6},{5,7},{6,4},{7,5},{8,10},{9,11},{10,... | collective-permute-start | bytes 3145736 | tf_op jit(solution)/shard_map/ppermute | solution.py:62
  80.8 6.4 %collective-permute-start.27 = (f32[8,32,128]{2,1,0:T(8,128)S(1)}, f32[8,32,128]{2,1,0:T(8,128)S(1)}, u32[]{:S(2)}, u32[]{:S(2)}) collective-permute-start(f32[8,32,128]{2,1,0:T(8,128)S(1)} %get-tuple-element.40), channel_id=1, source_target_pairs={{0,8},{4,12},{8,0},{12,4},{16,24},{20,28},{24,16},{28,20},{1,9},{5... | collective-permute-start | bytes 393224 | tf_op jit(solution)/shard_map/ppermute | solution.py:62
  82.5 6.7 %collective-permute-start.28 = (f32[8,32,128]{2,1,0:T(8,128)S(1)}, f32[8,32,128]{2,1,0:T(8,128)S(1)}, u32[]{:S(2)}, u32[]{:S(2)}) collective-permute-start(f32[8,32,128]{2,1,0:T(8,128)S(1)} %get-tuple-element.41), channel_id=1, source_target_pairs={{0,12},{4,8},{8,4},{12,0},{16,28},{20,24},{24,20},{28,16},{1,13},{... | collective-permute-start | bytes 393224 | tf_op jit(solution)/shard_map/ppermute | solution.py:62
  97.9 13.3 %collective-permute-start.35 = (f32[4,16,32,128]{3,2,1,0:T(8,128)S(1)}, f32[4,16,32,128]{3,2,1,0:T(8,128)S(1)}, u32[]{:S(2)}, u32[]{:S(2)}) collective-permute-start(f32[4,16,32,128]{3,2,1,0:T(8,128)S(1)} %shard_map.66.refs_2_), channel_id=1, source_target_pairs={{0,1},{1,0},{2,3},{3,2},{4,5},{5,4},{6,7},{7,6},{8,9},{9,8},{10,11... | collective-permute-start | bytes 3145736 | tf_op jit(solution)/shard_map/ppermute | solution.py:62
  99.2 6.3 %collective-permute-start.31 = (f32[8,32,128]{2,1,0:T(8,128)S(1)}, f32[8,32,128]{2,1,0:T(8,128)S(1)}, u32[]{:S(2)}, u32[]{:S(2)}) collective-permute-start(f32[8,32,128]{2,1,0:T(8,128)S(1)} %get-tuple-element.44), channel_id=1, source_target_pairs={{0,8},{4,12},{8,0},{12,4},{16,24},{20,28},{24,16},{28,20},{1,9},{5... | collective-permute-start | bytes 393224 | tf_op jit(solution)/shard_map/ppermute | solution.py:62
  100.9 6.9 %collective-permute-start.32 = (f32[8,32,128]{2,1,0:T(8,128)S(1)}, f32[8,32,128]{2,1,0:T(8,128)S(1)}, u32[]{:S(2)}, u32[]{:S(2)}) collective-permute-start(f32[8,32,128]{2,1,0:T(8,128)S(1)} %get-tuple-element.45), channel_id=1, source_target_pairs={{0,12},{4,8},{8,4},{12,0},{16,28},{20,24},{24,20},{28,16},{1,13},{... | collective-permute-start | bytes 393224 | tf_op jit(solution)/shard_map/ppermute | solution.py:62
  119.0 6.2 %collective-permute-start.38 = (f32[8,32,128]{2,1,0:T(8,128)S(1)}, f32[8,32,128]{2,1,0:T(8,128)S(1)}, u32[]{:S(2)}, u32[]{:S(2)}) collective-permute-start(f32[8,32,128]{2,1,0:T(8,128)S(1)} %get-tuple-element.50), channel_id=1, source_target_pairs={{0,12},{4,8},{8,4},{12,0},{16,28},{20,24},{24,20},{28,16},{1,13},{... | collective-permute-start | bytes 393224 | tf_op jit(solution)/shard_map/ppermute | solution.py:62
  (26 other events, 138.6 us)

commit v3 on v2

--- a/solution.py
+++ b/solution.py
@@ -78,7 +78,7 @@
 
 
 def gather_row(own):
-    held = own
+    held, got = own, own
     for mask in far_masks(lax.axis_size("row")):
         got = swap(held, "row", mask)
         held = jnp.concatenate([held, got], axis=0)
@@ -95,14 +95,14 @@
             total = total + other
         keep, send = jnp.split(total, 2, axis=0)
         total, other = keep, swap(send, "row", mask)
-    return total, other
+    return got, (total, other)
 
 
 def first_kernel(level, inverse_ref, sides_ref, lower_ref, out_ref, early_ref, inverse, sides, sems):
     copies = [
         pltpu.make_async_copy(inverse_ref.at[0], inverse, sems.at[0]),
         pltpu.make_async_copy(sides_ref.at[0], sides, sems.at[1]),
-        pltpu.make_async_copy(lower_ref.at[level, pl.ds(0, early_ref.shape[0])], early_ref, sems.at[2]),
+        pltpu.make_async_copy(lower_ref.at[level - 1, pl.ds(0, early_ref.shape[0])], early_ref, sems.at[2]),
     ]
     for copy in copies:
         copy.start()
@@ -144,9 +144,9 @@
             out_ref[i, pl.ds(offset, share), width:] = low
 
 
-def stand_kernel(lower_ref, out_ref, own, sem):
+def stand_kernel(level, lower_ref, after_ref, out_ref, own, sem):
     count, fan_in, share, width = own.shape
-    copy = pltpu.make_async_copy(lower_ref.at[0], own, sem)
+    copy = pltpu.make_async_copy(lower_ref.at[level], own, sem)
     copy.start()
     copy.wait()
     for j in range(count):
@@ -155,8 +155,26 @@
         out_ref[j, width:] = low
 
 
-def partial_kernel(col_ref, slot_ref, x0, x1, x2, x3, lower_ref, early_ref, token_ref, *refs):
-    outs, (blocks, picked, turned) = refs[:-3], refs[-3:]
+def fold_kernel(lower_ref, own_inverse_ref, sides_ref, inverse_ref, out_ref, base_ref, own, own_inverse, sides, sems):
+    count, fan_in, share, width = own.shape
+    copies = [
+        pltpu.make_async_copy(lower_ref.at[0], own, sems.at[0]),
+        pltpu.make_async_copy(own_inverse_ref.at[1], own_inverse, sems.at[1]),
+        pltpu.make_async_copy(sides_ref.at[1], sides, sems.at[2]),
+    ]
+    for copy in copies:
+        copy.start()
+    for copy in copies:
+        copy.wait()
+    for j in range(count):
+        high, low = split(times_turned(own[j].reshape(fan_in * share, width), inverse_ref[j]).T)
+        out_ref[j, :width] = high
+        out_ref[j, width:] = low
+        base_ref[j] = nn(own_inverse[j], sides[j])
+
+
+def partial_kernel(turn, col_ref, slot_ref, x0, x1, x2, x3, lower_ref, *refs):
+    outs, (blocks, picked, sums) = refs[-6:-3], refs[-3:]
     count = lower_ref.shape[0]
     fan_in = slot_ref.shape[0] // count
     each, share, columns = x0.shape
@@ -172,23 +190,35 @@
     for j in range(count):
         both = half(lower_ref[j], picked[j], (1, 0))
         both = both[:width] + both[width:]
-        turned[j] = (both[:, :columns] + both[:, columns:]).T
-    columns = outs[0].shape[1]
+        both = both[:, :columns] + both[:, columns:]
+        sums[j] = both.T if turn else both
+    each, piece, _ = outs[0].shape
+    if turn:
+        sums[count] = refs[0][...].reshape(count * share, columns).T
     for place, mask in enumerate((0, 2, 1, 3)):
-        start = pl.multiple_of((col_ref[0] ^ mask) * columns, columns)
-        out = outs[place] if place < 2 else outs[2].at[pl.ds((place - 2) * count, count)]
+        start = pl.multiple_of((col_ref[0] ^ mask) * piece, piece)
+        out = outs[place] if place < 2 else outs[2].at[pl.ds((place - 2) * each, each)]
+        for j in range(each):
+            out[j] = sums[j, pl.ds(start, piece), :]
+
+
+def solve_kernel(col_ref, u0, u1, u2, sides_ref, inverse_ref, out_ref, lower_ref, parts):
+    count = out_ref.shape[0]
+    share = u0.shape[2] // count
+    for j in range(count):
+        out_ref[j] = times_turned(sides_ref[j] - ((u0[j] + u1[j]) + u2[j]), inverse_ref[j])
+    parts[0], parts[1], parts[2], parts[3] = u0[count], u1[count], u2[count], u2[count + 1]
+    for c in range(parts.shape[0]):
+        part = parts[col_ref[0] ^ c]
         for j in range(count):
-            out[j] = turned[j, pl.ds(start, columns), :]
-
-
-def solve_first_kernel(u0, u1, u2, sides_ref, inverse_ref, out_ref):
-    for j in range(out_ref.shape[0]):
-        out_ref[j] = times_turned(sides_ref[j] - ((u0[j] + u1[j]) + u2[j]), inverse_ref[j])
+            lower_ref[j, :, c * share:(c + 1) * share] = part[:, j * share:(j + 1) * share]
 
 
 def block_of(lower, j):
-    some = lower[0].shape[0]
-    return lower[j // some][j % some]
+    for some in lower:
+        if j < some.shape[0]:
+            return some[j]
+        j -= some.shape[0]
 
 
 def forward_levels(slot_ref, xs, sides_ref, inverse_ref, lower, out_ref, blocks, picked):
@@ -226,11 +256,6 @@
         out[...] = total[q * each:(q + 1) * each]
 
 
-def forward_kernel(chunks, slot_ref, x0, x1, x2, x3, sides_ref, inverse_ref, *refs):
-    lower, (out_ref, blocks, picked) = refs[:chunks], refs[chunks:]
-    forward_levels(slot_ref, (x0, x1, x2, x3), sides_ref, inverse_ref, lower, out_ref, blocks, picked)
-
-
 def top_kernel(chunks, slot_ref, x0, x1, x2, x3, sides_ref, inverse_ref, *refs):
     lower, outs = refs[:chunks], refs[chunks + 1:chunks + 5]
     sol_ref, (blocks, picked, solved, total) = refs[chunks], refs[chunks + 5:]
@@ -241,37 +266,46 @@
 
 
 def backward_kernel(chunks, slot_ref, ret0, ret1, forward_ref, inverse_ref, *refs):
-    lower, outs = refs[:chunks], refs[chunks + 1:chunks + 5]
-    sol_ref, total = refs[chunks], refs[chunks + 5]
+    lower, (sol_ref, *outs, total) = refs[:chunks], refs[-6:]
     for j in range(sol_ref.shape[0]):
         sol_ref[j] = times(forward_ref[j] - (ret0[j] + ret1[j]), inverse_ref[j])
     backward_terms(slot_ref, sol_ref, lower, outs, total)
 
 
-def last_kernel(col_ref, ret0, ret1, sides_ref, inverse_ref, s1, s2, s3, *refs):
-    outs, (solved, packed) = refs[:-2], refs[-2:]
-    count = sides_ref.shape[0]
-    share = sides_ref.shape[2] // len(outs)
-    for j in range(count):
-        rest = times_turned(sides_ref[j], inverse_ref[j]) - (ret0[j] + ret1[j])
-        solved[j] = times(rest, inverse_ref[j])
-    for level, source in enumerate((solved, s1, s2, s3)):
+def cut(col_ref, sources, outs, packed):
+    share = sources[0].shape[2] // len(outs)
+    for level, source in enumerate(sources):
         for c in range(len(outs)):
             packed[c, level] = jnp.concatenate(
-                [source[j, :, c * share:(c + 1) * share] for j in range(count)], axis=1
+                [source[j, :, c * share:(c + 1) * share] for j in range(source.shape[0])], axis=1
             )
     for mask, out in enumerate(outs):
         out[...] = packed[col_ref[0] ^ mask]
 
 
+def cut_kernel(some, col_ref, *refs):
+    cut(col_ref, refs[:some], refs[-5:-1], refs[-1])
+
+
+def last_kernel(col_ref, ret0, ret1, sides_ref, inverse_ref, *refs):
+    outs, (solved, packed) = refs[:-2], refs[-2:]
+    for j in range(sides_ref.shape[0]):
+        rest = times_turned(sides_ref[j], inverse_ref[j]) - (ret0[j] + ret1[j])
+        solved[j] = times(rest, inverse_ref[j])
+    cut(col_ref, [solved], outs, packed)
+
+
 def out_kernel(col_ref, *refs):
     parts, (out_ref, whole) = refs[:-2], refs[-2:]
     levels, count, share, columns = out_ref.shape
-    piece = parts[0].shape[1]
-    for mask, part in enumerate(parts):
-        start = pl.multiple_of((col_ref[0] ^ mask) * piece, piece)
-        for level in range(levels):
-            whole[level, pl.ds(start, piece), :] = part[level]
+    place = 0
+    for group in (parts[:4], parts[4:]):
+        some, piece, _ = group[0].shape
+        for mask, part in enumerate(group):
+            start = pl.multiple_of((col_ref[0] ^ mask) * piece, piece)
+            for level in range(some):
+                whole[place + level, pl.ds(start, piece), :] = part[level]
+        place += some
     for level in range(levels):
         out_ref[level] = whole[level].T.reshape(count, share, columns)
 
@@ -291,20 +325,28 @@
     )(value, *others)
 
 
-def pack_kernel(level, start, lower_ref, *refs):
-    out_ref, sem = refs[-2:]
-    copy = pltpu.make_async_copy(lower_ref.at[level, pl.ds(start, out_ref.shape[0])], out_ref, sem)
-    copy.start()
-    copy.wait()
-
-
-def pack(lower_blocks, level, start, size, *others):
+def pack_kernel(pieces, lower_ref, *refs):
+    out_ref, sems = refs[-2:]
+    copies, place = [], 0
+    for i, (level, start, size) in enumerate(pieces):
+        copies.append(
+            pltpu.make_async_copy(lower_ref.at[level, pl.ds(start, size)], out_ref.at[pl.ds(place, size)], sems.at[i])
+        )
+        place += size
+    for copy in copies:
+        copy.start()
+    for copy in copies:
+        copy.wait()
+
+
+def pack(lower_blocks, pieces, *others):
+    total = sum(size for _, _, size in pieces)
     return pl.pallas_call(
-        functools.partial(pack_kernel, level, start),
-        out_shape=jax.ShapeDtypeStruct((size,) + lower_blocks.shape[2:], F32),
+        functools.partial(pack_kernel, pieces),
+        out_shape=jax.ShapeDtypeStruct((total,) + lower_blocks.shape[2:], F32),
         in_specs=[HBM] + [VMEM] * len(others),
         out_specs=VMEM,
-        scratch_shapes=[pltpu.SemaphoreType.DMA],
+        scratch_shapes=[pltpu.SemaphoreType.DMA((len(pieces),))],
         compiler_params=pltpu.CompilerParams(vmem_limit_bytes=8 * 1024 * 1024),
         cost_estimate=TINY,
     )(lower_blocks, *others)
@@ -329,10 +371,9 @@
     block = like(count, mine, width)
     quarter = like(rows // 4 * count, mine, width)
 
-    def join(level, start, across):
-        some = across.shape[0]
+    def join(level, start, some, parts, place=0):
         own_spec = pl.BlockSpec((None, 1, fan_in, share, width), lambda j: (level, start + j, 0, 0, 0))
-        part_spec = pl.BlockSpec((1, fan_in, share, width), lambda j: (j, 0, 0, 0))
+        part_spec = pl.BlockSpec((1, fan_in, share, width), lambda j: (place + j, 0, 0, 0))
         out_spec = pl.BlockSpec((1, fan_in * width, 2 * width), lambda j: (j, 0, 0))
         return pl.pallas_call(
             join_kernel,
@@ -342,7 +383,7 @@
             out_specs=out_spec,
             compiler_params=pltpu.CompilerParams(vmem_limit_bytes=24 * 1024 * 1024),
             cost_estimate=TINY,
-        )(col, lower_blocks, lower_beside, *near(across))
+        )(col, lower_blocks, lower_beside, *parts)
 
     def near(value):
         return value, swap(value, "col", 1)
@@ -350,7 +391,7 @@
     top = levels - 1
     middle = count // 2
     first, early = call(
-        functools.partial(first_kernel, 1), [like(count, share, columns), like(middle, fan_in, share, width)], [HBM] * 3,
+        functools.partial(first_kernel, top), [like(count, share, columns), like(middle, fan_in, share, width)], [HBM] * 3,
         scratch=[
             pltpu.VMEM((count, share, width), F32),
             pltpu.VMEM((count, width, columns), F32),
@@ -375,22 +416,48 @@
     )(col, right_sides.reshape(levels * count, width, columns))
     sides = [sides[i * count:(i + 1) * count] for i in range(levels)]
 
+    folded, base = call(
+        fold_kernel, [like(count, 2 * width, fan_in * share, dtype=BF16), like(count, share, columns)], [HBM] * 3 + [VMEM],
+        scratch=[
+            pltpu.VMEM(lower_blocks.shape[1:], F32),
+            pltpu.VMEM((count, share, width), F32),
+            pltpu.VMEM((count, width, columns), F32),
+            pltpu.SemaphoreType.DMA((3,)),
+        ],
+    )(lower_blocks, inverse_diag, right_sides, inverse[1])
+
+    def partial(turn, level, gathered, standing, hold, *others):
+        each = count + turn
+        kept, passed, sent = call(
+            functools.partial(partial_kernel, turn), [like(each, share, columns)] * 2 + [like(2 * each, share, columns)],
+            [SMEM] * 2 + [VMEM] * (5 + len(others)),
+            scratch=[
+                pltpu.VMEM((rows * count, share, 2 * columns), BF16),
+                pltpu.VMEM((count, fan_in * share, 2 * columns), BF16),
+                pltpu.VMEM((each, width, columns), F32),
+            ],
+        )(col, slots[level], *gathered, standing, *others)
+        beside = swap(sent, "col", 1)
+        terms = passed[:count] + beside[each:each + count]
+        if turn:
+            terms = jnp.concatenate([terms, passed[count:], beside[each + count:]], axis=0)
+        return kept, beside[:each], swap(after(terms, hold), "col", 2)
+
+    kept, beside, across = partial(False, 0, gathered, folded, early)
+    forward_rows = base - ((kept + beside) + across)
+    late = swap(pack(lower_blocks, [(top - 1, middle, count - middle), (1, 0, 1)], across), "col", 2)
+    got, gathered = gather_row(forward_rows)
+
+    forward = [None] * levels
     standing = call(
-        stand_kernel, like(count, 2 * width, fan_in * share, dtype=BF16), [HBM],
+        functools.partial(stand_kernel, 1), like(count, 2 * width, fan_in * share, dtype=BF16), [HBM, VMEM],
         scratch=[pltpu.VMEM(lower_blocks.shape[1:], F32), pltpu.SemaphoreType.DMA],
-    )(lower_blocks)
-    kept, passed, sent = call(
-        partial_kernel, [block] * 2 + [like(2 * count, mine, width)], [SMEM] * 2 + [VMEM] * 7,
-        scratch=[
-            pltpu.VMEM((rows * count, share, 2 * columns), BF16),
-            pltpu.VMEM((count, fan_in * share, 2 * columns), BF16),
-            pltpu.VMEM((count, columns, width), F32),
-        ],
-    )(col, slots[0], *gathered, standing, early, token)
-    beside = swap(sent, "col", 1)
-    across = swap(passed + beside[count:], "col", 2)
-
-    late = swap(pack(lower_blocks, 1, middle, count - middle, across), "col", 2)
+    )(lower_blocks, got)
+    updates = partial(True, 1, gathered, standing, late, forward_rows)
+    forward[2], forward[1] = call(
+        solve_kernel, [block] * 2, [SMEM] + [VMEM] * 5, scratch=[pltpu.VMEM((cols, mine, width), F32)]
+    )(col, *updates, sides[2], inverse[2])
+    inner = swap(pack(lower_blocks, [(1, 1, count - 1), (0, 0, middle)], updates[2]), "col", 2)
 
     picking = [
         pltpu.VMEM((rows * count, 2 * mine, width), BF16),
@@ -398,62 +465,51 @@
     ]
     total = [pltpu.VMEM((rows * count, mine, width), F32)]
 
-    forward, lower = [None] * levels, [None] * (levels - 1)
-    forward[1] = call(solve_first_kernel, block, [VMEM] * 5)(
-        kept, beside[:count], across, sides[1], inverse[1]
-    )
-
-    got, gathered = gather_row(forward[1])
-    whole_early = swap(pack(lower_blocks, 2, 0, middle, forward[1]), "col", 2)
-    whole_late = swap(pack(lower_blocks, 2, middle, count - middle, got), "col", 2)
-    lower[1] = [
-        join(1, 0, early),
-        join(1, middle, after(late, got)),
-    ]
-    forward[2] = call(
-        functools.partial(forward_kernel, len(lower[1])), block, [SMEM] + [VMEM] * 6 + [VMEM] * len(lower[1]),
-        scratch=picking,
-    )(slots[1], *gathered, sides[2], inverse[2], *lower[1])
-
-    last = swap(pack(lower_blocks, 0, 0, count, forward[2]), "col", 2)
+    lower = [None] * (levels - 1)
     got, gathered = gather_row(forward[2])
-    lower[2] = [
-        join(2, 0, after(whole_early, got)),
-        join(2, middle, after(whole_late, *gathered[1:])),
-    ]
-
+    early, late = near(early), near(late)
+    lower[2] = [join(top - 1, 0, middle, early), join(top - 1, middle, count - middle, late)]
     solved = [None] * levels
     solved[top], *terms = call(
         functools.partial(top_kernel, len(lower[2])), [block] + [quarter] * 4,
         [SMEM] + [VMEM] * 6 + [VMEM] * len(lower[2]),
         scratch=picking + [pltpu.VMEM((count, mine, width), F32)] + total,
     )(slots[2], *gathered, sides[top], inverse[top], *lower[2])
-
-    returned = scatter_row(terms)
+    outer = swap(pack(lower_blocks, [(0, middle, count - middle)], solved[top]), "col", 2)
+
+    got, returned = scatter_row(terms)
+    inner = near(after(inner, *got))
+    lower[1] = [join(1, 0, 1, late, count - middle), join(1, 1, count - 1, inner)]
     solved[2], *terms = call(
-        functools.partial(backward_kernel, len(lower[1])), [block] + [quarter] * 4,
-        [SMEM] + [VMEM] * 4 + [VMEM] * len(lower[1]), scratch=total,
+        functools.partial(backward_kernel, 2), [block] + [quarter] * 4, [SMEM] + [VMEM] * 6, scratch=total,
     )(slots[1], *returned, forward[2], inverse[2], *lower[1])
 
-    returned = scatter_row(terms)
-    lower[0] = [join(0, 0, after(last, solved[2]))]
+    got, returned = scatter_row(terms)
+    lower[0] = [join(0, 0, middle, inner, count - 1), join(0, middle, count - middle, near(after(outer, *got)))]
     solved[1], *terms = call(
-        functools.partial(backward_kernel, len(lower[0])), [block] + [quarter] * 4,
-        [SMEM] + [VMEM] * 4 + [VMEM] * len(lower[0]), scratch=total,
+        functools.partial(backward_kernel, 2), [block] + [quarter] * 4, [SMEM] + [VMEM] * 6, scratch=total,
     )(slots[0], *returned, forward[1], inverse[1], *lower[0])
 
-    pieces = call(
-        last_kernel, [like(levels, mine, count * share)] * cols, [SMEM] + [VMEM] * (4 + top),
+    def spread(parts):
+        return [parts[0]] + [swap(parts[mask], "col", mask) for mask in range(1, cols)]
+
+    got, returned = scatter_row(terms)
+    upper = call(
+        functools.partial(cut_kernel, top), [like(top, mine, count * share)] * cols,
+        [SMEM] + [VMEM] * (top + len(got)),
+        scratch=[pltpu.VMEM((cols, top, mine, count * share), F32)],
+    )(col, *solved[1:], *got)
+    lowest = call(
+        last_kernel, [like(1, mine, count * share)] * cols, [SMEM] + [VMEM] * 4,
         scratch=[
             pltpu.VMEM((count, mine, width), F32),
-            pltpu.VMEM((cols, levels, mine, count * share), F32),
+            pltpu.VMEM((cols, 1, mine, count * share), F32),
         ],
-    )(col, *scatter_row(terms), sides[0], inverse[0], *solved[1:])
-    pieces = [pieces[0]] + [swap(pieces[mask], "col", mask) for mask in range(1, cols)]
+    )(col, *returned, sides[0], inverse[0])
     return call(
-        out_kernel, like(levels, count, share, columns), [SMEM] + [VMEM] * cols,
+        out_kernel, like(levels, count, share, columns), [SMEM] + [VMEM] * (2 * cols),
         scratch=[pltpu.VMEM((levels, columns, count * share), F32)],
-    )(col, *pieces)
+    )(col, *spread(lowest), *spread(upper))
 
 
 def solution(mesh):

time: 139 us -> 134 us (0.964)
  waiting for transfers between devices: 57 us -> 50.8 us
  Pallas kernels: 24.9 us -> 27.7 us
    ppermute x43 -> x46, waiting for transfers between devices: 57 us -> 50.8 us  [swap(): return lax.ppermute(value, axis, [(i, i ^ mask) for i in range(size)])]
    pallas_call x5 -> x6, Pallas kernels: 7.92 us -> 8.84 us  [join(): pl.pallas_call(join_kernel, grid=(some,), out_shape=like(some, fan_in * w...]
    ppermute x43 -> x46, starting transfers between devices: 52.8 us -> 51.9 us  [swap(): return lax.ppermute(value, axis, [(i, i ^ mask) for i in range(size)])]
    pallas_call x13 -> x14, Pallas kernels: 12.1 us -> 12.5 us  [the longest x2 4.12 us: on_device(): call(functools.partial(backward_kernel, 2), [block] + [quarter] * 4, [SME...]
  transfers between devices with their start and end apart: 43 -> 46, of which waited for: 30 -> 31; matrix products, arithmetic and copies ran while one was open for 1% -> 1% of each run, Pallas kernels for 15% -> 18%
where the time goes in v3:
time: 134 us
  starting transfers between devices  51.9 us (39%)
  waiting for transfers between devices  50.8 us (38%)
  Pallas kernels  27.7 us (21%)
  local copies, waits for them, and re-layouts  2.51 us (2%)
    ppermute x46, starting transfers between devices, swap(): return lax.ppermute(value, axis, [(i, i ^ mask) for i in range(size)])  51.9 us
    ppermute x46, waiting for transfers between devices, swap(): return lax.ppermute(value, axis, [(i, i ^ mask) for i in range(size)])  50.8 us
    pallas_call x6, Pallas kernels, join(): pl.pallas_call(join_kernel, grid=(some,), out_shape=like(some, fan_in * w...  8.84 us
    pallas_call x2, Pallas kernels, on_device(): call(functools.partial(backward_kernel, 2), [block] + [quarter] * 4, [SME...  4.12 us
    pallas_call x1, Pallas kernels, on_device(): call(functools.partial(top_kernel, len(lower[2])), [block] + [quarter] *...  3.05 us
  transfers between devices with their start and end apart: 46, of which 31 were waited for; matrix products, arithmetic and copies ran while one was open for 1% of the time, Pallas kernels for 18%

profile of v3, /device:TPU:0, one launch (start us, length us, event | category | flops | bytes accessed | tf_op | source)
XLA Modules:
  0.0 133.6 jit_solution(4566923294163321812)
XLA Ops:
  0.5 2.6 %collective-permute-start.1 = (f32[16,32,128]{2,1,0:T(8,128)}, f32[16,32,128]{2,1,0:T(8,128)}, u32[]{:S(2)}, u32[]{:S(2)}) collective-permute-start(f32[16,32,128]{2,1,0:T(8,128)} %bitcast.11), channel_id=1, source_target_pairs={{0,2},{1,3},{2,0},{3,1},{4,6},{5,7},{6,4},{7,5},{8,10},{9,11},{10,... | collective-permute-start | bytes 786440 | tf_op jit(solution)/shard_map/ppermute | solution.py:62
  3.2 2.2 %shard_map.48 = (f32[4,32,128]{2,1,0:T(8,128)}, f32[2,16,32,128]{3,2,1,0:T(8,128)}) custom-call(f32[4,4,32,128]{3,2,1,0:T(8,128)} %inverse_ref.1, f32[4,4,128,128]{3,2,1,0:T(8,128)} %sides_ref.3, f32[3,4,16,32,128]{4,3,2,1,0:T(8,128)} %refs_0_.11), custom_call_target="tpu_custom_call" | custom-call | flops 1 | bytes 1 | tf_op jit(solution)/shard_map/pallas_call | solution.py:393
  5.4 2.7 %collective-permute-start.3 = (f32[4,32,128]{2,1,0:T(8,128)}, f32[4,32,128]{2,1,0:T(8,128)S(1)}, u32[]{:S(2)}, u32[]{:S(2)}) collective-permute-start(f32[4,32,128]{2,1,0:T(8,128)} %get-tuple-element.43), channel_id=1, source_target_pairs={{0,16},{4,20},{8,24},{12,28},{16,0},{20,4},{24,8},{28,12},{1,17},{... | collective-permute-start | bytes 196616 | tf_op jit(solution)/shard_map/ppermute | solution.py:62
  15.8 1.8 %shard_map.46 = (bf16[16,128,256]{2,1,0:T(8,128)(2,1)S(1)}, f32[8,128]{1,0:T(8,128)}) custom-call(s32[1]{0:T(128)} %bitcast.col_ref, f32[16,32,128]{2,1,0:T(8,128)S(1)} %bitcast.12, f32[16,32,128]{2,1,0:T(8,128)} %collective-permute-done.refs_1_, f32[16,32,128]{2,1,0:T(8,128)} %collective-permute-done.1.refs_2_, f32[16,32,128]{2,1,0:T(8,128)} %collective-permute-done.2.refs_3_), custom_call_target="tpu_custom_call" | custom-call | flops 1 | bytes 1 | tf_op jit(solution)/shard_map/pallas_call | solution.py:408
  25.1 1.7 %collective-permute-start.9 = (f32[4,32,128]{2,1,0:T(8,128)S(1)}, f32[4,32,128]{2,1,0:T(8,128)S(1)}, u32[]{:S(2)}, u32[]{:S(2)}) collective-permute-start(f32[4,32,128]{2,1,0:T(8,128)S(1)} %shard_map.50), channel_id=1, source_target_pairs={{0,2},{1,3},{2,0},{3,1},{4,6},{5,7},{6,4},{7,5},{8,10},{9,11},{10,... | collective-permute-start | bytes 196616 | tf_op jit(solution)/shard_map/ppermute | solution.py:62
  26.9 2.5 %collective-permute-done.9.refs_0_ = f32[4,32,128]{2,1,0:T(8,128)S(1)} collective-permute-done((f32[4,32,128]{2,1,0:T(8,128)S(1)}, f32[4,32,128]{2,1,0:T(8,128)S(1)}, u32[]{:S(2)}, u32[]{:S(2)}) %collective-permute-start.9) | collective-permute-done | bytes 65568 | tf_op jit(solution)/shard_map/ppermute | solution.py:62
  29.4 2.9 %collective-permute-start.10 = (f32[4,32,128]{2,1,0:T(8,128)S(1)}, f32[4,32,128]{2,1,0:T(8,128)S(1)}, u32[]{:S(2)}, u32[]{:S(2)}) collective-permute-start(f32[4,32,128]{2,1,0:T(8,128)S(1)} %fusion.1.refs_0_), channel_id=1, source_target_pairs={{0,16},{4,20},{8,24},{12,28},{16,0},{20,4},{24,8},{28,12},{1,17},{... | collective-permute-start | bytes 196616 | tf_op jit(solution)/shard_map/ppermute | solution.py:62
  38.9 2.5 %collective-permute-done.11.x1 = f32[8,32,128]{2,1,0:T(8,128)S(1)} collective-permute-done((f32[8,32,128]{2,1,0:T(8,128)S(1)}, f32[8,32,128]{2,1,0:T(8,128)S(1)}, u32[]{:S(2)}, u32[]{:S(2)}) %collective-permute-start.11) | collective-permute-done | bytes 131104 | tf_op jit(solution)/shard_map/ppermute | solution.py:62
  41.4 2.3 %collective-permute-done.13.x3 = f32[8,32,128]{2,1,0:T(8,128)S(1)} collective-permute-done((f32[8,32,128]{2,1,0:T(8,128)S(1)}, f32[8,32,128]{2,1,0:T(8,128)S(1)}, u32[]{:S(2)}, u32[]{:S(2)}) %collective-permute-start.13) | collective-permute-done | bytes 131104 | tf_op jit(solution)/shard_map/ppermute | solution.py:62
  46.4 4.2 %collective-permute-done.15.refs_0_.refs_2_ = f32[3,16,32,128]{3,2,1,0:T(8,128)S(1)} collective-permute-done((f32[3,16,32,128]{3,2,1,0:T(8,128)S(1)}, f32[3,16,32,128]{3,2,1,0:T(8,128)S(1)}, u32[]{:S(2)}, u32[]{:S(2)}) %collective-permute-start.15) | collective-permute-done | bytes 786464 | tf_op jit(solution)/shard_map/ppermute | solution.py:62
  52.2 3.7 %collective-permute-done.16.u2.refs_0_ = f32[6,32,128]{2,1,0:T(8,128)S(1)} collective-permute-done((f32[6,32,128]{2,1,0:T(8,128)S(1)}, f32[6,32,128]{2,1,0:T(8,128)S(1)}, u32[]{:S(2)}, u32[]{:S(2)}) %collective-permute-start.16) | collective-permute-done | bytes 98336 | tf_op jit(solution)/shard_map/ppermute | solution.py:62
  58.9 6.5 %collective-permute-done.17 = f32[4,32,128]{2,1,0:T(8,128)S(1)} collective-permute-done((f32[4,32,128]{2,1,0:T(8,128)S(1)}, f32[4,32,128]{2,1,0:T(8,128)S(1)}, u32[]{:S(2)}, u32[]{:S(2)}) %collective-permute-start.17) | collective-permute-done | bytes 65568 | tf_op jit(solution)/shard_map/ppermute | solution.py:62
  67.1 1.8 %collective-permute-start.20 = (f32[8,32,128]{2,1,0:T(8,128)S(1)}, f32[8,32,128]{2,1,0:T(8,128)S(1)}, u32[]{:S(2)}, u32[]{:S(2)}) collective-permute-start(f32[8,32,128]{2,1,0:T(8,128)S(1)} %constant_dynamic-update-slice_fusion.2.x0), channel_id=1, source_target_pairs={{0,12},{4,8},{8,4},{12,0},{16,28},{20,24},{24,20},{28,16},{1,13},{... | collective-permute-start | bytes 393224 | tf_op jit(solution)/shard_map/ppermute | solution.py:62
  73.3 3.0 %shard_map.59 = (f32[4,32,128]{2,1,0:T(8,128)S(1)}, f32[8,32,128]{2,1,0:T(8,128)S(1)}, f32[8,32,128]{2,1,0:T(8,128)S(1)}, f32[8,32,128]{2,1,0:T(8,128)S(1)}, f32[8,32,128]{2,1,0:T(8,128)S(1)}) custom-call(s32[64]{0:T(128)S(1)} %get-tuple-element.90.slot_ref, f32[8,32,128]{2,1,0:T(8,128)S(1)} %constant_dynamic-update-slice_fusion.2.x0, ...), custom_call_target="tpu_custom_call" | custom-call | flops 1 | bytes 1 | tf_op jit(solution)/shard_map/pallas_call | solution.py:473
  79.9 3.6 %collective-permute-done.28.value_ref = f32[5,16,32,128]{3,2,1,0:T(8,128)S(1)} collective-permute-done((f32[5,16,32,128]{3,2,1,0:T(8,128)S(1)}, f32[5,16,32,128]{3,2,1,0:T(8,128)S(1)}, u32[]{:S(2)}, u32[]{:S(2)}) %collective-permute-start.28) | collective-permute-done | bytes 1310752 | tf_op jit(solution)/shard_map/ppermute | solution.py:62
  88.1 2.3 %shard_map.63.refs_1_ = bf16[3,2048,256]{2,1,0:T(8,128)(2,1)S(1)} custom-call(s32[1]{0:T(128)} %bitcast.col_ref, f32[3,4,16,32,128]{4,3,2,1,0:T(8,128)S(1)} %copy-done.1, f32[3,4,16,32,128]{4,3,2,1,0:T(8,128)} %collective-permute-done.21.refs_1_, f32[5,16,32,128]{3,2,1,0:T(8,128)S(1)} %shard_map.62.refs_2_, ...), custom_call_target="tpu_custom_call" | custom-call | flops 1 | bytes 1 | tf_op jit(solution)/shard_map/pallas_call | solution.py:378
  91.9 2.1 %shard_map.64 = (f32[4,32,128]{2,1,0:T(8,128)S(1)}, f32[8,32,128]{2,1,0:T(8,128)S(1)}, f32[8,32,128]{2,1,0:T(8,128)S(1)}, f32[8,32,128]{2,1,0:T(8,128)S(1)}, f32[8,32,128]{2,1,0:T(8,128)S(1)}) custom-call(s32[64]{0:T(128)S(1)} %get-tuple-element.91.slot_ref, f32[4,32,128]{2,1,0:T(8,128)S(1)} %get-tuple-element.89.ret0, ...), custom_call_target="tpu_custom_call" | custom-call | flops 1 | bytes 1 | tf_op jit(solution)/shard_map/pallas_call | solution.py:483
  95.2 1.8 %collective-permute-start.31 = (f32[8,32,128]{2,1,0:T(8,128)S(1)}, f32[8,32,128]{2,1,0:T(8,128)S(1)}, u32[]{:S(2)}, u32[]{:S(2)}) collective-permute-start(f32[8,32,128]{2,1,0:T(8,128)S(1)} %get-tuple-element.59), channel_id=1, source_target_pairs={{0,8},{4,12},{8,0},{12,4},{16,24},{20,28},{24,16},{28,20},{1,9},{5... | collective-permute-start | bytes 393224 | tf_op jit(solution)/shard_map/ppermute | solution.py:62
  102.2 2.5 %collective-permute-start.33 = (f32[4,32,128]{2,1,0:T(8,128)S(1)}, f32[4,32,128]{2,1,0:T(8,128)S(1)}, u32[]{:S(2)}, u32[]{:S(2)}) collective-permute-start(f32[4,32,128]{2,1,0:T(8,128)S(1)} %get-tuple-element.86), channel_id=1, source_target_pairs={{0,16},{4,20},{8,24},{12,28},{16,0},{20,4},{24,8},{28,12},{1,17},{... | collective-permute-start | bytes 196616 | tf_op jit(solution)/shard_map/ppermute | solution.py:62
  109.0 2.1 %shard_map.69 = (f32[4,32,128]{2,1,0:T(8,128)S(1)}, f32[8,32,128]{2,1,0:T(8,128)S(1)}, f32[8,32,128]{2,1,0:T(8,128)S(1)}, f32[8,32,128]{2,1,0:T(8,128)S(1)}, f32[8,32,128]{2,1,0:T(8,128)S(1)}) custom-call(s32[64]{0:T(128)S(1)} %get-tuple-element.92.slot_ref, f32[4,32,128]{2,1,0:T(8,128)S(1)} %get-tuple-element.87.ret0, ...), custom_call_target="tpu_custom_call" | custom-call | flops 1 | bytes 1 | tf_op jit(solution)/shard_map/pallas_call | solution.py:489
  112.2 2.4 %collective-permute-start.36 = (f32[8,32,128]{2,1,0:T(8,128)S(1)}, f32[8,32,128]{2,1,0:T(8,128)S(1)}, u32[]{:S(2)}, u32[]{:S(2)}) collective-permute-start(f32[8,32,128]{2,1,0:T(8,128)S(1)} %get-tuple-element.64), channel_id=1, source_target_pairs={{0,4},{4,0},{8,12},{12,8},{16,20},{20,16},{24,28},{28,24},{1,5},{5... | collective-permute-start | bytes 393224 | tf_op jit(solution)/shard_map/ppermute | solution.py:62
  114.7 3.2 %collective-permute-done.38.refs_5_ = f32[8,32,128]{2,1,0:T(8,128)S(1)} collective-permute-done((f32[8,32,128]{2,1,0:T(8,128)S(1)}, f32[8,32,128]{2,1,0:T(8,128)S(1)}, u32[]{:S(2)}, u32[]{:S(2)}) %collective-permute-start.38) | collective-permute-done | bytes 131104 | tf_op jit(solution)/shard_map/ppermute | solution.py:62
  119.0 2.8 %collective-permute-start.39 = (f32[4,32,128]{2,1,0:T(8,128)S(1)}, f32[4,32,128]{2,1,0:T(8,128)S(1)}, u32[]{:S(2)}, u32[]{:S(2)}) collective-permute-start(f32[4,32,128]{2,1,0:T(8,128)S(1)} %get-tuple-element.84), channel_id=1, source_target_pairs={{0,16},{4,20},{8,24},{12,28},{16,0},{20,4},{24,8},{28,12},{1,17},{... | collective-permute-start | bytes 196616 | tf_op jit(solution)/shard_map/ppermute | solution.py:62
  125.2 4.3 %collective-permute-start.41 = (f32[1,32,128]{2,1,0:T(8,128)S(1)}, f32[1,32,128]{2,1,0:T(8,128)S(1)}, u32[]{:S(2)}, u32[]{:S(2)}) collective-permute-start(f32[1,32,128]{2,1,0:T(8,128)S(1)} %get-tuple-element.69), channel_id=1, source_target_pairs={{0,2},{1,3},{2,0},{3,1},{4,6},{5,7},{6,4},{7,5},{8,10},{9,11},{10,... | collective-permute-start | bytes 49160 | tf_op jit(solution)/shard_map/ppermute | solution.py:62
  (130 shorter events, 65.6 us)
Async XLA Ops:
  0.0 13.8 %collective-permute-start = (f32[16,32,128]{2,1,0:T(8,128)}, f32[16,32,128]{2,1,0:T(8,128)}, u32[]{:S(2)}, u32[]{:S(2)}) collective-permute-start(f32[16,32,128]{2,1,0:T(8,128)} %bitcast.10), channel_id=1, source_target_pairs={{0,1},{1,0},{2,3},{3,2},{4,5},{5,4},{6,7},{7,6},{8,9},{9,8},{10,11... | collective-permute-start | bytes 786440 | tf_op jit(solution)/shard_map/ppermute | solution.py:62
  0.5 9.8 %collective-permute-start.1 = (f32[16,32,128]{2,1,0:T(8,128)}, f32[16,32,128]{2,1,0:T(8,128)}, u32[]{:S(2)}, u32[]{:S(2)}) collective-permute-start(f32[16,32,128]{2,1,0:T(8,128)} %bitcast.11), channel_id=1, source_target_pairs={{0,2},{1,3},{2,0},{3,1},{4,6},{5,7},{6,4},{7,5},{8,10},{9,11},{10,... | collective-permute-start | bytes 786440 | tf_op jit(solution)/shard_map/ppermute | solution.py:62
  3.0 64.0 %collective-permute-start.21 = (f32[3,4,16,32,128]{4,3,2,1,0:T(8,128)}, f32[3,4,16,32,128]{4,3,2,1,0:T(8,128)}, u32[]{:S(2)}, u32[]{:S(2)}) collective-permute-start(f32[3,4,16,32,128]{4,3,2,1,0:T(8,128)} %refs_0_.11), channel_id=1, source_target_pairs={{0,1},{1,0},{2,3},{3,2},{4,5},{5,4},{6,7},{7,6},{8,9},{9,8},{10,11... | collective-permute-start | bytes 9437192 | tf_op jit(solution)/shard_map/ppermute | solution.py:62
  5.4 6.9 %collective-permute-start.3 = (f32[4,32,128]{2,1,0:T(8,128)}, f32[4,32,128]{2,1,0:T(8,128)S(1)}, u32[]{:S(2)}, u32[]{:S(2)}) collective-permute-start(f32[4,32,128]{2,1,0:T(8,128)} %get-tuple-element.43), channel_id=1, source_target_pairs={{0,16},{4,20},{8,24},{12,28},{16,0},{20,4},{24,8},{28,12},{1,17},{... | collective-permute-start | bytes 196616 | tf_op jit(solution)/shard_map/ppermute | solution.py:62
  8.0 16.1 %collective-permute-start.8 = (f32[2,16,32,128]{3,2,1,0:T(8,128)}, f32[2,16,32,128]{3,2,1,0:T(8,128)}, u32[]{:S(2)}, u32[]{:S(2)}) collective-permute-start(f32[2,16,32,128]{3,2,1,0:T(8,128)} %get-tuple-element.48), channel_id=1, source_target_pairs={{0,2},{1,3},{2,0},{3,1},{4,6},{5,7},{6,4},{7,5},{8,10},{9,11},{10,... | collective-permute-start | bytes 1572872 | tf_op jit(solution)/shard_map/ppermute | solution.py:62
  12.3 7.8 %collective-permute-start.4 = (f32[8,32,128]{2,1,0:T(8,128)S(1)}, f32[8,32,128]{2,1,0:T(8,128)S(1)}, u32[]{:S(2)}, u32[]{:S(2)}) collective-permute-start(f32[8,32,128]{2,1,0:T(8,128)S(1)} %constant_dynamic-update-slice_fusion.x0), channel_id=1, source_target_pairs={{0,4},{4,0},{8,12},{12,8},{16,20},{20,16},{24,28},{28,24},{1,5},{5... | collective-permute-start | bytes 393224 | tf_op jit(solution)/shard_map/ppermute | solution.py:62
  13.8 6.3 %collective-permute-start.5 = (f32[8,32,128]{2,1,0:T(8,128)S(1)}, f32[8,32,128]{2,1,0:T(8,128)S(1)}, u32[]{:S(2)}, u32[]{:S(2)}) collective-permute-start(f32[8,32,128]{2,1,0:T(8,128)S(1)} %constant_dynamic-update-slice_fusion.x0), channel_id=1, source_target_pairs={{0,8},{4,12},{8,0},{12,4},{16,24},{20,28},{24,16},{28,20},{1,9},{5... | collective-permute-start | bytes 393224 | tf_op jit(solution)/shard_map/ppermute | solution.py:62
  14.6 7.0 %collective-permute-start.6 = (f32[8,32,128]{2,1,0:T(8,128)S(1)}, f32[8,32,128]{2,1,0:T(8,128)S(1)}, u32[]{:S(2)}, u32[]{:S(2)}) collective-permute-start(f32[8,32,128]{2,1,0:T(8,128)S(1)} %constant_dynamic-update-slice_fusion.x0), channel_id=1, source_target_pairs={{0,12},{4,8},{8,4},{12,0},{16,28},{20,24},{24,20},{28,16},{1,13},{... | collective-permute-start | bytes 393224 | tf_op jit(solution)/shard_map/ppermute | solution.py:62
  32.4 18.2 %collective-permute-start.15 = (f32[3,16,32,128]{3,2,1,0:T(8,128)S(1)}, f32[3,16,32,128]{3,2,1,0:T(8,128)S(1)}, u32[]{:S(2)}, u32[]{:S(2)}) collective-permute-start(f32[3,16,32,128]{3,2,1,0:T(8,128)S(1)} %shard_map.53), channel_id=1, source_target_pairs={{0,2},{1,3},{2,0},{3,1},{4,6},{5,7},{6,4},{7,5},{8,10},{9,11},{10,... | collective-permute-start | bytes 2359304 | tf_op jit(solution)/shard_map/ppermute | solution.py:62
  34.9 6.4 %collective-permute-start.11 = (f32[8,32,128]{2,1,0:T(8,128)S(1)}, f32[8,32,128]{2,1,0:T(8,128)S(1)}, u32[]{:S(2)}, u32[]{:S(2)}) collective-permute-start(f32[8,32,128]{2,1,0:T(8,128)S(1)} %pad_maximum_fusion.x0), channel_id=1, source_target_pairs={{0,4},{4,0},{8,12},{12,8},{16,20},{20,16},{24,28},{28,24},{1,5},{5... | collective-permute-start | bytes 393224 | tf_op jit(solution)/shard_map/ppermute | solution.py:62
  56.1 27.3 %collective-permute-start.28 = (f32[5,16,32,128]{3,2,1,0:T(8,128)S(1)}, f32[5,16,32,128]{3,2,1,0:T(8,128)S(1)}, u32[]{:S(2)}, u32[]{:S(2)}) collective-permute-start(f32[5,16,32,128]{3,2,1,0:T(8,128)S(1)} %shard_map.61), channel_id=1, source_target_pairs={{0,2},{1,3},{2,0},{3,1},{4,6},{5,7},{6,4},{7,5},{8,10},{9,11},{10,... | collective-permute-start | bytes 3932168 | tf_op jit(solution)/shard_map/ppermute | solution.py:62
  57.7 12.7 %collective-permute-start.23 = (f32[3,16,32,128]{3,2,1,0:T(8,128)S(1)}, f32[3,16,32,128]{3,2,1,0:T(8,128)S(1)}, u32[]{:S(2)}, u32[]{:S(2)}) collective-permute-start(f32[3,16,32,128]{3,2,1,0:T(8,128)S(1)} %collective-permute-done.15.refs_0_.refs_2_), channel_id=1, source_target_pairs={{0,1},{1,0},{2,3},{3,2},{4,5},{5,4},{6,7},{7,6},{8,9},{9,8},{10,11... | collective-permute-start | bytes 2359304 | tf_op jit(solution)/shard_map/ppermute | solution.py:62
  57.7 9.2 %collective-permute-start.22 = (f32[2,16,32,128]{3,2,1,0:T(8,128)}, f32[2,16,32,128]{3,2,1,0:T(8,128)S(1)}, u32[]{:S(2)}, u32[]{:S(2)}) collective-permute-start(f32[2,16,32,128]{3,2,1,0:T(8,128)} %collective-permute-done.8.refs_0_.refs_2_), channel_id=1, source_target_pairs={{0,1},{1,0},{2,3},{3,2},{4,5},{5,4},{6,7},{7,6},{8,9},{9,8},{10,11... | collective-permute-start | bytes 1572872 | tf_op jit(solution)/shard_map/ppermute | solution.py:62
  58.8 6.6 %collective-permute-start.17 = (f32[4,32,128]{2,1,0:T(8,128)S(1)}, f32[4,32,128]{2,1,0:T(8,128)S(1)}, u32[]{:S(2)}, u32[]{:S(2)}) collective-permute-start(f32[4,32,128]{2,1,0:T(8,128)S(1)} %get-tuple-element.52.forward_ref), channel_id=1, source_target_pairs={{0,16},{4,20},{8,24},{12,28},{16,0},{20,4},{24,8},{28,12},{1,17},{... | collective-permute-start | bytes 196616 | tf_op jit(solution)/shard_map/ppermute | solution.py:62
  65.4 6.4 %collective-permute-start.18 = (f32[8,32,128]{2,1,0:T(8,128)S(1)}, f32[8,32,128]{2,1,0:T(8,128)S(1)}, u32[]{:S(2)}, u32[]{:S(2)}) collective-permute-start(f32[8,32,128]{2,1,0:T(8,128)S(1)} %constant_dynamic-update-slice_fusion.2.x0), channel_id=1, source_target_pairs={{0,4},{4,0},{8,12},{12,8},{16,20},{20,16},{24,28},{28,24},{1,5},{5... | collective-permute-start | bytes 393224 | tf_op jit(solution)/shard_map/ppermute | solution.py:62
  76.3 7.1 %collective-permute-start.26 = (f32[8,32,128]{2,1,0:T(8,128)S(1)}, f32[8,32,128]{2,1,0:T(8,128)S(1)}, u32[]{:S(2)}, u32[]{:S(2)}) collective-permute-start(f32[8,32,128]{2,1,0:T(8,128)S(1)} %get-tuple-element.56), channel_id=1, source_target_pairs={{0,12},{4,8},{8,4},{12,0},{16,28},{20,24},{24,20},{28,16},{1,13},{... | collective-permute-start | bytes 393224 | tf_op jit(solution)/shard_map/ppermute | solution.py:62
  84.5 14.4 %collective-permute-start.34 = (f32[2,16,32,128]{3,2,1,0:T(8,128)S(1)}, f32[2,16,32,128]{3,2,1,0:T(8,128)S(1)}, u32[]{:S(2)}, u32[]{:S(2)}) collective-permute-start(f32[2,16,32,128]{3,2,1,0:T(8,128)S(1)} %shard_map.66), channel_id=1, source_target_pairs={{0,2},{1,3},{2,0},{3,1},{4,6},{5,7},{6,4},{7,5},{8,10},{9,11},{10,... | collective-permute-start | bytes 1572872 | tf_op jit(solution)/shard_map/ppermute | solution.py:62
  85.3 6.6 %collective-permute-start.27 = (f32[4,32,128]{2,1,0:T(8,128)S(1)}, f32[4,32,128]{2,1,0:T(8,128)S(1)}, u32[]{:S(2)}, u32[]{:S(2)}) collective-permute-start(f32[4,32,128]{2,1,0:T(8,128)S(1)} %get-tuple-element.88), channel_id=1, source_target_pairs={{0,16},{4,20},{8,24},{12,28},{16,0},{20,4},{24,8},{28,12},{1,17},{... | collective-permute-start | bytes 196616 | tf_op jit(solution)/shard_map/ppermute | solution.py:62
  95.2 6.3 %collective-permute-start.31 = (f32[8,32,128]{2,1,0:T(8,128)S(1)}, f32[8,32,128]{2,1,0:T(8,128)S(1)}, u32[]{:S(2)}, u32[]{:S(2)}) collective-permute-start(f32[8,32,128]{2,1,0:T(8,128)S(1)} %get-tuple-element.59), channel_id=1, source_target_pairs={{0,8},{4,12},{8,0},{12,4},{16,24},{20,28},{24,16},{28,20},{1,9},{5... | collective-permute-start | bytes 393224 | tf_op jit(solution)/shard_map/ppermute | solution.py:62
  102.2 6.9 %collective-permute-start.33 = (f32[4,32,128]{2,1,0:T(8,128)S(1)}, f32[4,32,128]{2,1,0:T(8,128)S(1)}, u32[]{:S(2)}, u32[]{:S(2)}) collective-permute-start(f32[4,32,128]{2,1,0:T(8,128)S(1)} %get-tuple-element.86), channel_id=1, source_target_pairs={{0,16},{4,20},{8,24},{12,28},{16,0},{20,4},{24,8},{28,12},{1,17},{... | collective-permute-start | bytes 196616 | tf_op jit(solution)/shard_map/ppermute | solution.py:62
  111.1 6.7 %collective-permute-start.38 = (f32[8,32,128]{2,1,0:T(8,128)S(1)}, f32[8,32,128]{2,1,0:T(8,128)S(1)}, u32[]{:S(2)}, u32[]{:S(2)}) collective-permute-start(f32[8,32,128]{2,1,0:T(8,128)S(1)} %get-tuple-element.66), channel_id=1, source_target_pairs={{0,12},{4,8},{8,4},{12,0},{16,28},{20,24},{24,20},{28,16},{1,13},{... | collective-permute-start | bytes 393224 | tf_op jit(solution)/shard_map/ppermute | solution.py:62
  112.2 6.7 %collective-permute-start.36 = (f32[8,32,128]{2,1,0:T(8,128)S(1)}, f32[8,32,128]{2,1,0:T(8,128)S(1)}, u32[]{:S(2)}, u32[]{:S(2)}) collective-permute-start(f32[8,32,128]{2,1,0:T(8,128)S(1)} %get-tuple-element.64), channel_id=1, source_target_pairs={{0,4},{4,0},{8,12},{12,8},{16,20},{20,16},{24,28},{28,24},{1,5},{5... | collective-permute-start | bytes 393224 | tf_op jit(solution)/shard_map/ppermute | solution.py:62
  122.0 7.6 %collective-permute-start.43 = (f32[3,32,128]{2,1,0:T(8,128)S(1)}, f32[3,32,128]{2,1,0:T(8,128)S(1)}, u32[]{:S(2)}, u32[]{:S(2)}) collective-permute-start(f32[3,32,128]{2,1,0:T(8,128)S(1)} %get-tuple-element.74), channel_id=1, source_target_pairs={{0,1},{1,0},{2,3},{3,2},{4,5},{5,4},{6,7},{7,6},{8,9},{9,8},{10,11... | collective-permute-start | bytes 147464 | tf_op jit(solution)/shard_map/ppermute | solution.py:62
  122.0 7.6 %collective-permute-start.44 = (f32[3,32,128]{2,1,0:T(8,128)S(1)}, f32[3,32,128]{2,1,0:T(8,128)S(1)}, u32[]{:S(2)}, u32[]{:S(2)}) collective-permute-start(f32[3,32,128]{2,1,0:T(8,128)S(1)} %get-tuple-element.75), channel_id=1, source_target_pairs={{0,2},{1,3},{2,0},{3,1},{4,6},{5,7},{6,4},{7,5},{8,10},{9,11},{10,... | collective-permute-start | bytes 147464 | tf_op jit(solution)/shard_map/ppermute | solution.py:62
  (27 other events, 150.2 us)

commit v4 on v3

--- a/solution.py
+++ b/solution.py
@@ -14,6 +14,7 @@
 SMEM = pl.BlockSpec(memory_space=pltpu.SMEM)
 ANY = pl.BlockSpec(memory_space=pl.ANY)
 HBM = pl.BlockSpec(memory_space=pltpu.HBM)
+CUTS = (0.625, 0.25, 0.5)
 TINY = pl.CostEstimate(flops=1, bytes_accessed=1, transcendentals=0)
 
 
@@ -98,11 +99,11 @@
     return got, (total, other)
 
 
-def first_kernel(level, inverse_ref, sides_ref, lower_ref, out_ref, early_ref, inverse, sides, sems):
+def first_kernel(start, inverse_ref, sides_ref, lower_ref, out_ref, early_ref, inverse, sides, sems):
     copies = [
         pltpu.make_async_copy(inverse_ref.at[0], inverse, sems.at[0]),
         pltpu.make_async_copy(sides_ref.at[0], sides, sems.at[1]),
-        pltpu.make_async_copy(lower_ref.at[level - 1, pl.ds(0, early_ref.shape[0])], early_ref, sems.at[2]),
+        pltpu.make_async_copy(lower_ref.at[pl.ds(start, early_ref.shape[0])], early_ref, sems.at[2]),
     ]
     for copy in copies:
         copy.start()
@@ -113,23 +114,15 @@
     copies[2].wait()
 
 
-def turn_kernel(col_ref, sides_ref, out_ref, whole):
-    count = out_ref.shape[1]
-    start = pl.multiple_of(col_ref[0] * count, count)
-    for i in range(out_ref.shape[0]):
-        whole[i % 2] = sides_ref[i].T
-        out_ref[i] = whole[i % 2, pl.ds(start, count), :]
-
-
-def join_kernel(col_ref, *refs):
+def join_kernel(place, some, col_ref, *refs):
     parts, out_ref = refs[:-1], refs[-1]
-    share, width = parts[0].shape[2:]
+    _, share, width = parts[0].shape
     for mask, part in enumerate(parts):
         offset = pl.multiple_of((col_ref[0] ^ mask) * share, share)
-        for d in range(part.shape[1]):
-            high, low = split(part[0, d])
-            out_ref[0, pl.ds(d * width + offset, share), :width] = high
-            out_ref[0, pl.ds(d * width + offset, share), width:] = low
+        for d in range(some):
+            high, low = split(part[place + d])
+            out_ref[pl.ds(d * width + offset, share), :width] = high
+            out_ref[pl.ds(d * width + offset, share), width:] = low
 
 
 def join_inverse_kernel(col_ref, *refs):
@@ -144,11 +137,20 @@
             out_ref[i, pl.ds(offset, share), width:] = low
 
 
-def stand_kernel(level, lower_ref, after_ref, out_ref, own, sem):
+def stand_kernel(level, col_ref, lower_ref, all_sides_ref, after_ref, out_ref, sides_ref, own, sides, whole, sems):
     count, fan_in, share, width = own.shape
-    copy = pltpu.make_async_copy(lower_ref.at[level], own, sem)
-    copy.start()
-    copy.wait()
+    copies = [
+        pltpu.make_async_copy(all_sides_ref, sides, sems.at[0]),
+        pltpu.make_async_copy(lower_ref.at[level], own, sems.at[1]),
+    ]
+    for copy in copies:
+        copy.start()
+    copies[0].wait()
+    start = pl.multiple_of(col_ref[0] * sides_ref.shape[1], sides_ref.shape[1])
+    for i in range(sides_ref.shape[0]):
+        whole[i % 2] = sides[i // count, i % count].T
+        sides_ref[i] = whole[i % 2, pl.ds(start, sides_ref.shape[1]), :]
+    copies[1].wait()
     for j in range(count):
         high, low = split(own[j].reshape(fan_in * share, width).T)
         out_ref[j, :width] = high
@@ -214,14 +216,15 @@
             lower_ref[j, :, c * share:(c + 1) * share] = part[:, j * share:(j + 1) * share]
 
 
-def block_of(lower, j):
-    for some in lower:
-        if j < some.shape[0]:
-            return some[j]
-        j -= some.shape[0]
-
-
-def forward_levels(slot_ref, xs, sides_ref, inverse_ref, lower, out_ref, blocks, picked):
+def runs_of(spans, lower, j, fan_in):
+    width = lower[0].shape[1] // 2
+    for (start, end), ref in zip(spans, lower):
+        low, high = max(start, j * fan_in), min(end, (j + 1) * fan_in)
+        if low < high:
+            yield low - j * fan_in, high - j * fan_in, ref[(low - start) * width:(high - start) * width, :]
+
+
+def forward_levels(spans, slot_ref, xs, sides_ref, inverse_ref, lower, out_ref, blocks, picked):
     count, columns, width = out_ref.shape
     fan_in = slot_ref.shape[0] // count
     each = xs[0].shape[0]
@@ -235,41 +238,46 @@
             picked[j, :, d * width:(d + 1) * width] = blocks[slot_ref[j * fan_in + d]]
     rest = []
     for j in range(count):
-        both = half(picked[j], block_of(lower, j), (1, 0))
-        both = both[:, :width] + both[:, width:]
-        rest.append(sides_ref[j] - (both[:columns] + both[columns:]))
+        value = sides_ref[j]
+        for low, high, rows in runs_of(spans, lower, j, fan_in):
+            both = half(picked[j, :, low * width:high * width], rows, (1, 0))
+            both = both[:, :width] + both[:, width:]
+            value = value - (both[:columns] + both[columns:])
+        rest.append(value)
     for j in range(count):
         out_ref[j] = times_turned(rest[j], inverse_ref[j])
 
 
-def backward_terms(slot_ref, solved, lower, outs, total):
+def backward_terms(spans, slot_ref, solved, lower, outs, total):
     count, _, width = solved.shape
     fan_in = slot_ref.shape[0] // count
     total[...] = jnp.zeros_like(total)
     for j in range(count):
-        terms = times_turned(solved[j], block_of(lower, j))
-        for d in range(fan_in):
-            slot = slot_ref[j * fan_in + d]
-            total[slot] = total[slot] + terms[:, d * width:(d + 1) * width]
+        for low, high, rows in runs_of(spans, lower, j, fan_in):
+            terms = times_turned(solved[j], rows)
+            for d in range(low, high):
+                slot = slot_ref[j * fan_in + d]
+                total[slot] = total[slot] + terms[:, (d - low) * width:(d - low + 1) * width]
     each = outs[0].shape[0]
     for q, out in enumerate(outs):
         out[...] = total[q * each:(q + 1) * each]
 
 
-def top_kernel(chunks, slot_ref, x0, x1, x2, x3, sides_ref, inverse_ref, *refs):
+def top_kernel(spans, slot_ref, x0, x1, x2, x3, sides_ref, inverse_ref, *refs):
+    chunks = len(spans)
     lower, outs = refs[:chunks], refs[chunks + 1:chunks + 5]
     sol_ref, (blocks, picked, solved, total) = refs[chunks], refs[chunks + 5:]
-    forward_levels(slot_ref, (x0, x1, x2, x3), sides_ref, inverse_ref, lower, solved, blocks, picked)
+    forward_levels(spans, slot_ref, (x0, x1, x2, x3), sides_ref, inverse_ref, lower, solved, blocks, picked)
     for j in range(sol_ref.shape[0]):
         sol_ref[j] = times(solved[j], inverse_ref[j])
-    backward_terms(slot_ref, sol_ref, lower, outs, total)
-
-
-def backward_kernel(chunks, slot_ref, ret0, ret1, forward_ref, inverse_ref, *refs):
-    lower, (sol_ref, *outs, total) = refs[:chunks], refs[-6:]
+    backward_terms(spans, slot_ref, sol_ref, lower, outs, total)
+
+
+def backward_kernel(spans, slot_ref, ret0, ret1, forward_ref, inverse_ref, *refs):
+    lower, (sol_ref, *outs, total) = refs[:len(spans)], refs[-6:]
     for j in range(sol_ref.shape[0]):
         sol_ref[j] = times(forward_ref[j] - (ret0[j] + ret1[j]), inverse_ref[j])
-    backward_terms(slot_ref, sol_ref, lower, outs, total)
+    backward_terms(spans, slot_ref, sol_ref, lower, outs, total)
 
 
 def cut(col_ref, sources, outs, packed):
@@ -314,11 +322,11 @@
     refs[-1][...] = value_ref[...]
 
 
-def after(value, *others):
+def after(value, *others, spec=VMEM):
     return pl.pallas_call(
         same_kernel,
         out_shape=jax.ShapeDtypeStruct(value.shape, value.dtype),
-        in_specs=[VMEM] * (1 + len(others)),
+        in_specs=[VMEM] + [spec] * len(others),
         out_specs=VMEM,
         compiler_params=pltpu.CompilerParams(vmem_limit_bytes=8 * 1024 * 1024),
         cost_estimate=TINY,
@@ -328,10 +336,8 @@
 def pack_kernel(pieces, lower_ref, *refs):
     out_ref, sems = refs[-2:]
     copies, place = [], 0
-    for i, (level, start, size) in enumerate(pieces):
-        copies.append(
-            pltpu.make_async_copy(lower_ref.at[level, pl.ds(start, size)], out_ref.at[pl.ds(place, size)], sems.at[i])
-        )
+    for i, (start, size) in enumerate(pieces):
+        copies.append(pltpu.make_async_copy(lower_ref.at[pl.ds(start, size)], out_ref.at[pl.ds(place, size)], sems.at[i]))
         place += size
     for copy in copies:
         copy.start()
@@ -339,17 +345,17 @@
         copy.wait()
 
 
-def pack(lower_blocks, pieces, *others):
-    total = sum(size for _, _, size in pieces)
+def pack(blocks, pieces, *others):
+    total = sum(size for _, size in pieces)
     return pl.pallas_call(
         functools.partial(pack_kernel, pieces),
-        out_shape=jax.ShapeDtypeStruct((total,) + lower_blocks.shape[2:], F32),
+        out_shape=jax.ShapeDtypeStruct((total,) + blocks.shape[1:], F32),
         in_specs=[HBM] + [VMEM] * len(others),
         out_specs=VMEM,
         scratch_shapes=[pltpu.SemaphoreType.DMA((len(pieces),))],
         compiler_params=pltpu.CompilerParams(vmem_limit_bytes=8 * 1024 * 1024),
         cost_estimate=TINY,
-    )(lower_blocks, *others)
+    )(blocks, *others)
 
 
 def on_device(right_sides, inverse_diag, lower_blocks, depends_on):
@@ -371,50 +377,38 @@
     block = like(count, mine, width)
     quarter = like(rows // 4 * count, mine, width)
 
-    def join(level, start, some, parts, place=0):
-        own_spec = pl.BlockSpec((None, 1, fan_in, share, width), lambda j: (level, start + j, 0, 0, 0))
-        part_spec = pl.BlockSpec((1, fan_in, share, width), lambda j: (place + j, 0, 0, 0))
-        out_spec = pl.BlockSpec((1, fan_in * width, 2 * width), lambda j: (j, 0, 0))
-        return pl.pallas_call(
-            join_kernel,
-            grid=(some,),
-            out_shape=like(some, fan_in * width, 2 * width, dtype=BF16),
-            in_specs=[SMEM, own_spec, own_spec, part_spec, part_spec],
-            out_specs=out_spec,
-            compiler_params=pltpu.CompilerParams(vmem_limit_bytes=24 * 1024 * 1024),
-            cost_estimate=TINY,
-        )(col, lower_blocks, lower_beside, *parts)
+    def join(parts, place, some):
+        return call(
+            functools.partial(join_kernel, place, some), like(some * width, 2 * width, dtype=BF16), [SMEM] + [VMEM] * cols
+        )(col, *parts)
 
     def near(value):
         return value, swap(value, "col", 1)
 
     top = levels - 1
-    middle = count // 2
+    flat = lower_blocks.reshape((levels - 1) * entries, share, width)
+    unit = fan_in // 2
+    cuts = [int(entries * part) // unit * unit for part in CUTS]
+    spans = [((0, cut), (cut, entries)) for cut in cuts]
+    at2, at1, at0 = (top - 1) * entries, (top - 2) * entries, (top - 3) * entries
     first, early = call(
-        functools.partial(first_kernel, top), [like(count, share, columns), like(middle, fan_in, share, width)], [HBM] * 3,
+        functools.partial(first_kernel, at2), [like(count, share, columns), like(cuts[0], share, width)], [HBM] * 3,
         scratch=[
             pltpu.VMEM((count, share, width), F32),
             pltpu.VMEM((count, width, columns), F32),
             pltpu.SemaphoreType.DMA((3,)),
         ],
         limit=60,
-    )(inverse_diag, right_sides, lower_blocks)
-    early = swap(early, "col", 2)
+    )(inverse_diag, right_sides, flat)
+    early = near(early) + (swap(early, "col", 2),)
     _, gathered = gather_row(first)
     all_inverse = inverse_diag.reshape(levels * count, share, width)
     parts_inverse = near(all_inverse) + near(swap(all_inverse, "col", 2))
-    lower_beside = swap(lower_blocks, "col", 1)
 
     inverse, token = call(
         join_inverse_kernel, [like(levels * count, width, 2 * width, dtype=BF16), like(8, width)], [SMEM] + [VMEM] * cols
     )(col, *parts_inverse)
     inverse = [inverse[i * count:(i + 1) * count] for i in range(levels)]
-
-    sides = call(
-        turn_kernel, like(levels * count, mine, width), [SMEM, VMEM],
-        scratch=[pltpu.VMEM((2, columns, width), F32)],
-    )(col, right_sides.reshape(levels * count, width, columns))
-    sides = [sides[i * count:(i + 1) * count] for i in range(levels)]
 
     folded, base = call(
         fold_kernel, [like(count, 2 * width, fan_in * share, dtype=BF16), like(count, share, columns)], [HBM] * 3 + [VMEM],
@@ -441,23 +435,33 @@
         terms = passed[:count] + beside[each:each + count]
         if turn:
             terms = jnp.concatenate([terms, passed[count:], beside[each + count:]], axis=0)
-        return kept, beside[:each], swap(after(terms, hold), "col", 2)
-
-    kept, beside, across = partial(False, 0, gathered, folded, early)
+        return kept, beside[:each], swap(after(terms, hold, spec=VMEM if turn else ANY), "col", 2)
+
+    kept, beside, across = partial(False, 0, gathered, folded, early[2])
     forward_rows = base - ((kept + beside) + across)
-    late = swap(pack(lower_blocks, [(top - 1, middle, count - middle), (1, 0, 1)], across), "col", 2)
+    late = pack(flat, [(at2 + cuts[0], entries - cuts[0]), (at1, cuts[1])], across)
+    late = near(late) + (swap(late, "col", 2),)
     got, gathered = gather_row(forward_rows)
 
     forward = [None] * levels
-    standing = call(
-        functools.partial(stand_kernel, 1), like(count, 2 * width, fan_in * share, dtype=BF16), [HBM, VMEM],
-        scratch=[pltpu.VMEM(lower_blocks.shape[1:], F32), pltpu.SemaphoreType.DMA],
-    )(lower_blocks, got)
-    updates = partial(True, 1, gathered, standing, late, forward_rows)
+    standing, sides = call(
+        functools.partial(stand_kernel, 1),
+        [like(count, 2 * width, fan_in * share, dtype=BF16), like(levels * count, mine, width)],
+        [SMEM, HBM, HBM, VMEM],
+        scratch=[
+            pltpu.VMEM(lower_blocks.shape[1:], F32),
+            pltpu.VMEM(right_sides.shape, F32),
+            pltpu.VMEM((2, columns, width), F32),
+            pltpu.SemaphoreType.DMA((2,)),
+        ],
+    )(col, lower_blocks, right_sides, got)
+    sides = [sides[i * count:(i + 1) * count] for i in range(levels)]
+    updates = partial(True, 1, gathered, standing, late[2], forward_rows)
     forward[2], forward[1] = call(
         solve_kernel, [block] * 2, [SMEM] + [VMEM] * 5, scratch=[pltpu.VMEM((cols, mine, width), F32)]
     )(col, *updates, sides[2], inverse[2])
-    inner = swap(pack(lower_blocks, [(1, 1, count - 1), (0, 0, middle)], updates[2]), "col", 2)
+    inner = pack(flat, [(at1 + cuts[1], entries - cuts[1]), (at0, cuts[2])], updates[2])
+    inner_across = swap(inner, "col", 2)
 
     picking = [
         pltpu.VMEM((rows * count, 2 * mine, width), BF16),
@@ -467,27 +471,29 @@
 
     lower = [None] * (levels - 1)
     got, gathered = gather_row(forward[2])
-    early, late = near(early), near(late)
-    lower[2] = [join(top - 1, 0, middle, early), join(top - 1, middle, count - middle, late)]
+    early, late = early[:2] + near(early[2]), late[:2] + near(late[2])
+    lower[2] = [join(early, 0, cuts[0]), join(late, 0, entries - cuts[0])]
     solved = [None] * levels
     solved[top], *terms = call(
-        functools.partial(top_kernel, len(lower[2])), [block] + [quarter] * 4,
+        functools.partial(top_kernel, spans[0]), [block] + [quarter] * 4,
         [SMEM] + [VMEM] * 6 + [VMEM] * len(lower[2]),
         scratch=picking + [pltpu.VMEM((count, mine, width), F32)] + total,
     )(slots[2], *gathered, sides[top], inverse[top], *lower[2])
-    outer = swap(pack(lower_blocks, [(0, middle, count - middle)], solved[top]), "col", 2)
+    outer = pack(flat, [(at0 + cuts[2], entries - cuts[2])], solved[top])
+    outer_across = swap(outer, "col", 2)
 
     got, returned = scatter_row(terms)
-    inner = near(after(inner, *got))
-    lower[1] = [join(1, 0, 1, late, count - middle), join(1, 1, count - 1, inner)]
+    inner = near(inner) + near(after(inner_across, *got))
+    lower[1] = [join(late, entries - cuts[0], cuts[1]), join(inner, 0, entries - cuts[1])]
     solved[2], *terms = call(
-        functools.partial(backward_kernel, 2), [block] + [quarter] * 4, [SMEM] + [VMEM] * 6, scratch=total,
+        functools.partial(backward_kernel, spans[1]), [block] + [quarter] * 4, [SMEM] + [VMEM] * 6, scratch=total,
     )(slots[1], *returned, forward[2], inverse[2], *lower[1])
 
     got, returned = scatter_row(terms)
-    lower[0] = [join(0, 0, middle, inner, count - 1), join(0, middle, count - middle, near(after(outer, *got)))]
+    outer = near(outer) + near(after(outer_across, *got))
+    lower[0] = [join(inner, entries - cuts[1], cuts[2]), join(outer, 0, entries - cuts[2])]
     solved[1], *terms = call(
-        functools.partial(backward_kernel, 2), [block] + [quarter] * 4, [SMEM] + [VMEM] * 6, scratch=total,
+        functools.partial(backward_kernel, spans[2]), [block] + [quarter] * 4, [SMEM] + [VMEM] * 6, scratch=total,
     )(slots[0], *returned, forward[1], inverse[1], *lower[0])
 
     def spread(parts):

time: 134 us -> 132 us (0.985)
  waiting for transfers between devices: 50.8 us -> 61.7 us
  Pallas kernels: 27.7 us -> 19.4 us
  starting transfers between devices: 51.9 us -> 47.9 us
    ppermute x46 -> x49, waiting for transfers between devices: 50.8 us -> 61.7 us  [swap(): return lax.ppermute(value, axis, [(i, i ^ mask) for i in range(size)])]
    pallas_call x12 -> x11, Pallas kernels: 18.9 us -> 12.5 us  [the longest x1 2.99 us: on_device(): call(functools.partial(top_kernel, spans[0]), [block] + [quarter] * 4, [S...]
    ppermute x46 -> x49, starting transfers between devices: 51.9 us -> 47.9 us  [swap(): return lax.ppermute(value, axis, [(i, i ^ mask) for i in range(size)])]
  transfers between devices with their start and end apart: 46 -> 49, of which waited for: 31 -> 33; matrix products, arithmetic and copies ran while one was open for 1% -> 1% of each run, Pallas kernels for 18% -> 12%
where the time goes in v4:
time: 132 us
  waiting for transfers between devices  61.7 us (47%)
  starting transfers between devices  47.9 us (36%)
  Pallas kernels  19.4 us (15%)
  local copies, waits for them, and re-layouts  2.39 us (2%)
    ppermute x49, waiting for transfers between devices, swap(): return lax.ppermute(value, axis, [(i, i ^ mask) for i in range(size)])  61.7 us
    ppermute x49, starting transfers between devices, swap(): return lax.ppermute(value, axis, [(i, i ^ mask) for i in range(size)])  47.9 us
    pallas_call x1, Pallas kernels, on_device(): call(functools.partial(top_kernel, spans[0]), [block] + [quarter] * 4, [S...  2.99 us
  transfers between devices with their start and end apart: 49, of which 33 were waited for; matrix products, arithmetic and copies ran while one was open for 1% of the time, Pallas kernels for 12%

profile of v4, /device:TPU:0, one launch (start us, length us, event | category | flops | bytes accessed | tf_op | source)
XLA Modules:
  0.0 132.0 jit_solution(2722626375162144553)
XLA Ops:
  0.5 2.6 %collective-permute-start.1 = (f32[16,32,128]{2,1,0:T(8,128)}, f32[16,32,128]{2,1,0:T(8,128)S(1)}, u32[]{:S(2)}, u32[]{:S(2)}) collective-permute-start(f32[16,32,128]{2,1,0:T(8,128)} %bitcast.14), channel_id=1, source_target_pairs={{0,2},{1,3},{2,0},{3,1},{4,6},{5,7},{6,4},{7,5},{8,10},{9,11},{10,... | collective-permute-start | bytes 786440 | tf_op jit(solution)/shard_map/ppermute | solution.py:63
  3.0 2.3 %shard_map.48 = (f32[4,32,128]{2,1,0:T(8,128)}, f32[40,32,128]{2,1,0:T(8,128)}) custom-call(f32[4,4,32,128]{3,2,1,0:T(8,128)} %inverse_ref.1, f32[4,4,128,128]{3,2,1,0:T(8,128)} %all_sides_ref.1, f32[192,32,128]{2,1,0:T(8,128)} %bitcast.9), custom_call_target="tpu_custom_call" | custom-call | flops 1 | bytes 1 | tf_op jit(solution)/shard_map/pallas_call | solution.py:394
  5.4 2.7 %collective-permute-start.3 = (f32[4,32,128]{2,1,0:T(8,128)}, f32[4,32,128]{2,1,0:T(8,128)S(1)}, u32[]{:S(2)}, u32[]{:S(2)}) collective-permute-start(f32[4,32,128]{2,1,0:T(8,128)} %get-tuple-element.45), channel_id=1, source_target_pairs={{0,16},{4,20},{8,24},{12,28},{16,0},{20,4},{24,8},{28,12},{1,17},{... | collective-permute-start | bytes 196616 | tf_op jit(solution)/shard_map/ppermute | solution.py:63
  26.0 3.1 %collective-permute-done.9.refs_0_ = f32[4,32,128]{2,1,0:T(8,128)S(1)} collective-permute-done((f32[4,32,128]{2,1,0:T(8,128)S(1)}, f32[4,32,128]{2,1,0:T(8,128)S(1)}, u32[]{:S(2)}, u32[]{:S(2)}) %collective-permute-start.9) | collective-permute-done | bytes 65568 | tf_op jit(solution)/shard_map/ppermute | solution.py:63
  29.1 2.3 %collective-permute-start.10 = (f32[4,32,128]{2,1,0:T(8,128)S(1)}, f32[4,32,128]{2,1,0:T(8,128)S(1)}, u32[]{:S(2)}, u32[]{:S(2)}) collective-permute-start(f32[4,32,128]{2,1,0:T(8,128)S(1)} %fusion.1.refs_0_), channel_id=1, source_target_pairs={{0,16},{4,20},{8,24},{12,28},{16,0},{20,4},{24,8},{28,12},{1,17},{... | collective-permute-start | bytes 196616 | tf_op jit(solution)/shard_map/ppermute | solution.py:63
  40.8 2.5 %collective-permute-done.13.x3 = f32[8,32,128]{2,1,0:T(8,128)S(1)} collective-permute-done((f32[8,32,128]{2,1,0:T(8,128)S(1)}, f32[8,32,128]{2,1,0:T(8,128)S(1)}, u32[]{:S(2)}, u32[]{:S(2)}) %collective-permute-start.13) | collective-permute-done | bytes 131104 | tf_op jit(solution)/shard_map/ppermute | solution.py:63
  48.5 3.1 %collective-permute-done.16.u2.refs_0_ = f32[6,32,128]{2,1,0:T(8,128)S(1)} collective-permute-done((f32[6,32,128]{2,1,0:T(8,128)S(1)}, f32[6,32,128]{2,1,0:T(8,128)S(1)}, u32[]{:S(2)}, u32[]{:S(2)}) %collective-permute-start.16) | collective-permute-done | bytes 98336 | tf_op jit(solution)/shard_map/ppermute | solution.py:63
  54.0 2.3 %collective-permute-start.17 = (f32[4,32,128]{2,1,0:T(8,128)S(1)}, f32[4,32,128]{2,1,0:T(8,128)S(1)}, u32[]{:S(2)}, u32[]{:S(2)}) collective-permute-start(f32[4,32,128]{2,1,0:T(8,128)S(1)} %get-tuple-element.56.forward_ref), channel_id=1, source_target_pairs={{0,16},{4,20},{8,24},{12,28},{16,0},{20,4},{24,8},{28,12},{1,17},{... | collective-permute-start | bytes 196616 | tf_op jit(solution)/shard_map/ppermute | solution.py:63
  56.3 3.2 %collective-permute-done.17 = f32[4,32,128]{2,1,0:T(8,128)S(1)} collective-permute-done((f32[4,32,128]{2,1,0:T(8,128)S(1)}, f32[4,32,128]{2,1,0:T(8,128)S(1)}, u32[]{:S(2)}, u32[]{:S(2)}) %collective-permute-start.17) | collective-permute-done | bytes 65568 | tf_op jit(solution)/shard_map/ppermute | solution.py:63
  59.5 3.4 %collective-permute-start.18 = (f32[8,32,128]{2,1,0:T(8,128)S(1)}, f32[8,32,128]{2,1,0:T(8,128)S(1)}, u32[]{:S(2)}, u32[]{:S(2)}) collective-permute-start(f32[8,32,128]{2,1,0:T(8,128)S(1)} %constant_dynamic-update-slice_fusion.2.x0), channel_id=1, source_target_pairs={{0,4},{4,0},{8,12},{12,8},{16,20},{20,16},{24,28},{28,24},{1,5},{5... | collective-permute-start | bytes 393224 | tf_op jit(solution)/shard_map/ppermute | solution.py:63
  67.1 2.2 %collective-permute-done.19.x2 = f32[8,32,128]{2,1,0:T(8,128)S(1)} collective-permute-done((f32[8,32,128]{2,1,0:T(8,128)S(1)}, f32[8,32,128]{2,1,0:T(8,128)S(1)}, u32[]{:S(2)}, u32[]{:S(2)}) %collective-permute-start.19) | collective-permute-done | bytes 131104 | tf_op jit(solution)/shard_map/ppermute | solution.py:63
  71.2 3.0 %shard_map.58 = (f32[4,32,128]{2,1,0:T(8,128)S(1)}, f32[8,32,128]{2,1,0:T(8,128)S(1)}, f32[8,32,128]{2,1,0:T(8,128)S(1)}, f32[8,32,128]{2,1,0:T(8,128)S(1)}, f32[8,32,128]{2,1,0:T(8,128)S(1)}) custom-call(s32[64]{0:T(128)S(1)} %get-tuple-element.94.slot_ref, f32[8,32,128]{2,1,0:T(8,128)S(1)} %constant_dynamic-update-slice_fusion.2.x0, ...), custom_call_target="tpu_custom_call" | custom-call | flops 1 | bytes 1 | tf_op jit(solution)/shard_map/pallas_call | solution.py:477
  77.7 3.8 %collective-permute-done.27.refs_2_ = f32[8,32,128]{2,1,0:T(8,128)S(1)} collective-permute-done((f32[8,32,128]{2,1,0:T(8,128)S(1)}, f32[8,32,128]{2,1,0:T(8,128)S(1)}, u32[]{:S(2)}, u32[]{:S(2)}) %collective-permute-start.27) | collective-permute-done | bytes 131104 | tf_op jit(solution)/shard_map/ppermute | solution.py:63
  83.6 2.4 %collective-permute-start.28 = (f32[4,32,128]{2,1,0:T(8,128)S(1)}, f32[4,32,128]{2,1,0:T(8,128)S(1)}, u32[]{:S(2)}, u32[]{:S(2)}) collective-permute-start(f32[4,32,128]{2,1,0:T(8,128)S(1)} %get-tuple-element.92), channel_id=1, source_target_pairs={{0,16},{4,20},{8,24},{12,28},{16,0},{20,4},{24,8},{28,12},{1,17},{... | collective-permute-start | bytes 196616 | tf_op jit(solution)/shard_map/ppermute | solution.py:63
  86.8 3.4 %collective-permute-done.28.ret1 = f32[4,32,128]{2,1,0:T(8,128)S(1)} collective-permute-done((f32[4,32,128]{2,1,0:T(8,128)S(1)}, f32[4,32,128]{2,1,0:T(8,128)S(1)}, u32[]{:S(2)}, u32[]{:S(2)}) %collective-permute-start.28) | collective-permute-done | bytes 65568 | tf_op jit(solution)/shard_map/ppermute | solution.py:63
  90.3 2.1 %shard_map.63 = (f32[4,32,128]{2,1,0:T(8,128)S(1)}, f32[8,32,128]{2,1,0:T(8,128)S(1)}, f32[8,32,128]{2,1,0:T(8,128)S(1)}, f32[8,32,128]{2,1,0:T(8,128)S(1)}, f32[8,32,128]{2,1,0:T(8,128)S(1)}) custom-call(s32[64]{0:T(128)S(1)} %get-tuple-element.95.slot_ref, f32[4,32,128]{2,1,0:T(8,128)S(1)} %get-tuple-element.93.ret0, ...), custom_call_target="tpu_custom_call" | custom-call | flops 1 | bytes 1 | tf_op jit(solution)/shard_map/pallas_call | solution.py:488
  92.7 2.6 %collective-permute-start.33 = (f32[8,32,128]{2,1,0:T(8,128)S(1)}, f32[8,32,128]{2,1,0:T(8,128)S(1)}, u32[]{:S(2)}, u32[]{:S(2)}) collective-permute-start(f32[8,32,128]{2,1,0:T(8,128)S(1)} %get-tuple-element.63), channel_id=1, source_target_pairs={{0,8},{4,12},{8,0},{12,4},{16,24},{20,28},{24,16},{28,20},{1,9},{5... | collective-permute-start | bytes 393224 | tf_op jit(solution)/shard_map/ppermute | solution.py:63
  95.9 2.0 %collective-permute-done.37.value_ref = f32[32,32,128]{2,1,0:T(8,128)S(1)} collective-permute-done((f32[32,32,128]{2,1,0:T(8,128)S(1)}, f32[32,32,128]{2,1,0:T(8,128)S(1)}, u32[]{:S(2)}, u32[]{:S(2)}) %collective-permute-start.37) | collective-permute-done | bytes 524320 | tf_op jit(solution)/shard_map/ppermute | solution.py:63
  103.9 4.4 %collective-permute-done.35.ret1 = f32[4,32,128]{2,1,0:T(8,128)S(1)} collective-permute-done((f32[4,32,128]{2,1,0:T(8,128)S(1)}, f32[4,32,128]{2,1,0:T(8,128)S(1)}, u32[]{:S(2)}, u32[]{:S(2)}) %collective-permute-start.35) | collective-permute-done | bytes 65568 | tf_op jit(solution)/shard_map/ppermute | solution.py:63
  108.3 2.1 %shard_map.68 = (f32[4,32,128]{2,1,0:T(8,128)S(1)}, f32[8,32,128]{2,1,0:T(8,128)S(1)}, f32[8,32,128]{2,1,0:T(8,128)S(1)}, f32[8,32,128]{2,1,0:T(8,128)S(1)}, f32[8,32,128]{2,1,0:T(8,128)S(1)}) custom-call(s32[64]{0:T(128)S(1)} %get-tuple-element.96.slot_ref, f32[4,32,128]{2,1,0:T(8,128)S(1)} %get-tuple-element.91.ret0, ...), custom_call_target="tpu_custom_call" | custom-call | flops 1 | bytes 1 | tf_op jit(solution)/shard_map/pallas_call | solution.py:495
  110.5 2.7 %collective-permute-start.40 = (f32[8,32,128]{2,1,0:T(8,128)S(1)}, f32[8,32,128]{2,1,0:T(8,128)S(1)}, u32[]{:S(2)}, u32[]{:S(2)}) collective-permute-start(f32[8,32,128]{2,1,0:T(8,128)S(1)} %get-tuple-element.69), channel_id=1, source_target_pairs={{0,8},{4,12},{8,0},{12,4},{16,24},{20,28},{24,16},{28,20},{1,9},{5... | collective-permute-start | bytes 393224 | tf_op jit(solution)/shard_map/ppermute | solution.py:63
  114.0 3.8 %collective-permute-done.41.refs_5_ = f32[8,32,128]{2,1,0:T(8,128)S(1)} collective-permute-done((f32[8,32,128]{2,1,0:T(8,128)S(1)}, f32[8,32,128]{2,1,0:T(8,128)S(1)}, u32[]{:S(2)}, u32[]{:S(2)}) %collective-permute-start.41) | collective-permute-done | bytes 131104 | tf_op jit(solution)/shard_map/ppermute | solution.py:63
  122.2 3.4 %collective-permute-done.42.ret1 = f32[4,32,128]{2,1,0:T(8,128)S(1)} collective-permute-done((f32[4,32,128]{2,1,0:T(8,128)S(1)}, f32[4,32,128]{2,1,0:T(8,128)S(1)}, u32[]{:S(2)}, u32[]{:S(2)}) %collective-permute-start.42) | collective-permute-done | bytes 65568 | tf_op jit(solution)/shard_map/ppermute | solution.py:63
  128.4 1.9 %collective-permute-done.44.refs_2_ = f32[1,32,128]{2,1,0:T(8,128)S(1)} collective-permute-done((f32[1,32,128]{2,1,0:T(8,128)S(1)}, f32[1,32,128]{2,1,0:T(8,128)S(1)}, u32[]{:S(2)}, u32[]{:S(2)}) %collective-permute-start.44) | collective-permute-done | bytes 16416 | tf_op jit(solution)/shard_map/ppermute | solution.py:63
  (135 shorter events, 64.5 us)
Async XLA Ops:
  0.0 14.4 %collective-permute-start = (f32[16,32,128]{2,1,0:T(8,128)}, f32[16,32,128]{2,1,0:T(8,128)S(1)}, u32[]{:S(2)}, u32[]{:S(2)}) collective-permute-start(f32[16,32,128]{2,1,0:T(8,128)} %bitcast.13), channel_id=1, source_target_pairs={{0,1},{1,0},{2,3},{3,2},{4,5},{5,4},{6,7},{7,6},{8,9},{9,8},{10,11... | collective-permute-start | bytes 786440 | tf_op jit(solution)/shard_map/ppermute | solution.py:63
  0.5 9.7 %collective-permute-start.1 = (f32[16,32,128]{2,1,0:T(8,128)}, f32[16,32,128]{2,1,0:T(8,128)S(1)}, u32[]{:S(2)}, u32[]{:S(2)}) collective-permute-start(f32[16,32,128]{2,1,0:T(8,128)} %bitcast.14), channel_id=1, source_target_pairs={{0,2},{1,3},{2,0},{3,1},{4,6},{5,7},{6,4},{7,5},{8,10},{9,11},{10,... | collective-permute-start | bytes 786440 | tf_op jit(solution)/shard_map/ppermute | solution.py:63
  5.4 6.8 %collective-permute-start.3 = (f32[4,32,128]{2,1,0:T(8,128)}, f32[4,32,128]{2,1,0:T(8,128)S(1)}, u32[]{:S(2)}, u32[]{:S(2)}) collective-permute-start(f32[4,32,128]{2,1,0:T(8,128)} %get-tuple-element.45), channel_id=1, source_target_pairs={{0,16},{4,20},{8,24},{12,28},{16,0},{20,4},{24,8},{28,12},{1,17},{... | collective-permute-start | bytes 196616 | tf_op jit(solution)/shard_map/ppermute | solution.py:63
  8.1 16.7 %collective-permute-start.8 = (f32[40,32,128]{2,1,0:T(8,128)}, f32[40,32,128]{2,1,0:T(8,128)S(1)}, u32[]{:S(2)}, u32[]{:S(2)}) collective-permute-start(f32[40,32,128]{2,1,0:T(8,128)} %get-tuple-element.50.refs_0_), channel_id=1, source_target_pairs={{0,2},{1,3},{2,0},{3,1},{4,6},{5,7},{6,4},{7,5},{8,10},{9,11},{10,... | collective-permute-start | bytes 1966088 | tf_op jit(solution)/shard_map/ppermute | solution.py:63
  12.2 6.6 %collective-permute-start.4 = (f32[8,32,128]{2,1,0:T(8,128)S(1)}, f32[8,32,128]{2,1,0:T(8,128)S(1)}, u32[]{:S(2)}, u32[]{:S(2)}) collective-permute-start(f32[8,32,128]{2,1,0:T(8,128)S(1)} %constant_dynamic-update-slice_fusion.x0), channel_id=1, source_target_pairs={{0,4},{4,0},{8,12},{12,8},{16,20},{20,16},{24,28},{28,24},{1,5},{5... | collective-permute-start | bytes 393224 | tf_op jit(solution)/shard_map/ppermute | solution.py:63
  14.4 7.1 %collective-permute-start.6 = (f32[8,32,128]{2,1,0:T(8,128)S(1)}, f32[8,32,128]{2,1,0:T(8,128)S(1)}, u32[]{:S(2)}, u32[]{:S(2)}) collective-permute-start(f32[8,32,128]{2,1,0:T(8,128)S(1)} %constant_dynamic-update-slice_fusion.x0), channel_id=1, source_target_pairs={{0,12},{4,8},{8,4},{12,0},{16,28},{20,24},{24,20},{28,16},{1,13},{... | collective-permute-start | bytes 393224 | tf_op jit(solution)/shard_map/ppermute | solution.py:63
  31.6 15.3 %collective-permute-start.15 = (f32[40,32,128]{2,1,0:T(8,128)S(1)}, f32[40,32,128]{2,1,0:T(8,128)S(1)}, u32[]{:S(2)}, u32[]{:S(2)}) collective-permute-start(f32[40,32,128]{2,1,0:T(8,128)S(1)} %shard_map.53.refs_0_), channel_id=1, source_target_pairs={{0,2},{1,3},{2,0},{3,1},{4,6},{5,7},{6,4},{7,5},{8,10},{9,11},{10,... | collective-permute-start | bytes 1966088 | tf_op jit(solution)/shard_map/ppermute | solution.py:63
  51.7 31.4 %collective-permute-start.30 = (f32[80,32,128]{2,1,0:T(8,128)S(1)}, f32[80,32,128]{2,1,0:T(8,128)S(1)}, u32[]{:S(2)}, u32[]{:S(2)}) collective-permute-start(f32[80,32,128]{2,1,0:T(8,128)S(1)} %shard_map.60.refs_0_), channel_id=1, source_target_pairs={{0,2},{1,3},{2,0},{3,1},{4,6},{5,7},{6,4},{7,5},{8,10},{9,11},{10,... | collective-permute-start | bytes 3932168 | tf_op jit(solution)/shard_map/ppermute | solution.py:63
  53.3 9.7 %collective-permute-start.22 = (f32[40,32,128]{2,1,0:T(8,128)S(1)}, f32[40,32,128]{2,1,0:T(8,128)S(1)}, u32[]{:S(2)}, u32[]{:S(2)}) collective-permute-start(f32[40,32,128]{2,1,0:T(8,128)S(1)} %collective-permute-done.8.refs_0_.refs_2_), channel_id=1, source_target_pairs={{0,1},{1,0},{2,3},{3,2},{4,5},{5,4},{6,7},{7,6},{8,9},{9,8},{10,11... | collective-permute-start | bytes 1966088 | tf_op jit(solution)/shard_map/ppermute | solution.py:63
  53.8 9.6 %collective-permute-start.23 = (f32[40,32,128]{2,1,0:T(8,128)S(1)}, f32[40,32,128]{2,1,0:T(8,128)S(1)}, u32[]{:S(2)}, u32[]{:S(2)}) collective-permute-start(f32[40,32,128]{2,1,0:T(8,128)S(1)} %shard_map.53.refs_0_), channel_id=1, source_target_pairs={{0,1},{1,0},{2,3},{3,2},{4,5},{5,4},{6,7},{7,6},{8,9},{9,8},{10,11... | collective-permute-start | bytes 1966088 | tf_op jit(solution)/shard_map/ppermute | solution.py:63
  59.5 7.6 %collective-permute-start.18 = (f32[8,32,128]{2,1,0:T(8,128)S(1)}, f32[8,32,128]{2,1,0:T(8,128)S(1)}, u32[]{:S(2)}, u32[]{:S(2)}) collective-permute-start(f32[8,32,128]{2,1,0:T(8,128)S(1)} %constant_dynamic-update-slice_fusion.2.x0), channel_id=1, source_target_pairs={{0,4},{4,0},{8,12},{12,8},{16,20},{20,16},{24,28},{28,24},{1,5},{5... | collective-permute-start | bytes 393224 | tf_op jit(solution)/shard_map/ppermute | solution.py:63
  63.4 7.8 %collective-permute-start.20 = (f32[8,32,128]{2,1,0:T(8,128)S(1)}, f32[8,32,128]{2,1,0:T(8,128)S(1)}, u32[]{:S(2)}, u32[]{:S(2)}) collective-permute-start(f32[8,32,128]{2,1,0:T(8,128)S(1)} %constant_dynamic-update-slice_fusion.2.x0), channel_id=1, source_target_pairs={{0,12},{4,8},{8,4},{12,0},{16,28},{20,24},{24,20},{28,16},{1,13},{... | collective-permute-start | bytes 393224 | tf_op jit(solution)/shard_map/ppermute | solution.py:63
  74.2 7.4 %collective-permute-start.27 = (f32[8,32,128]{2,1,0:T(8,128)S(1)}, f32[8,32,128]{2,1,0:T(8,128)S(1)}, u32[]{:S(2)}, u32[]{:S(2)}) collective-permute-start(f32[8,32,128]{2,1,0:T(8,128)S(1)} %get-tuple-element.60), channel_id=1, source_target_pairs={{0,12},{4,8},{8,4},{12,0},{16,28},{20,24},{24,20},{28,16},{1,13},{... | collective-permute-start | bytes 393224 | tf_op jit(solution)/shard_map/ppermute | solution.py:63
  75.8 7.2 %collective-permute-start.26 = (f32[8,32,128]{2,1,0:T(8,128)S(1)}, f32[8,32,128]{2,1,0:T(8,128)S(1)}, u32[]{:S(2)}, u32[]{:S(2)}) collective-permute-start(f32[8,32,128]{2,1,0:T(8,128)S(1)} %get-tuple-element.59), channel_id=1, source_target_pairs={{0,8},{4,12},{8,0},{12,4},{16,24},{20,28},{24,16},{28,20},{1,9},{5... | collective-permute-start | bytes 393224 | tf_op jit(solution)/shard_map/ppermute | solution.py:63
  77.7 8.6 %collective-permute-start.29 = (f32[80,32,128]{2,1,0:T(8,128)S(1)}, f32[80,32,128]{2,1,0:T(8,128)S(1)}, u32[]{:S(2)}, u32[]{:S(2)}) collective-permute-start(f32[80,32,128]{2,1,0:T(8,128)S(1)} %shard_map.60.refs_0_), channel_id=1, source_target_pairs={{0,1},{1,0},{2,3},{3,2},{4,5},{5,4},{6,7},{7,6},{8,9},{9,8},{10,11... | collective-permute-start | bytes 3932168 | tf_op jit(solution)/shard_map/ppermute | solution.py:63
  83.5 14.4 %collective-permute-start.37 = (f32[32,32,128]{2,1,0:T(8,128)S(1)}, f32[32,32,128]{2,1,0:T(8,128)S(1)}, u32[]{:S(2)}, u32[]{:S(2)}) collective-permute-start(f32[32,32,128]{2,1,0:T(8,128)S(1)} %shard_map.65.refs_0_), channel_id=1, source_target_pairs={{0,2},{1,3},{2,0},{3,1},{4,6},{5,7},{6,4},{7,5},{8,10},{9,11},{10,... | collective-permute-start | bytes 1572872 | tf_op jit(solution)/shard_map/ppermute | solution.py:63
  83.6 6.6 %collective-permute-start.28 = (f32[4,32,128]{2,1,0:T(8,128)S(1)}, f32[4,32,128]{2,1,0:T(8,128)S(1)}, u32[]{:S(2)}, u32[]{:S(2)}) collective-permute-start(f32[4,32,128]{2,1,0:T(8,128)S(1)} %get-tuple-element.92), channel_id=1, source_target_pairs={{0,16},{4,20},{8,24},{12,28},{16,0},{20,4},{24,8},{28,12},{1,17},{... | collective-permute-start | bytes 196616 | tf_op jit(solution)/shard_map/ppermute | solution.py:63
  92.3 7.3 %collective-permute-start.34 = (f32[8,32,128]{2,1,0:T(8,128)S(1)}, f32[8,32,128]{2,1,0:T(8,128)S(1)}, u32[]{:S(2)}, u32[]{:S(2)}) collective-permute-start(f32[8,32,128]{2,1,0:T(8,128)S(1)} %get-tuple-element.64), channel_id=1, source_target_pairs={{0,12},{4,8},{8,4},{12,0},{16,28},{20,24},{24,20},{28,16},{1,13},{... | collective-permute-start | bytes 393224 | tf_op jit(solution)/shard_map/ppermute | solution.py:63
  92.7 8.8 %collective-permute-start.33 = (f32[8,32,128]{2,1,0:T(8,128)S(1)}, f32[8,32,128]{2,1,0:T(8,128)S(1)}, u32[]{:S(2)}, u32[]{:S(2)}) collective-permute-start(f32[8,32,128]{2,1,0:T(8,128)S(1)} %get-tuple-element.63), channel_id=1, source_target_pairs={{0,8},{4,12},{8,0},{12,4},{16,24},{20,28},{24,16},{28,20},{1,9},{5... | collective-permute-start | bytes 393224 | tf_op jit(solution)/shard_map/ppermute | solution.py:63
  95.9 7.3 %collective-permute-start.36 = (f32[32,32,128]{2,1,0:T(8,128)S(1)}, f32[32,32,128]{2,1,0:T(8,128)S(1)}, u32[]{:S(2)}, u32[]{:S(2)}) collective-permute-start(f32[32,32,128]{2,1,0:T(8,128)S(1)} %shard_map.65.refs_0_), channel_id=1, source_target_pairs={{0,1},{1,0},{2,3},{3,2},{4,5},{5,4},{6,7},{7,6},{8,9},{9,8},{10,11... | collective-permute-start | bytes 1572872 | tf_op jit(solution)/shard_map/ppermute | solution.py:63
  110.4 7.3 %collective-permute-start.41 = (f32[8,32,128]{2,1,0:T(8,128)S(1)}, f32[8,32,128]{2,1,0:T(8,128)S(1)}, u32[]{:S(2)}, u32[]{:S(2)}) collective-permute-start(f32[8,32,128]{2,1,0:T(8,128)S(1)} %get-tuple-element.70), channel_id=1, source_target_pairs={{0,12},{4,8},{8,4},{12,0},{16,28},{20,24},{24,20},{28,16},{1,13},{... | collective-permute-start | bytes 393224 | tf_op jit(solution)/shard_map/ppermute | solution.py:63
  110.5 9.0 %collective-permute-start.40 = (f32[8,32,128]{2,1,0:T(8,128)S(1)}, f32[8,32,128]{2,1,0:T(8,128)S(1)}, u32[]{:S(2)}, u32[]{:S(2)}) collective-permute-start(f32[8,32,128]{2,1,0:T(8,128)S(1)} %get-tuple-element.69), channel_id=1, source_target_pairs={{0,8},{4,12},{8,0},{12,4},{16,24},{20,28},{24,16},{28,20},{1,9},{5... | collective-permute-start | bytes 393224 | tf_op jit(solution)/shard_map/ppermute | solution.py:63
  120.2 7.7 %collective-permute-start.46 = (f32[3,32,128]{2,1,0:T(8,128)S(1)}, f32[3,32,128]{2,1,0:T(8,128)S(1)}, u32[]{:S(2)}, u32[]{:S(2)}) collective-permute-start(f32[3,32,128]{2,1,0:T(8,128)S(1)} %get-tuple-element.78), channel_id=1, source_target_pairs={{0,1},{1,0},{2,3},{3,2},{4,5},{5,4},{6,7},{7,6},{8,9},{9,8},{10,11... | collective-permute-start | bytes 147464 | tf_op jit(solution)/shard_map/ppermute | solution.py:63
  120.3 8.1 %collective-permute-start.47 = (f32[3,32,128]{2,1,0:T(8,128)S(1)}, f32[3,32,128]{2,1,0:T(8,128)S(1)}, u32[]{:S(2)}, u32[]{:S(2)}) collective-permute-start(f32[3,32,128]{2,1,0:T(8,128)S(1)} %get-tuple-element.79), channel_id=1, source_target_pairs={{0,2},{1,3},{2,0},{3,1},{4,6},{5,7},{6,4},{7,5},{8,10},{9,11},{10,... | collective-permute-start | bytes 147464 | tf_op jit(solution)/shard_map/ppermute | solution.py:63
  (30 other events, 163.6 us)

commit v5 on v4

--- a/solution.py
+++ b/solution.py
@@ -295,27 +295,41 @@
     cut(col_ref, refs[:some], refs[-5:-1], refs[-1])
 
 
-def last_kernel(col_ref, ret0, ret1, sides_ref, inverse_ref, *refs):
+def ahead_kernel(ret_ref, sides_ref, inverse_ref, out_ref):
+    for j in range(out_ref.shape[0]):
+        out_ref[j] = times(times_turned(sides_ref[j], inverse_ref[j]) - ret_ref[j], inverse_ref[j])
+
+
+def last_kernel(col_ref, ret_ref, ahead_ref, inverse_ref, *refs):
     outs, (solved, packed) = refs[:-2], refs[-2:]
-    for j in range(sides_ref.shape[0]):
-        rest = times_turned(sides_ref[j], inverse_ref[j]) - (ret0[j] + ret1[j])
-        solved[j] = times(rest, inverse_ref[j])
+    for j in range(ahead_ref.shape[0]):
+        solved[j] = ahead_ref[j] - times(ret_ref[j], inverse_ref[j])
     cut(col_ref, [solved], outs, packed)
 
 
+def place(col_ref, parts, whole, outs):
+    some, piece, columns = parts[0].shape
+    for mask, part in enumerate(parts):
+        start = pl.multiple_of((col_ref[0] ^ mask) * piece, piece)
+        for level in range(some):
+            whole[level, pl.ds(start, piece), :] = part[level]
+    for level in range(some):
+        outs[level] = whole[level].T.reshape(outs.shape[1:])
+
+
+def upper_kernel(col_ref, *refs):
+    place(col_ref, refs[:4], refs[5], refs[4])
+
+
 def out_kernel(col_ref, *refs):
-    parts, (out_ref, whole) = refs[:-2], refs[-2:]
-    levels, count, share, columns = out_ref.shape
-    place = 0
-    for group in (parts[:4], parts[4:]):
-        some, piece, _ = group[0].shape
-        for mask, part in enumerate(group):
-            start = pl.multiple_of((col_ref[0] ^ mask) * piece, piece)
-            for level in range(some):
-                whole[place + level, pl.ds(start, piece), :] = part[level]
-        place += some
-    for level in range(levels):
-        out_ref[level] = whole[level].T.reshape(count, share, columns)
+    parts, (upper_ref, out_ref, whole, lowest, sems) = refs[:4], refs[4:]
+    above = pltpu.make_async_copy(upper_ref, out_ref.at[pl.ds(1, upper_ref.shape[0])], sems.at[0])
+    above.start()
+    place(col_ref, parts, whole, lowest)
+    below = pltpu.make_async_copy(lowest, out_ref.at[pl.ds(0, 1)], sems.at[1])
+    below.start()
+    above.wait()
+    below.wait()
 
 
 def same_kernel(value_ref, *refs):
@@ -403,7 +417,7 @@
     early = near(early) + (swap(early, "col", 2),)
     _, gathered = gather_row(first)
     all_inverse = inverse_diag.reshape(levels * count, share, width)
-    parts_inverse = near(all_inverse) + near(swap(all_inverse, "col", 2))
+    parts_inverse = (all_inverse, swap(after(all_inverse, first), "col", 1)) + near(swap(all_inverse, "col", 2))
 
     inverse, token = call(
         join_inverse_kernel, [like(levels * count, width, 2 * width, dtype=BF16), like(8, width)], [SMEM] + [VMEM] * cols
@@ -505,17 +519,31 @@
         [SMEM] + [VMEM] * (top + len(got)),
         scratch=[pltpu.VMEM((cols, top, mine, count * share), F32)],
     )(col, *solved[1:], *got)
+    ahead = call(ahead_kernel, block, [VMEM] * 3)(returned[0], sides[0], inverse[0])
     lowest = call(
-        last_kernel, [like(1, mine, count * share)] * cols, [SMEM] + [VMEM] * 4,
+        last_kernel, [like(1, mine, count * share)] * cols, [SMEM] + [VMEM] * 3,
         scratch=[
             pltpu.VMEM((count, mine, width), F32),
             pltpu.VMEM((cols, 1, mine, count * share), F32),
         ],
-    )(col, *returned, sides[0], inverse[0])
-    return call(
-        out_kernel, like(levels, count, share, columns), [SMEM] + [VMEM] * (2 * cols),
-        scratch=[pltpu.VMEM((levels, columns, count * share), F32)],
-    )(col, *spread(lowest), *spread(upper))
+    )(col, returned[1], ahead, inverse[0])
+    upper = call(
+        upper_kernel, like(top, count, share, columns), [SMEM] + [VMEM] * cols,
+        scratch=[pltpu.VMEM((top, columns, count * share), F32)],
+    )(col, *spread(upper))
+    return pl.pallas_call(
+        out_kernel,
+        out_shape=like(levels, count, share, columns),
+        in_specs=[SMEM] + [VMEM] * (cols + 1),
+        out_specs=HBM,
+        scratch_shapes=[
+            pltpu.VMEM((1, columns, count * share), F32),
+            pltpu.VMEM((1, count, share, columns), F32),
+            pltpu.SemaphoreType.DMA((2,)),
+        ],
+        compiler_params=pltpu.CompilerParams(vmem_limit_bytes=24 * 1024 * 1024),
+        cost_estimate=TINY,
+    )(col, *spread(lowest), upper)
 
 
 def solution(mesh):

time: 132 us -> 131 us (level)
  starting transfers between devices: 47.9 us -> 39.5 us
  waiting for transfers between devices: 61.7 us -> 68.7 us
    ppermute x49, starting transfers between devices: 47.9 us -> 39.5 us  [swap(): return lax.ppermute(value, axis, [(i, i ^ mask) for i in range(size)])]
    ppermute x49, waiting for transfers between devices: 61.7 us -> 68.7 us  [swap(): return lax.ppermute(value, axis, [(i, i ^ mask) for i in range(size)])]
  transfers between devices with their start and end apart: 49 -> 49, of which waited for: 33 -> 33; matrix products, arithmetic and copies ran while one was open for 1% -> 0% of each run, Pallas kernels for 12% -> 13%
where the time goes in v5:
time: 131 us
  waiting for transfers between devices  68.7 us (52%)
  starting transfers between devices  39.5 us (30%)
  Pallas kernels  19.7 us (15%)
  local copies, waits for them, and re-layouts  2.42 us (2%)
    ppermute x49, waiting for transfers between devices, swap(): return lax.ppermute(value, axis, [(i, i ^ mask) for i in range(size)])  68.7 us
    ppermute x49, starting transfers between devices, swap(): return lax.ppermute(value, axis, [(i, i ^ mask) for i in range(size)])  39.5 us
    pallas_call x1, Pallas kernels, on_device(): call(functools.partial(top_kernel, spans[0]), [block] + [quarter] * 4, [S...  3.02 us
  transfers between devices with their start and end apart: 49, of which 33 were waited for; matrix products, arithmetic and copies ran while one was open for 0% of the time, Pallas kernels for 13%

profile of v5, /device:TPU:0, one launch (start us, length us, event | category | flops | bytes accessed | tf_op | source)
XLA Modules:
  0.0 131.1 jit_solution(5403309618931613322)
XLA Ops:
  0.0 3.0 %collective-permute-start.1 = (f32[16,32,128]{2,1,0:T(8,128)}, f32[16,32,128]{2,1,0:T(8,128)S(1)}, u32[]{:S(2)}, u32[]{:S(2)}) collective-permute-start(f32[16,32,128]{2,1,0:T(8,128)} %bitcast.13), channel_id=1, source_target_pairs={{0,2},{1,3},{2,0},{3,1},{4,6},{5,7},{6,4},{7,5},{8,10},{9,11},{10,... | collective-permute-start | bytes 786440 | tf_op jit(solution)/shard_map/ppermute | solution.py:63
  3.0 2.3 %shard_map.46 = (f32[4,32,128]{2,1,0:T(8,128)}, f32[40,32,128]{2,1,0:T(8,128)}) custom-call(f32[4,4,32,128]{3,2,1,0:T(8,128)} %own_inverse_ref.1, f32[4,4,128,128]{3,2,1,0:T(8,128)} %all_sides_ref.1, f32[192,32,128]{2,1,0:T(8,128)} %bitcast.9), custom_call_target="tpu_custom_call" | custom-call | flops 1 | bytes 1 | tf_op jit(solution)/shard_map/pallas_call | solution.py:408
  5.3 2.7 %collective-permute-start.3 = (f32[4,32,128]{2,1,0:T(8,128)}, f32[4,32,128]{2,1,0:T(8,128)S(1)}, u32[]{:S(2)}, u32[]{:S(2)}) collective-permute-start(f32[4,32,128]{2,1,0:T(8,128)} %get-tuple-element.43.refs_0_), channel_id=1, source_target_pairs={{0,16},{4,20},{8,24},{12,28},{16,0},{20,4},{24,8},{28,12},{1,17},{... | collective-permute-start | bytes 196616 | tf_op jit(solution)/shard_map/ppermute | solution.py:63
  22.8 3.5 %collective-permute-done.8.refs_0_.refs_2_ = f32[40,32,128]{2,1,0:T(8,128)S(1)} collective-permute-done((f32[40,32,128]{2,1,0:T(8,128)}, f32[40,32,128]{2,1,0:T(8,128)S(1)}, u32[]{:S(2)}, u32[]{:S(2)}) %collective-permute-start.8) | collective-permute-done | bytes 655392 | tf_op jit(solution)/shard_map/ppermute | solution.py:63
  26.8 3.8 %collective-permute-done.9.refs_0_ = f32[4,32,128]{2,1,0:T(8,128)S(1)} collective-permute-done((f32[4,32,128]{2,1,0:T(8,128)S(1)}, f32[4,32,128]{2,1,0:T(8,128)S(1)}, u32[]{:S(2)}, u32[]{:S(2)}) %collective-permute-start.9) | collective-permute-done | bytes 65568 | tf_op jit(solution)/shard_map/ppermute | solution.py:63
  32.5 3.3 %collective-permute-done.10.after_ref = f32[4,32,128]{2,1,0:T(8,128)S(1)} collective-permute-done((f32[4,32,128]{2,1,0:T(8,128)S(1)}, f32[4,32,128]{2,1,0:T(8,128)S(1)}, u32[]{:S(2)}, u32[]{:S(2)}) %collective-permute-start.10) | collective-permute-done | bytes 65568 | tf_op jit(solution)/shard_map/ppermute | solution.py:63
  37.4 2.1 %collective-permute-start.12 = (f32[8,32,128]{2,1,0:T(8,128)S(1)}, f32[8,32,128]{2,1,0:T(8,128)S(1)}, u32[]{:S(2)}, u32[]{:S(2)}) collective-permute-start(f32[8,32,128]{2,1,0:T(8,128)S(1)} %pad_maximum_fusion.x0), channel_id=1, source_target_pairs={{0,8},{4,12},{8,0},{12,4},{16,24},{20,28},{24,16},{28,20},{1,9},{5... | collective-permute-start | bytes 393224 | tf_op jit(solution)/shard_map/ppermute | solution.py:63
  42.5 2.9 %collective-permute-done.13.x3 = f32[8,32,128]{2,1,0:T(8,128)S(1)} collective-permute-done((f32[8,32,128]{2,1,0:T(8,128)S(1)}, f32[8,32,128]{2,1,0:T(8,128)S(1)}, u32[]{:S(2)}, u32[]{:S(2)}) %collective-permute-start.13) | collective-permute-done | bytes 131104 | tf_op jit(solution)/shard_map/ppermute | solution.py:63
  48.2 4.8 %collective-permute-done.16.u2.refs_0_ = f32[6,32,128]{2,1,0:T(8,128)S(1)} collective-permute-done((f32[6,32,128]{2,1,0:T(8,128)S(1)}, f32[6,32,128]{2,1,0:T(8,128)S(1)}, u32[]{:S(2)}, u32[]{:S(2)}) %collective-permute-start.16) | collective-permute-done | bytes 98336 | tf_op jit(solution)/shard_map/ppermute | solution.py:63
  55.6 5.1 %collective-permute-done.17 = f32[4,32,128]{2,1,0:T(8,128)S(1)} collective-permute-done((f32[4,32,128]{2,1,0:T(8,128)S(1)}, f32[4,32,128]{2,1,0:T(8,128)S(1)}, u32[]{:S(2)}, u32[]{:S(2)}) %collective-permute-start.17) | collective-permute-done | bytes 65568 | tf_op jit(solution)/shard_map/ppermute | solution.py:63
  61.9 2.5 %collective-permute-start.20 = (f32[8,32,128]{2,1,0:T(8,128)S(1)}, f32[8,32,128]{2,1,0:T(8,128)S(1)}, u32[]{:S(2)}, u32[]{:S(2)}) collective-permute-start(f32[8,32,128]{2,1,0:T(8,128)S(1)} %constant_dynamic-update-slice_fusion.2.x0), channel_id=1, source_target_pairs={{0,12},{4,8},{8,4},{12,0},{16,28},{20,24},{24,20},{28,16},{1,13},{... | collective-permute-start | bytes 393224 | tf_op jit(solution)/shard_map/ppermute | solution.py:63
  67.8 2.9 %collective-permute-done.20.x3 = f32[8,32,128]{2,1,0:T(8,128)S(1)} collective-permute-done((f32[8,32,128]{2,1,0:T(8,128)S(1)}, f32[8,32,128]{2,1,0:T(8,128)S(1)}, u32[]{:S(2)}, u32[]{:S(2)}) %collective-permute-start.20) | collective-permute-done | bytes 131104 | tf_op jit(solution)/shard_map/ppermute | solution.py:63
  70.7 3.0 %shard_map.59 = (f32[4,32,128]{2,1,0:T(8,128)S(1)}, f32[8,32,128]{2,1,0:T(8,128)S(1)}, f32[8,32,128]{2,1,0:T(8,128)S(1)}, f32[8,32,128]{2,1,0:T(8,128)S(1)}, f32[8,32,128]{2,1,0:T(8,128)S(1)}) custom-call(s32[64]{0:T(128)S(1)} %get-tuple-element.94.slot_ref, f32[8,32,128]{2,1,0:T(8,128)S(1)} %constant_dynamic-update-slice_fusion.2.x0, ...), custom_call_target="tpu_custom_call" | custom-call | flops 1 | bytes 1 | tf_op jit(solution)/shard_map/pallas_call | solution.py:491
  77.3 3.6 %collective-permute-done.27.refs_2_ = f32[8,32,128]{2,1,0:T(8,128)S(1)} collective-permute-done((f32[8,32,128]{2,1,0:T(8,128)S(1)}, f32[8,32,128]{2,1,0:T(8,128)S(1)}, u32[]{:S(2)}, u32[]{:S(2)}) %collective-permute-start.27) | collective-permute-done | bytes 131104 | tf_op jit(solution)/shard_map/ppermute | solution.py:63
  86.9 4.0 %collective-permute-done.28.ret1 = f32[4,32,128]{2,1,0:T(8,128)S(1)} collective-permute-done((f32[4,32,128]{2,1,0:T(8,128)S(1)}, f32[4,32,128]{2,1,0:T(8,128)S(1)}, u32[]{:S(2)}, u32[]{:S(2)}) %collective-permute-start.28) | collective-permute-done | bytes 65568 | tf_op jit(solution)/shard_map/ppermute | solution.py:63
  90.9 2.1 %shard_map.64 = (f32[4,32,128]{2,1,0:T(8,128)S(1)}, f32[8,32,128]{2,1,0:T(8,128)S(1)}, f32[8,32,128]{2,1,0:T(8,128)S(1)}, f32[8,32,128]{2,1,0:T(8,128)S(1)}, f32[8,32,128]{2,1,0:T(8,128)S(1)}) custom-call(s32[64]{0:T(128)S(1)} %get-tuple-element.95.slot_ref, f32[4,32,128]{2,1,0:T(8,128)S(1)} %get-tuple-element.93.ret0, ...), custom_call_target="tpu_custom_call" | custom-call | flops 1 | bytes 1 | tf_op jit(solution)/shard_map/pallas_call | solution.py:502
  93.1 2.1 %collective-permute-start.33 = (f32[8,32,128]{2,1,0:T(8,128)S(1)}, f32[8,32,128]{2,1,0:T(8,128)S(1)}, u32[]{:S(2)}, u32[]{:S(2)}) collective-permute-start(f32[8,32,128]{2,1,0:T(8,128)S(1)} %get-tuple-element.63), channel_id=1, source_target_pairs={{0,8},{4,12},{8,0},{12,4},{16,24},{20,28},{24,16},{28,20},{1,9},{5... | collective-permute-start | bytes 393224 | tf_op jit(solution)/shard_map/ppermute | solution.py:63
  98.0 2.4 %collective-permute-done.34.refs_2_ = f32[8,32,128]{2,1,0:T(8,128)S(1)} collective-permute-done((f32[8,32,128]{2,1,0:T(8,128)S(1)}, f32[8,32,128]{2,1,0:T(8,128)S(1)}, u32[]{:S(2)}, u32[]{:S(2)}) %collective-permute-start.34) | collective-permute-done | bytes 131104 | tf_op jit(solution)/shard_map/ppermute | solution.py:63
  104.5 4.1 %collective-permute-done.35.ret1 = f32[4,32,128]{2,1,0:T(8,128)S(1)} collective-permute-done((f32[4,32,128]{2,1,0:T(8,128)S(1)}, f32[4,32,128]{2,1,0:T(8,128)S(1)}, u32[]{:S(2)}, u32[]{:S(2)}) %collective-permute-start.35) | collective-permute-done | bytes 65568 | tf_op jit(solution)/shard_map/ppermute | solution.py:63
  108.6 2.1 %shard_map.69 = (f32[4,32,128]{2,1,0:T(8,128)S(1)}, f32[8,32,128]{2,1,0:T(8,128)S(1)}, f32[8,32,128]{2,1,0:T(8,128)S(1)}, f32[8,32,128]{2,1,0:T(8,128)S(1)}, f32[8,32,128]{2,1,0:T(8,128)S(1)}) custom-call(s32[64]{0:T(128)S(1)} %get-tuple-element.96.slot_ref, f32[4,32,128]{2,1,0:T(8,128)S(1)} %get-tuple-element.91.ret0, ...), custom_call_target="tpu_custom_call" | custom-call | flops 1 | bytes 1 | tf_op jit(solution)/shard_map/pallas_call | solution.py:509
  110.8 2.6 %collective-permute-start.40 = (f32[8,32,128]{2,1,0:T(8,128)S(1)}, f32[8,32,128]{2,1,0:T(8,128)S(1)}, u32[]{:S(2)}, u32[]{:S(2)}) collective-permute-start(f32[8,32,128]{2,1,0:T(8,128)S(1)} %get-tuple-element.69), channel_id=1, source_target_pairs={{0,8},{4,12},{8,0},{12,4},{16,24},{20,28},{24,16},{28,20},{1,9},{5... | collective-permute-start | bytes 393224 | tf_op jit(solution)/shard_map/ppermute | solution.py:63
  114.2 3.8 %collective-permute-done.41.refs_5_ = f32[8,32,128]{2,1,0:T(8,128)S(1)} collective-permute-done((f32[8,32,128]{2,1,0:T(8,128)S(1)}, f32[8,32,128]{2,1,0:T(8,128)S(1)}, u32[]{:S(2)}, u32[]{:S(2)}) %collective-permute-start.41) | collective-permute-done | bytes 131104 | tf_op jit(solution)/shard_map/ppermute | solution.py:63
  123.2 2.8 %collective-permute-done.42.ret_ref = f32[4,32,128]{2,1,0:T(8,128)S(1)} collective-permute-done((f32[4,32,128]{2,1,0:T(8,128)S(1)}, f32[4,32,128]{2,1,0:T(8,128)S(1)}, u32[]{:S(2)}, u32[]{:S(2)}) %collective-permute-start.42) | collective-permute-done | bytes 65568 | tf_op jit(solution)/shard_map/ppermute | solution.py:63
  128.4 1.8 %collective-permute-done.44.refs_2_ = f32[1,32,128]{2,1,0:T(8,128)S(1)} collective-permute-done((f32[1,32,128]{2,1,0:T(8,128)S(1)}, f32[1,32,128]{2,1,0:T(8,128)S(1)}, u32[]{:S(2)}, u32[]{:S(2)}) %collective-permute-start.44) | collective-permute-done | bytes 16416 | tf_op jit(solution)/shard_map/ppermute | solution.py:63
  (140 shorter events, 57.4 us)
Async XLA Ops:
  0.0 9.8 %collective-permute-start.1 = (f32[16,32,128]{2,1,0:T(8,128)}, f32[16,32,128]{2,1,0:T(8,128)S(1)}, u32[]{:S(2)}, u32[]{:S(2)}) collective-permute-start(f32[16,32,128]{2,1,0:T(8,128)} %bitcast.13), channel_id=1, source_target_pairs={{0,2},{1,3},{2,0},{3,1},{4,6},{5,7},{6,4},{7,5},{8,10},{9,11},{10,... | collective-permute-start | bytes 786440 | tf_op jit(solution)/shard_map/ppermute | solution.py:63
  8.9 17.4 %collective-permute-start.8 = (f32[40,32,128]{2,1,0:T(8,128)}, f32[40,32,128]{2,1,0:T(8,128)S(1)}, u32[]{:S(2)}, u32[]{:S(2)}) collective-permute-start(f32[40,32,128]{2,1,0:T(8,128)} %get-tuple-element.50.refs_0_), channel_id=1, source_target_pairs={{0,2},{1,3},{2,0},{3,1},{4,6},{5,7},{6,4},{7,5},{8,10},{9,11},{10,... | collective-permute-start | bytes 1966088 | tf_op jit(solution)/shard_map/ppermute | solution.py:63
  11.1 6.6 %collective-permute-start.4 = (f32[8,32,128]{2,1,0:T(8,128)S(1)}, f32[8,32,128]{2,1,0:T(8,128)S(1)}, u32[]{:S(2)}, u32[]{:S(2)}) collective-permute-start(f32[8,32,128]{2,1,0:T(8,128)S(1)} %constant_dynamic-update-slice_fusion.x0), channel_id=1, source_target_pairs={{0,4},{4,0},{8,12},{12,8},{16,20},{20,16},{24,28},{28,24},{1,5},{5... | collective-permute-start | bytes 393224 | tf_op jit(solution)/shard_map/ppermute | solution.py:63
  31.2 16.8 %collective-permute-start.15 = (f32[40,32,128]{2,1,0:T(8,128)S(1)}, f32[40,32,128]{2,1,0:T(8,128)S(1)}, u32[]{:S(2)}, u32[]{:S(2)}) collective-permute-start(f32[40,32,128]{2,1,0:T(8,128)S(1)} %shard_map.54.refs_0_), channel_id=1, source_target_pairs={{0,2},{1,3},{2,0},{3,1},{4,6},{5,7},{6,4},{7,5},{8,10},{9,11},{10,... | collective-permute-start | bytes 1966088 | tf_op jit(solution)/shard_map/ppermute | solution.py:63
  53.1 30.1 %collective-permute-start.30 = (f32[80,32,128]{2,1,0:T(8,128)S(1)}, f32[80,32,128]{2,1,0:T(8,128)S(1)}, u32[]{:S(2)}, u32[]{:S(2)}) collective-permute-start(f32[80,32,128]{2,1,0:T(8,128)S(1)} %shard_map.61.refs_0_), channel_id=1, source_target_pairs={{0,2},{1,3},{2,0},{3,1},{4,6},{5,7},{6,4},{7,5},{8,10},{9,11},{10,... | collective-permute-start | bytes 3932168 | tf_op jit(solution)/shard_map/ppermute | solution.py:63
  53.5 7.3 %collective-permute-start.21 = (f32[40,32,128]{2,1,0:T(8,128)S(1)}, f32[40,32,128]{2,1,0:T(8,128)S(1)}, u32[]{:S(2)}, u32[]{:S(2)}) collective-permute-start(f32[40,32,128]{2,1,0:T(8,128)S(1)} %copy-done.4), channel_id=1, source_target_pairs={{0,1},{1,0},{2,3},{3,2},{4,5},{5,4},{6,7},{7,6},{8,9},{9,8},{10,11... | collective-permute-start | bytes 1966088 | tf_op jit(solution)/shard_map/ppermute | solution.py:63
  53.5 7.9 %collective-permute-start.22 = (f32[40,32,128]{2,1,0:T(8,128)S(1)}, f32[40,32,128]{2,1,0:T(8,128)S(1)}, u32[]{:S(2)}, u32[]{:S(2)}) collective-permute-start(f32[40,32,128]{2,1,0:T(8,128)S(1)} %collective-permute-done.8.refs_0_.refs_2_), channel_id=1, source_target_pairs={{0,1},{1,0},{2,3},{3,2},{4,5},{5,4},{6,7},{7,6},{8,9},{9,8},{10,11... | collective-permute-start | bytes 1966088 | tf_op jit(solution)/shard_map/ppermute | solution.py:63
  54.0 7.9 %collective-permute-start.23 = (f32[40,32,128]{2,1,0:T(8,128)S(1)}, f32[40,32,128]{2,1,0:T(8,128)S(1)}, u32[]{:S(2)}, u32[]{:S(2)}) collective-permute-start(f32[40,32,128]{2,1,0:T(8,128)S(1)} %shard_map.54.refs_0_), channel_id=1, source_target_pairs={{0,1},{1,0},{2,3},{3,2},{4,5},{5,4},{6,7},{7,6},{8,9},{9,8},{10,11... | collective-permute-start | bytes 1966088 | tf_op jit(solution)/shard_map/ppermute | solution.py:63
  54.2 6.5 %collective-permute-start.17 = (f32[4,32,128]{2,1,0:T(8,128)S(1)}, f32[4,32,128]{2,1,0:T(8,128)S(1)}, u32[]{:S(2)}, u32[]{:S(2)}) collective-permute-start(f32[4,32,128]{2,1,0:T(8,128)S(1)} %get-tuple-element.56.forward_ref), channel_id=1, source_target_pairs={{0,16},{4,20},{8,24},{12,28},{16,0},{20,4},{24,8},{28,12},{1,17},{... | collective-permute-start | bytes 196616 | tf_op jit(solution)/shard_map/ppermute | solution.py:63
  61.9 8.8 %collective-permute-start.20 = (f32[8,32,128]{2,1,0:T(8,128)S(1)}, f32[8,32,128]{2,1,0:T(8,128)S(1)}, u32[]{:S(2)}, u32[]{:S(2)}) collective-permute-start(f32[8,32,128]{2,1,0:T(8,128)S(1)} %constant_dynamic-update-slice_fusion.2.x0), channel_id=1, source_target_pairs={{0,12},{4,8},{8,4},{12,0},{16,28},{20,24},{24,20},{28,16},{1,13},{... | collective-permute-start | bytes 393224 | tf_op jit(solution)/shard_map/ppermute | solution.py:63
  73.7 7.1 %collective-permute-start.27 = (f32[8,32,128]{2,1,0:T(8,128)S(1)}, f32[8,32,128]{2,1,0:T(8,128)S(1)}, u32[]{:S(2)}, u32[]{:S(2)}) collective-permute-start(f32[8,32,128]{2,1,0:T(8,128)S(1)} %get-tuple-element.60), channel_id=1, source_target_pairs={{0,12},{4,8},{8,4},{12,0},{16,28},{20,24},{24,20},{28,16},{1,13},{... | collective-permute-start | bytes 393224 | tf_op jit(solution)/shard_map/ppermute | solution.py:63
  74.3 7.2 %collective-permute-start.26 = (f32[8,32,128]{2,1,0:T(8,128)S(1)}, f32[8,32,128]{2,1,0:T(8,128)S(1)}, u32[]{:S(2)}, u32[]{:S(2)}) collective-permute-start(f32[8,32,128]{2,1,0:T(8,128)S(1)} %get-tuple-element.59), channel_id=1, source_target_pairs={{0,8},{4,12},{8,0},{12,4},{16,24},{20,28},{24,16},{28,20},{1,9},{5... | collective-permute-start | bytes 393224 | tf_op jit(solution)/shard_map/ppermute | solution.py:63
  77.3 8.4 %collective-permute-start.29 = (f32[80,32,128]{2,1,0:T(8,128)S(1)}, f32[80,32,128]{2,1,0:T(8,128)S(1)}, u32[]{:S(2)}, u32[]{:S(2)}) collective-permute-start(f32[80,32,128]{2,1,0:T(8,128)S(1)} %shard_map.61.refs_0_), channel_id=1, source_target_pairs={{0,1},{1,0},{2,3},{3,2},{4,5},{5,4},{6,7},{7,6},{8,9},{9,8},{10,11... | collective-permute-start | bytes 3932168 | tf_op jit(solution)/shard_map/ppermute | solution.py:63
  83.6 14.4 %collective-permute-start.37 = (f32[32,32,128]{2,1,0:T(8,128)S(1)}, f32[32,32,128]{2,1,0:T(8,128)S(1)}, u32[]{:S(2)}, u32[]{:S(2)}) collective-permute-start(f32[32,32,128]{2,1,0:T(8,128)S(1)} %shard_map.66.refs_0_), channel_id=1, source_target_pairs={{0,2},{1,3},{2,0},{3,1},{4,6},{5,7},{6,4},{7,5},{8,10},{9,11},{10,... | collective-permute-start | bytes 1572872 | tf_op jit(solution)/shard_map/ppermute | solution.py:63
  84.4 6.6 %collective-permute-start.28 = (f32[4,32,128]{2,1,0:T(8,128)S(1)}, f32[4,32,128]{2,1,0:T(8,128)S(1)}, u32[]{:S(2)}, u32[]{:S(2)}) collective-permute-start(f32[4,32,128]{2,1,0:T(8,128)S(1)} %get-tuple-element.92), channel_id=1, source_target_pairs={{0,16},{4,20},{8,24},{12,28},{16,0},{20,4},{24,8},{28,12},{1,17},{... | collective-permute-start | bytes 196616 | tf_op jit(solution)/shard_map/ppermute | solution.py:63
  93.0 7.3 %collective-permute-start.34 = (f32[8,32,128]{2,1,0:T(8,128)S(1)}, f32[8,32,128]{2,1,0:T(8,128)S(1)}, u32[]{:S(2)}, u32[]{:S(2)}) collective-permute-start(f32[8,32,128]{2,1,0:T(8,128)S(1)} %get-tuple-element.64), channel_id=1, source_target_pairs={{0,12},{4,8},{8,4},{12,0},{16,28},{20,24},{24,20},{28,16},{1,13},{... | collective-permute-start | bytes 393224 | tf_op jit(solution)/shard_map/ppermute | solution.py:63
  93.1 7.9 %collective-permute-start.33 = (f32[8,32,128]{2,1,0:T(8,128)S(1)}, f32[8,32,128]{2,1,0:T(8,128)S(1)}, u32[]{:S(2)}, u32[]{:S(2)}) collective-permute-start(f32[8,32,128]{2,1,0:T(8,128)S(1)} %get-tuple-element.63), channel_id=1, source_target_pairs={{0,8},{4,12},{8,0},{12,4},{16,24},{20,28},{24,16},{28,20},{1,9},{5... | collective-permute-start | bytes 393224 | tf_op jit(solution)/shard_map/ppermute | solution.py:63
  95.2 6.9 %collective-permute-start.32 = (f32[8,32,128]{2,1,0:T(8,128)S(1)}, f32[8,32,128]{2,1,0:T(8,128)S(1)}, u32[]{:S(2)}, u32[]{:S(2)}) collective-permute-start(f32[8,32,128]{2,1,0:T(8,128)S(1)} %get-tuple-element.62), channel_id=1, source_target_pairs={{0,4},{4,0},{8,12},{12,8},{16,20},{20,16},{24,28},{28,24},{1,5},{5... | collective-permute-start | bytes 393224 | tf_op jit(solution)/shard_map/ppermute | solution.py:63
  96.6 7.0 %collective-permute-start.36 = (f32[32,32,128]{2,1,0:T(8,128)S(1)}, f32[32,32,128]{2,1,0:T(8,128)S(1)}, u32[]{:S(2)}, u32[]{:S(2)}) collective-permute-start(f32[32,32,128]{2,1,0:T(8,128)S(1)} %shard_map.66.refs_0_), channel_id=1, source_target_pairs={{0,1},{1,0},{2,3},{3,2},{4,5},{5,4},{6,7},{7,6},{8,9},{9,8},{10,11... | collective-permute-start | bytes 1572872 | tf_op jit(solution)/shard_map/ppermute | solution.py:63
  110.6 7.3 %collective-permute-start.41 = (f32[8,32,128]{2,1,0:T(8,128)S(1)}, f32[8,32,128]{2,1,0:T(8,128)S(1)}, u32[]{:S(2)}, u32[]{:S(2)}) collective-permute-start(f32[8,32,128]{2,1,0:T(8,128)S(1)} %get-tuple-element.70), channel_id=1, source_target_pairs={{0,12},{4,8},{8,4},{12,0},{16,28},{20,24},{24,20},{28,16},{1,13},{... | collective-permute-start | bytes 393224 | tf_op jit(solution)/shard_map/ppermute | solution.py:63
  110.8 8.6 %collective-permute-start.40 = (f32[8,32,128]{2,1,0:T(8,128)S(1)}, f32[8,32,128]{2,1,0:T(8,128)S(1)}, u32[]{:S(2)}, u32[]{:S(2)}) collective-permute-start(f32[8,32,128]{2,1,0:T(8,128)S(1)} %get-tuple-element.69), channel_id=1, source_target_pairs={{0,8},{4,12},{8,0},{12,4},{16,24},{20,28},{24,16},{28,20},{1,9},{5... | collective-permute-start | bytes 393224 | tf_op jit(solution)/shard_map/ppermute | solution.py:63
  113.4 6.5 %collective-permute-start.39 = (f32[8,32,128]{2,1,0:T(8,128)S(1)}, f32[8,32,128]{2,1,0:T(8,128)S(1)}, u32[]{:S(2)}, u32[]{:S(2)}) collective-permute-start(f32[8,32,128]{2,1,0:T(8,128)S(1)} %get-tuple-element.68), channel_id=1, source_target_pairs={{0,4},{4,0},{8,12},{12,8},{16,20},{20,16},{24,28},{28,24},{1,5},{5... | collective-permute-start | bytes 393224 | tf_op jit(solution)/shard_map/ppermute | solution.py:63
  120.5 7.7 %collective-permute-start.47 = (f32[3,32,128]{2,1,0:T(8,128)S(1)}, f32[3,32,128]{2,1,0:T(8,128)S(1)}, u32[]{:S(2)}, u32[]{:S(2)}) collective-permute-start(f32[3,32,128]{2,1,0:T(8,128)S(1)} %get-tuple-element.79), channel_id=1, source_target_pairs={{0,2},{1,3},{2,0},{3,1},{4,6},{5,7},{6,4},{7,5},{8,10},{9,11},{10,... | collective-permute-start | bytes 147464 | tf_op jit(solution)/shard_map/ppermute | solution.py:63
  121.3 6.9 %collective-permute-start.48 = (f32[3,32,128]{2,1,0:T(8,128)S(1)}, f32[3,32,128]{2,1,0:T(8,128)S(1)}, u32[]{:S(2)}, u32[]{:S(2)}) collective-permute-start(f32[3,32,128]{2,1,0:T(8,128)S(1)} %get-tuple-element.80), channel_id=1, source_target_pairs={{0,3},{1,2},{2,1},{3,0},{4,7},{5,6},{6,5},{7,4},{8,11},{9,10},{10,... | collective-permute-start | bytes 147464 | tf_op jit(solution)/shard_map/ppermute | solution.py:63
  (31 other events, 153.1 us)

commit v6 on v5

--- a/solution.py
+++ b/solution.py
@@ -14,7 +14,7 @@
 SMEM = pl.BlockSpec(memory_space=pltpu.SMEM)
 ANY = pl.BlockSpec(memory_space=pl.ANY)
 HBM = pl.BlockSpec(memory_space=pltpu.HBM)
-CUTS = (0.625, 0.25, 0.5)
+CUTS = (0.625, 0.25, 0.375)
 TINY = pl.CostEstimate(flops=1, bytes_accessed=1, transcendentals=0)
 
 
@@ -474,7 +474,7 @@
     forward[2], forward[1] = call(
         solve_kernel, [block] * 2, [SMEM] + [VMEM] * 5, scratch=[pltpu.VMEM((cols, mine, width), F32)]
     )(col, *updates, sides[2], inverse[2])
-    inner = pack(flat, [(at1 + cuts[1], entries - cuts[1]), (at0, cuts[2])], updates[2])
+    inner = pack(flat, [(at1 + cuts[1], entries - cuts[1]), (at0, cuts[2])], forward[2])
     inner_across = swap(inner, "col", 2)
 
     picking = [

time: 131 us -> 132 us (level)
  transfers between devices with their start and end apart: 49 -> 49, of which waited for: 33 -> 32; matrix products, arithmetic and copies ran while one was open for 0% -> 0% of each run, Pallas kernels for 13% -> 13%
where the time goes in v6:
time: 132 us; the launch traced here: 131 us
  waiting for transfers between devices  68.1 us (52%)
  starting transfers between devices  39.6 us (30%)
  Pallas kernels  20.1 us (15%)
  local copies, waits for them, and re-layouts  2.89 us (2%)
    ppermute x49, waiting for transfers between devices, swap(): return lax.ppermute(value, axis, [(i, i ^ mask) for i in range(size)])  68.1 us
    ppermute x49, starting transfers between devices, swap(): return lax.ppermute(value, axis, [(i, i ^ mask) for i in range(size)])  39.6 us
    pallas_call x1, Pallas kernels, on_device(): call(functools.partial(top_kernel, spans[0]), [block] + [quarter] * 4, [S...  3.02 us
  transfers between devices with their start and end apart: 49, of which 32 were waited for; matrix products, arithmetic and copies ran while one was open for 0% of the time, Pallas kernels for 13%

profile of v6, /device:TPU:0, one launch (start us, length us, event | category | flops | bytes accessed | tf_op | source)
XLA Modules:
  0.0 131.4 jit_solution(10867315856444580338)
XLA Ops:
  0.0 3.0 %collective-permute-start.1 = (f32[16,32,128]{2,1,0:T(8,128)}, f32[16,32,128]{2,1,0:T(8,128)S(1)}, u32[]{:S(2)}, u32[]{:S(2)}) collective-permute-start(f32[16,32,128]{2,1,0:T(8,128)} %bitcast.13), channel_id=1, source_target_pairs={{0,2},{1,3},{2,0},{3,1},{4,6},{5,7},{6,4},{7,5},{8,10},{9,11},{10,... | collective-permute-start | bytes 786440 | tf_op jit(solution)/shard_map/ppermute | solution.py:63
  3.0 2.3 %shard_map.46 = (f32[4,32,128]{2,1,0:T(8,128)}, f32[40,32,128]{2,1,0:T(8,128)}) custom-call(f32[4,4,32,128]{3,2,1,0:T(8,128)} %own_inverse_ref.1, f32[4,4,128,128]{3,2,1,0:T(8,128)} %all_sides_ref.1, f32[192,32,128]{2,1,0:T(8,128)} %bitcast.9), custom_call_target="tpu_custom_call" | custom-call | flops 1 | bytes 1 | tf_op jit(solution)/shard_map/pallas_call | solution.py:408
  5.3 2.7 %collective-permute-start.3 = (f32[4,32,128]{2,1,0:T(8,128)}, f32[4,32,128]{2,1,0:T(8,128)S(1)}, u32[]{:S(2)}, u32[]{:S(2)}) collective-permute-start(f32[4,32,128]{2,1,0:T(8,128)} %get-tuple-element.43.refs_0_), channel_id=1, source_target_pairs={{0,16},{4,20},{8,24},{12,28},{16,0},{20,4},{24,8},{28,12},{1,17},{... | collective-permute-start | bytes 196616 | tf_op jit(solution)/shard_map/ppermute | solution.py:63
  22.8 3.5 %collective-permute-done.8.refs_0_.refs_2_ = f32[40,32,128]{2,1,0:T(8,128)S(1)} collective-permute-done((f32[40,32,128]{2,1,0:T(8,128)}, f32[40,32,128]{2,1,0:T(8,128)S(1)}, u32[]{:S(2)}, u32[]{:S(2)}) %collective-permute-start.8) | collective-permute-done | bytes 655392 | tf_op jit(solution)/shard_map/ppermute | solution.py:63
  26.8 3.8 %collective-permute-done.9.refs_0_ = f32[4,32,128]{2,1,0:T(8,128)S(1)} collective-permute-done((f32[4,32,128]{2,1,0:T(8,128)S(1)}, f32[4,32,128]{2,1,0:T(8,128)S(1)}, u32[]{:S(2)}, u32[]{:S(2)}) %collective-permute-start.9) | collective-permute-done | bytes 65568 | tf_op jit(solution)/shard_map/ppermute | solution.py:63
  32.5 3.3 %collective-permute-done.10.after_ref = f32[4,32,128]{2,1,0:T(8,128)S(1)} collective-permute-done((f32[4,32,128]{2,1,0:T(8,128)S(1)}, f32[4,32,128]{2,1,0:T(8,128)S(1)}, u32[]{:S(2)}, u32[]{:S(2)}) %collective-permute-start.10) | collective-permute-done | bytes 65568 | tf_op jit(solution)/shard_map/ppermute | solution.py:63
  37.4 2.1 %collective-permute-start.12 = (f32[8,32,128]{2,1,0:T(8,128)S(1)}, f32[8,32,128]{2,1,0:T(8,128)S(1)}, u32[]{:S(2)}, u32[]{:S(2)}) collective-permute-start(f32[8,32,128]{2,1,0:T(8,128)S(1)} %pad_maximum_fusion.x0), channel_id=1, source_target_pairs={{0,8},{4,12},{8,0},{12,4},{16,24},{20,28},{24,16},{28,20},{1,9},{5... | collective-permute-start | bytes 393224 | tf_op jit(solution)/shard_map/ppermute | solution.py:63
  42.5 2.9 %collective-permute-done.13.x3 = f32[8,32,128]{2,1,0:T(8,128)S(1)} collective-permute-done((f32[8,32,128]{2,1,0:T(8,128)S(1)}, f32[8,32,128]{2,1,0:T(8,128)S(1)}, u32[]{:S(2)}, u32[]{:S(2)}) %collective-permute-start.13) | collective-permute-done | bytes 131104 | tf_op jit(solution)/shard_map/ppermute | solution.py:63
  48.2 4.8 %collective-permute-done.16.u2 = f32[6,32,128]{2,1,0:T(8,128)S(1)} collective-permute-done((f32[6,32,128]{2,1,0:T(8,128)S(1)}, f32[6,32,128]{2,1,0:T(8,128)S(1)}, u32[]{:S(2)}, u32[]{:S(2)}) %collective-permute-start.16) | collective-permute-done | bytes 98336 | tf_op jit(solution)/shard_map/ppermute | solution.py:63
  55.7 5.4 %collective-permute-done.17 = f32[4,32,128]{2,1,0:T(8,128)S(1)} collective-permute-done((f32[4,32,128]{2,1,0:T(8,128)S(1)}, f32[4,32,128]{2,1,0:T(8,128)S(1)}, u32[]{:S(2)}, u32[]{:S(2)}) %collective-permute-start.17) | collective-permute-done | bytes 65568 | tf_op jit(solution)/shard_map/ppermute | solution.py:63
  62.4 2.4 %collective-permute-start.20 = (f32[8,32,128]{2,1,0:T(8,128)S(1)}, f32[8,32,128]{2,1,0:T(8,128)S(1)}, u32[]{:S(2)}, u32[]{:S(2)}) collective-permute-start(f32[8,32,128]{2,1,0:T(8,128)S(1)} %constant_dynamic-update-slice_fusion.2.x0), channel_id=1, source_target_pairs={{0,12},{4,8},{8,4},{12,0},{16,28},{20,24},{24,20},{28,16},{1,13},{... | collective-permute-start | bytes 393224 | tf_op jit(solution)/shard_map/ppermute | solution.py:63
  67.6 3.4 %collective-permute-done.20.x3 = f32[8,32,128]{2,1,0:T(8,128)S(1)} collective-permute-done((f32[8,32,128]{2,1,0:T(8,128)S(1)}, f32[8,32,128]{2,1,0:T(8,128)S(1)}, u32[]{:S(2)}, u32[]{:S(2)}) %collective-permute-start.20) | collective-permute-done | bytes 131104 | tf_op jit(solution)/shard_map/ppermute | solution.py:63
  71.1 3.0 %shard_map.59 = (f32[4,32,128]{2,1,0:T(8,128)S(1)}, f32[8,32,128]{2,1,0:T(8,128)S(1)}, f32[8,32,128]{2,1,0:T(8,128)S(1)}, f32[8,32,128]{2,1,0:T(8,128)S(1)}, f32[8,32,128]{2,1,0:T(8,128)S(1)}) custom-call(s32[64]{0:T(128)S(1)} %get-tuple-element.94.slot_ref, f32[8,32,128]{2,1,0:T(8,128)S(1)} %constant_dynamic-update-slice_fusion.2.x0, ...), custom_call_target="tpu_custom_call" | custom-call | flops 1 | bytes 1 | tf_op jit(solution)/shard_map/pallas_call | solution.py:491
  77.7 3.6 %collective-permute-done.27.refs_2_ = f32[8,32,128]{2,1,0:T(8,128)S(1)} collective-permute-done((f32[8,32,128]{2,1,0:T(8,128)S(1)}, f32[8,32,128]{2,1,0:T(8,128)S(1)}, u32[]{:S(2)}, u32[]{:S(2)}) %collective-permute-start.27) | collective-permute-done | bytes 131104 | tf_op jit(solution)/shard_map/ppermute | solution.py:63
  86.5 4.7 %collective-permute-done.28.ret1 = f32[4,32,128]{2,1,0:T(8,128)S(1)} collective-permute-done((f32[4,32,128]{2,1,0:T(8,128)S(1)}, f32[4,32,128]{2,1,0:T(8,128)S(1)}, u32[]{:S(2)}, u32[]{:S(2)}) %collective-permute-start.28) | collective-permute-done | bytes 65568 | tf_op jit(solution)/shard_map/ppermute | solution.py:63
  91.1 2.1 %shard_map.64 = (f32[4,32,128]{2,1,0:T(8,128)S(1)}, f32[8,32,128]{2,1,0:T(8,128)S(1)}, f32[8,32,128]{2,1,0:T(8,128)S(1)}, f32[8,32,128]{2,1,0:T(8,128)S(1)}, f32[8,32,128]{2,1,0:T(8,128)S(1)}) custom-call(s32[64]{0:T(128)S(1)} %get-tuple-element.95.slot_ref, f32[4,32,128]{2,1,0:T(8,128)S(1)} %get-tuple-element.93.ret0, ...), custom_call_target="tpu_custom_call" | custom-call | flops 1 | bytes 1 | tf_op jit(solution)/shard_map/pallas_call | solution.py:502
  93.3 2.1 %collective-permute-start.33 = (f32[8,32,128]{2,1,0:T(8,128)S(1)}, f32[8,32,128]{2,1,0:T(8,128)S(1)}, u32[]{:S(2)}, u32[]{:S(2)}) collective-permute-start(f32[8,32,128]{2,1,0:T(8,128)S(1)} %get-tuple-element.63), channel_id=1, source_target_pairs={{0,8},{4,12},{8,0},{12,4},{16,24},{20,28},{24,16},{28,20},{1,9},{5... | collective-permute-start | bytes 393224 | tf_op jit(solution)/shard_map/ppermute | solution.py:63
  96.8 3.6 %collective-permute-done.37.value_ref = f32[40,32,128]{2,1,0:T(8,128)S(1)} collective-permute-done((f32[40,32,128]{2,1,0:T(8,128)S(1)}, f32[40,32,128]{2,1,0:T(8,128)S(1)}, u32[]{:S(2)}, u32[]{:S(2)}) %collective-permute-start.37) | collective-permute-done | bytes 655392 | tf_op jit(solution)/shard_map/ppermute | solution.py:63
  105.0 3.8 %collective-permute-done.35.ret1 = f32[4,32,128]{2,1,0:T(8,128)S(1)} collective-permute-done((f32[4,32,128]{2,1,0:T(8,128)S(1)}, f32[4,32,128]{2,1,0:T(8,128)S(1)}, u32[]{:S(2)}, u32[]{:S(2)}) %collective-permute-start.35) | collective-permute-done | bytes 65568 | tf_op jit(solution)/shard_map/ppermute | solution.py:63
  108.8 2.1 %shard_map.69 = (f32[4,32,128]{2,1,0:T(8,128)S(1)}, f32[8,32,128]{2,1,0:T(8,128)S(1)}, f32[8,32,128]{2,1,0:T(8,128)S(1)}, f32[8,32,128]{2,1,0:T(8,128)S(1)}, f32[8,32,128]{2,1,0:T(8,128)S(1)}) custom-call(s32[64]{0:T(128)S(1)} %get-tuple-element.96.slot_ref, f32[4,32,128]{2,1,0:T(8,128)S(1)} %get-tuple-element.91.ret0, ...), custom_call_target="tpu_custom_call" | custom-call | flops 1 | bytes 1 | tf_op jit(solution)/shard_map/pallas_call | solution.py:509
  111.0 2.7 %collective-permute-start.40 = (f32[8,32,128]{2,1,0:T(8,128)S(1)}, f32[8,32,128]{2,1,0:T(8,128)S(1)}, u32[]{:S(2)}, u32[]{:S(2)}) collective-permute-start(f32[8,32,128]{2,1,0:T(8,128)S(1)} %get-tuple-element.69), channel_id=1, source_target_pairs={{0,8},{4,12},{8,0},{12,4},{16,24},{20,28},{24,16},{28,20},{1,9},{5... | collective-permute-start | bytes 393224 | tf_op jit(solution)/shard_map/ppermute | solution.py:63
  114.4 3.8 %collective-permute-done.41.refs_5_ = f32[8,32,128]{2,1,0:T(8,128)S(1)} collective-permute-done((f32[8,32,128]{2,1,0:T(8,128)S(1)}, f32[8,32,128]{2,1,0:T(8,128)S(1)}, u32[]{:S(2)}, u32[]{:S(2)}) %collective-permute-start.41) | collective-permute-done | bytes 131104 | tf_op jit(solution)/shard_map/ppermute | solution.py:63
  123.4 2.8 %collective-permute-done.42.ret_ref = f32[4,32,128]{2,1,0:T(8,128)S(1)} collective-permute-done((f32[4,32,128]{2,1,0:T(8,128)S(1)}, f32[4,32,128]{2,1,0:T(8,128)S(1)}, u32[]{:S(2)}, u32[]{:S(2)}) %collective-permute-start.42) | collective-permute-done | bytes 65568 | tf_op jit(solution)/shard_map/ppermute | solution.py:63
  128.6 1.8 %collective-permute-done.44.refs_2_ = f32[1,32,128]{2,1,0:T(8,128)S(1)} collective-permute-done((f32[1,32,128]{2,1,0:T(8,128)S(1)}, f32[1,32,128]{2,1,0:T(8,128)S(1)}, u32[]{:S(2)}, u32[]{:S(2)}) %collective-permute-start.44) | collective-permute-done | bytes 16416 | tf_op jit(solution)/shard_map/ppermute | solution.py:63
  (140 shorter events, 55.3 us)
Async XLA Ops:
  0.0 9.8 %collective-permute-start.1 = (f32[16,32,128]{2,1,0:T(8,128)}, f32[16,32,128]{2,1,0:T(8,128)S(1)}, u32[]{:S(2)}, u32[]{:S(2)}) collective-permute-start(f32[16,32,128]{2,1,0:T(8,128)} %bitcast.13), channel_id=1, source_target_pairs={{0,2},{1,3},{2,0},{3,1},{4,6},{5,7},{6,4},{7,5},{8,10},{9,11},{10,... | collective-permute-start | bytes 786440 | tf_op jit(solution)/shard_map/ppermute | solution.py:63
  8.9 17.4 %collective-permute-start.8 = (f32[40,32,128]{2,1,0:T(8,128)}, f32[40,32,128]{2,1,0:T(8,128)S(1)}, u32[]{:S(2)}, u32[]{:S(2)}) collective-permute-start(f32[40,32,128]{2,1,0:T(8,128)} %get-tuple-element.50.refs_0_), channel_id=1, source_target_pairs={{0,2},{1,3},{2,0},{3,1},{4,6},{5,7},{6,4},{7,5},{8,10},{9,11},{10,... | collective-permute-start | bytes 1966088 | tf_op jit(solution)/shard_map/ppermute | solution.py:63
  11.1 6.6 %collective-permute-start.4 = (f32[8,32,128]{2,1,0:T(8,128)S(1)}, f32[8,32,128]{2,1,0:T(8,128)S(1)}, u32[]{:S(2)}, u32[]{:S(2)}) collective-permute-start(f32[8,32,128]{2,1,0:T(8,128)S(1)} %constant_dynamic-update-slice_fusion.x0), channel_id=1, source_target_pairs={{0,4},{4,0},{8,12},{12,8},{16,20},{20,16},{24,28},{28,24},{1,5},{5... | collective-permute-start | bytes 393224 | tf_op jit(solution)/shard_map/ppermute | solution.py:63
  31.2 16.8 %collective-permute-start.15 = (f32[40,32,128]{2,1,0:T(8,128)S(1)}, f32[40,32,128]{2,1,0:T(8,128)S(1)}, u32[]{:S(2)}, u32[]{:S(2)}) collective-permute-start(f32[40,32,128]{2,1,0:T(8,128)S(1)} %shard_map.54.refs_0_), channel_id=1, source_target_pairs={{0,2},{1,3},{2,0},{3,1},{4,6},{5,7},{6,4},{7,5},{8,10},{9,11},{10,... | collective-permute-start | bytes 1966088 | tf_op jit(solution)/shard_map/ppermute | solution.py:63
  53.5 29.1 %collective-permute-start.30 = (f32[72,32,128]{2,1,0:T(8,128)S(1)}, f32[72,32,128]{2,1,0:T(8,128)S(1)}, u32[]{:S(2)}, u32[]{:S(2)}) collective-permute-start(f32[72,32,128]{2,1,0:T(8,128)S(1)} %shard_map.61.refs_0_), channel_id=1, source_target_pairs={{0,2},{1,3},{2,0},{3,1},{4,6},{5,7},{6,4},{7,5},{8,10},{9,11},{10,... | collective-permute-start | bytes 3538952 | tf_op jit(solution)/shard_map/ppermute | solution.py:63
  54.3 6.9 %collective-permute-start.21 = (f32[40,32,128]{2,1,0:T(8,128)S(1)}, f32[40,32,128]{2,1,0:T(8,128)S(1)}, u32[]{:S(2)}, u32[]{:S(2)}) collective-permute-start(f32[40,32,128]{2,1,0:T(8,128)S(1)} %copy-done.4), channel_id=1, source_target_pairs={{0,1},{1,0},{2,3},{3,2},{4,5},{5,4},{6,7},{7,6},{8,9},{9,8},{10,11... | collective-permute-start | bytes 1966088 | tf_op jit(solution)/shard_map/ppermute | solution.py:63
  54.3 7.0 %collective-permute-start.22 = (f32[40,32,128]{2,1,0:T(8,128)S(1)}, f32[40,32,128]{2,1,0:T(8,128)S(1)}, u32[]{:S(2)}, u32[]{:S(2)}) collective-permute-start(f32[40,32,128]{2,1,0:T(8,128)S(1)} %collective-permute-done.8.refs_0_.refs_2_), channel_id=1, source_target_pairs={{0,1},{1,0},{2,3},{3,2},{4,5},{5,4},{6,7},{7,6},{8,9},{9,8},{10,11... | collective-permute-start | bytes 1966088 | tf_op jit(solution)/shard_map/ppermute | solution.py:63
  54.8 7.6 %collective-permute-start.23 = (f32[40,32,128]{2,1,0:T(8,128)S(1)}, f32[40,32,128]{2,1,0:T(8,128)S(1)}, u32[]{:S(2)}, u32[]{:S(2)}) collective-permute-start(f32[40,32,128]{2,1,0:T(8,128)S(1)} %shard_map.54.refs_0_), channel_id=1, source_target_pairs={{0,1},{1,0},{2,3},{3,2},{4,5},{5,4},{6,7},{7,6},{8,9},{9,8},{10,11... | collective-permute-start | bytes 1966088 | tf_op jit(solution)/shard_map/ppermute | solution.py:63
  62.4 8.7 %collective-permute-start.20 = (f32[8,32,128]{2,1,0:T(8,128)S(1)}, f32[8,32,128]{2,1,0:T(8,128)S(1)}, u32[]{:S(2)}, u32[]{:S(2)}) collective-permute-start(f32[8,32,128]{2,1,0:T(8,128)S(1)} %constant_dynamic-update-slice_fusion.2.x0), channel_id=1, source_target_pairs={{0,12},{4,8},{8,4},{12,0},{16,28},{20,24},{24,20},{28,16},{1,13},{... | collective-permute-start | bytes 393224 | tf_op jit(solution)/shard_map/ppermute | solution.py:63
  74.1 7.1 %collective-permute-start.27 = (f32[8,32,128]{2,1,0:T(8,128)S(1)}, f32[8,32,128]{2,1,0:T(8,128)S(1)}, u32[]{:S(2)}, u32[]{:S(2)}) collective-permute-start(f32[8,32,128]{2,1,0:T(8,128)S(1)} %get-tuple-element.60), channel_id=1, source_target_pairs={{0,12},{4,8},{8,4},{12,0},{16,28},{20,24},{24,20},{28,16},{1,13},{... | collective-permute-start | bytes 393224 | tf_op jit(solution)/shard_map/ppermute | solution.py:63
  74.8 7.0 %collective-permute-start.26 = (f32[8,32,128]{2,1,0:T(8,128)S(1)}, f32[8,32,128]{2,1,0:T(8,128)S(1)}, u32[]{:S(2)}, u32[]{:S(2)}) collective-permute-start(f32[8,32,128]{2,1,0:T(8,128)S(1)} %get-tuple-element.59), channel_id=1, source_target_pairs={{0,8},{4,12},{8,0},{12,4},{16,24},{20,28},{24,16},{28,20},{1,9},{5... | collective-permute-start | bytes 393224 | tf_op jit(solution)/shard_map/ppermute | solution.py:63
  76.0 6.6 %collective-permute-start.25 = (f32[8,32,128]{2,1,0:T(8,128)S(1)}, f32[8,32,128]{2,1,0:T(8,128)S(1)}, u32[]{:S(2)}, u32[]{:S(2)}) collective-permute-start(f32[8,32,128]{2,1,0:T(8,128)S(1)} %get-tuple-element.58), channel_id=1, source_target_pairs={{0,4},{4,0},{8,12},{12,8},{16,20},{20,16},{24,28},{28,24},{1,5},{5... | collective-permute-start | bytes 393224 | tf_op jit(solution)/shard_map/ppermute | solution.py:63
  77.7 8.3 %collective-permute-start.29 = (f32[72,32,128]{2,1,0:T(8,128)S(1)}, f32[72,32,128]{2,1,0:T(8,128)S(1)}, u32[]{:S(2)}, u32[]{:S(2)}) collective-permute-start(f32[72,32,128]{2,1,0:T(8,128)S(1)} %shard_map.61.refs_0_), channel_id=1, source_target_pairs={{0,1},{1,0},{2,3},{3,2},{4,5},{5,4},{6,7},{7,6},{8,9},{9,8},{10,11... | collective-permute-start | bytes 3538952 | tf_op jit(solution)/shard_map/ppermute | solution.py:63
  83.2 17.2 %collective-permute-start.37 = (f32[40,32,128]{2,1,0:T(8,128)S(1)}, f32[40,32,128]{2,1,0:T(8,128)S(1)}, u32[]{:S(2)}, u32[]{:S(2)}) collective-permute-start(f32[40,32,128]{2,1,0:T(8,128)S(1)} %shard_map.66.refs_0_), channel_id=1, source_target_pairs={{0,2},{1,3},{2,0},{3,1},{4,6},{5,7},{6,4},{7,5},{8,10},{9,11},{10,... | collective-permute-start | bytes 1966088 | tf_op jit(solution)/shard_map/ppermute | solution.py:63
  84.6 6.6 %collective-permute-start.28 = (f32[4,32,128]{2,1,0:T(8,128)S(1)}, f32[4,32,128]{2,1,0:T(8,128)S(1)}, u32[]{:S(2)}, u32[]{:S(2)}) collective-permute-start(f32[4,32,128]{2,1,0:T(8,128)S(1)} %get-tuple-element.92), channel_id=1, source_target_pairs={{0,16},{4,20},{8,24},{12,28},{16,0},{20,4},{24,8},{28,12},{1,17},{... | collective-permute-start | bytes 196616 | tf_op jit(solution)/shard_map/ppermute | solution.py:63
  93.2 7.3 %collective-permute-start.34 = (f32[8,32,128]{2,1,0:T(8,128)S(1)}, f32[8,32,128]{2,1,0:T(8,128)S(1)}, u32[]{:S(2)}, u32[]{:S(2)}) collective-permute-start(f32[8,32,128]{2,1,0:T(8,128)S(1)} %get-tuple-element.64), channel_id=1, source_target_pairs={{0,12},{4,8},{8,4},{12,0},{16,28},{20,24},{24,20},{28,16},{1,13},{... | collective-permute-start | bytes 393224 | tf_op jit(solution)/shard_map/ppermute | solution.py:63
  93.3 8.3 %collective-permute-start.33 = (f32[8,32,128]{2,1,0:T(8,128)S(1)}, f32[8,32,128]{2,1,0:T(8,128)S(1)}, u32[]{:S(2)}, u32[]{:S(2)}) collective-permute-start(f32[8,32,128]{2,1,0:T(8,128)S(1)} %get-tuple-element.63), channel_id=1, source_target_pairs={{0,8},{4,12},{8,0},{12,4},{16,24},{20,28},{24,16},{28,20},{1,9},{5... | collective-permute-start | bytes 393224 | tf_op jit(solution)/shard_map/ppermute | solution.py:63
  95.4 6.9 %collective-permute-start.32 = (f32[8,32,128]{2,1,0:T(8,128)S(1)}, f32[8,32,128]{2,1,0:T(8,128)S(1)}, u32[]{:S(2)}, u32[]{:S(2)}) collective-permute-start(f32[8,32,128]{2,1,0:T(8,128)S(1)} %get-tuple-element.62), channel_id=1, source_target_pairs={{0,4},{4,0},{8,12},{12,8},{16,20},{20,16},{24,28},{28,24},{1,5},{5... | collective-permute-start | bytes 393224 | tf_op jit(solution)/shard_map/ppermute | solution.py:63
  96.8 6.9 %collective-permute-start.36 = (f32[40,32,128]{2,1,0:T(8,128)S(1)}, f32[40,32,128]{2,1,0:T(8,128)S(1)}, u32[]{:S(2)}, u32[]{:S(2)}) collective-permute-start(f32[40,32,128]{2,1,0:T(8,128)S(1)} %shard_map.66.refs_0_), channel_id=1, source_target_pairs={{0,1},{1,0},{2,3},{3,2},{4,5},{5,4},{6,7},{7,6},{8,9},{9,8},{10,11... | collective-permute-start | bytes 1966088 | tf_op jit(solution)/shard_map/ppermute | solution.py:63
  110.9 7.3 %collective-permute-start.41 = (f32[8,32,128]{2,1,0:T(8,128)S(1)}, f32[8,32,128]{2,1,0:T(8,128)S(1)}, u32[]{:S(2)}, u32[]{:S(2)}) collective-permute-start(f32[8,32,128]{2,1,0:T(8,128)S(1)} %get-tuple-element.70), channel_id=1, source_target_pairs={{0,12},{4,8},{8,4},{12,0},{16,28},{20,24},{24,20},{28,16},{1,13},{... | collective-permute-start | bytes 393224 | tf_op jit(solution)/shard_map/ppermute | solution.py:63
  111.0 8.8 %collective-permute-start.40 = (f32[8,32,128]{2,1,0:T(8,128)S(1)}, f32[8,32,128]{2,1,0:T(8,128)S(1)}, u32[]{:S(2)}, u32[]{:S(2)}) collective-permute-start(f32[8,32,128]{2,1,0:T(8,128)S(1)} %get-tuple-element.69), channel_id=1, source_target_pairs={{0,8},{4,12},{8,0},{12,4},{16,24},{20,28},{24,16},{28,20},{1,9},{5... | collective-permute-start | bytes 393224 | tf_op jit(solution)/shard_map/ppermute | solution.py:63
  120.7 6.7 %collective-permute-start.46 = (f32[3,32,128]{2,1,0:T(8,128)S(1)}, f32[3,32,128]{2,1,0:T(8,128)S(1)}, u32[]{:S(2)}, u32[]{:S(2)}) collective-permute-start(f32[3,32,128]{2,1,0:T(8,128)S(1)} %get-tuple-element.78), channel_id=1, source_target_pairs={{0,1},{1,0},{2,3},{3,2},{4,5},{5,4},{6,7},{7,6},{8,9},{9,8},{10,11... | collective-permute-start | bytes 147464 | tf_op jit(solution)/shard_map/ppermute | solution.py:63
  120.7 7.7 %collective-permute-start.47 = (f32[3,32,128]{2,1,0:T(8,128)S(1)}, f32[3,32,128]{2,1,0:T(8,128)S(1)}, u32[]{:S(2)}, u32[]{:S(2)}) collective-permute-start(f32[3,32,128]{2,1,0:T(8,128)S(1)} %get-tuple-element.79), channel_id=1, source_target_pairs={{0,2},{1,3},{2,0},{3,1},{4,6},{5,7},{6,4},{7,5},{8,10},{9,11},{10,... | collective-permute-start | bytes 147464 | tf_op jit(solution)/shard_map/ppermute | solution.py:63
  121.7 6.7 %collective-permute-start.48 = (f32[3,32,128]{2,1,0:T(8,128)S(1)}, f32[3,32,128]{2,1,0:T(8,128)S(1)}, u32[]{:S(2)}, u32[]{:S(2)}) collective-permute-start(f32[3,32,128]{2,1,0:T(8,128)S(1)} %get-tuple-element.80), channel_id=1, source_target_pairs={{0,3},{1,2},{2,1},{3,0},{4,7},{5,6},{6,5},{7,4},{8,11},{9,10},{10,... | collective-permute-start | bytes 147464 | tf_op jit(solution)/shard_map/ppermute | solution.py:63
  (31 other events, 148.9 us)
